TPU v7x, 32 devices: a whole 2x2x4 slice. The times are simulated.
32 devices in a mesh: band: 16 (over z, y, core), fft: 2 (over x).
Axes of the slice: x: 2, y: 2, z: 4, core: 2. Of those that a mesh axis runs over, the one named last changes fastest.
Arguments:
- orbitals: float32 [32, 96, 9216], P('band', 'fft'), may hold values from -6 to 6
- owners: int32 [1], replicated, may hold values from 0 to 15
- cutoff_mask: int32 [96, 9216], P(None, 'fft'), may hold values from 0 to 1, as said below
Outputs:
- exchange_local: float32 [32, 96, 9216], P('band', 'fft')
- exchange_block: float32 [2, 96, 9216], P(None, 'fft')
Inputs may be any that keep to these rules, and one draw needn't show every extreme that they name: cutoff_mask is 1 exactly at the frequencies whose squared length s(x)^2 + s(y)^2 + s(z)^2 lies between 1 and a cutoff, and 0 elsewhere (0 at frequency (0, 0, 0)); it is unchanged when the sign of any one frequency component is changed.
All inputs are finite; a program needn't handle non-finite values.
Results may differ from a plain program's by a relative error of at most 0.00029.
Values sent between devices are 32-bit elements; how exact they have to be, the bound alone decides.
No kernel may reach another device: no remote copies, remote signals or barrier semaphores. Data moves between devices by JAX's collectives and lax.ppermute only.
A program may use at most 128 MiB of HBM per device.

v0:
```python
import math

import jax
import jax.numpy as jnp
from jax import lax
from jax.sharding import PartitionSpec as P

COULOMB = 400.0
EXCHANGE_MIX = 0.25


def broadcast(value, axis, source):
    kept = jnp.where(lax.axis_index(axis) == source, value, 0).astype(value.dtype)
    return lax.psum(kept, axis)


def dft_tables(count):
    positions = jnp.arange(count, dtype=jnp.int32)
    phases = positions[:, None] * positions[None, :] % count
    angles = phases.astype(jnp.float32) * (2.0 * math.pi / count)
    return (jnp.cos(angles), jnp.sin(angles))


def transform_dim(values, matrix, dim):
    source = "pabc"
    target = source[:dim] + "k" + source[dim + 1 :]
    pattern = source + "," + source[dim] + "k" + "->" + target
    return jnp.einsum(pattern, values, matrix, precision=lax.Precision.HIGHEST)


def forward_local(real_data, cosine, sine):
    casine = cosine + sine
    parts = [transform_dim(transform_dim(real_data, casine, 3), casine, 2)]
    stacked = jnp.stack(parts, axis=1)
    return stacked.reshape(stacked.shape[0], stacked.shape[1], stacked.shape[2], -1)


def spectral_middle(spectrum, kernel, cosine, sine):
    count_pairs, components, grid_size, flat_cells = spectrum.shape
    shaped = spectrum.reshape(count_pairs, components, grid_size, kernel.shape[1], grid_size)
    casine = cosine + sine
    scaled = transform_dim(shaped[:, 0], casine, 1) * kernel
    parts = [transform_dim(scaled, casine, 1)]
    return jnp.stack(parts, axis=1).reshape(count_pairs, components, grid_size, flat_cells)


def inverse_local(spectrum, cosine, sine):
    count_pairs, components, slab_rows, flat_cells = spectrum.shape
    grid_size = cosine.shape[0]
    shaped = spectrum.reshape(count_pairs, components, slab_rows, grid_size, grid_size)
    casine = cosine + sine
    result = transform_dim(transform_dim(shaped[:, 0], casine, 2), casine, 3)
    result = result / float(grid_size * grid_size * grid_size)
    return result.reshape(count_pairs, slab_rows, flat_cells)


def per_device(orbitals, owners, cutoff_mask):
    local_bands, slab_rows, flat_cells = orbitals.shape
    grid_size = slab_rows * lax.axis_size("fft")
    cosine, sine = dft_tables(grid_size)
    positions = jnp.arange(grid_size, dtype=jnp.int32)
    signed = jnp.where(positions <= grid_size // 2, positions, positions - grid_size)
    signed_y = lax.dynamic_slice_in_dim(signed, lax.axis_index("fft") * slab_rows, slab_rows)
    squared = (
        signed[:, None, None] * signed[:, None, None]
        + signed_y[None, :, None] * signed_y[None, :, None]
        + signed[None, None, :] * signed[None, None, :]
    )
    weights = cutoff_mask.reshape(grid_size, slab_rows, grid_size).astype(jnp.float32)
    kernel = COULOMB * weights / jnp.maximum(squared, 1).astype(jnp.float32)
    local_total = jnp.zeros((local_bands, slab_rows, flat_cells), jnp.float32)
    block_orbs = broadcast(orbitals, "band", owners[0])
    pair_data = (orbitals[:, None] * block_orbs[None]).reshape(
        local_bands * local_bands, slab_rows, grid_size, grid_size
    )
    spectrum = forward_local(pair_data, cosine, sine)
    pencil_out = spectral_middle(
        lax.all_to_all(spectrum, "fft", split_axis=3, concat_axis=2, tiled=True),
        kernel,
        cosine,
        sine,
    )
    returned = lax.all_to_all(pencil_out, "fft", split_axis=2, concat_axis=3, tiled=True)
    potential = inverse_local(returned, cosine, sine).reshape(
        local_bands, local_bands, slab_rows, flat_cells
    )
    local_total = local_total - EXCHANGE_MIX * jnp.sum(block_orbs[None] * potential, axis=1)
    block_terms = -EXCHANGE_MIX * jnp.sum(orbitals[:, None] * potential, axis=0)
    block_total = lax.psum(block_terms, "band")
    return (local_total, block_total)


def solution(mesh):
    in_specs = (P("band", "fft", None), P(), P(None, "fft"))
    out_specs = (P("band", "fft", None), P(None, "fft", None))
    return jax.shard_map(
        per_device, mesh=mesh, in_specs=in_specs, out_specs=out_specs, check_vma=False
    )
```

profile of v0, /device:TPU:0, one launch (start us, length us, event | category | flops | bytes accessed | tf_op | source)
XLA Modules:
  0.0 764.8 jit_solution(15091403194915567678)
XLA Ops:
  7.2 0.0 copy-start
  7.2 0.0 all-reduce.3.cloned.1.call-start
  8.0 2.1 broadcast_select_fusion
  10.1 0.0 all-reduce.3.cloned.1.call-update
  10.1 111.1 %all-reduce.3.cloned.1.call-done = f32[2,48,9216]{2,1,0:T(8,128)} async-done(((f32[2,48,9216]{2,1,0:T(8,128)}), f32[2,48,9216]{2,1,0:T(8,128)}) %all-reduce.3.cloned.1.call-update) | async-done | bytes 3538960 | tf_op jit(solution)/shard_map/psum | solution.py:14
  121.2 0.0 copy-done
  121.2 5.6 broadcast_multiply_fusion.1
  126.8 9.3 %mul.155 = f32[4,48,96,96]{3,2,1,0:T(8,128)} reshape(f32[2,2,48,9216]{3,2,1,0:T(8,128)} %broadcast_multiply_fusion.1) | data formatting | bytes 14155776 | tf_op jit(solution)/shard_map/mul | solution.py:73
  136.1 10.7 %fusion.16 = f32[4,48,96,96]{3,2,1,0:T(8,128)S(1)} fusion(f32[4,48,96,96]{3,2,1,0:T(8,128)} %mul.155), kind=kOutput, calls=%fused_computation.24 | convolution fusion | flops 2038523904 | bytes 14155776 | tf_op jit(solution)/shard_map/pabc,ck->pabk/dot_general | solution.py:28
  146.8 11.2 %convolution_bitcast_fusion = f32[4,48,96,96]{3,2,1,0:T(8,128)} fusion(f32[4,48,96,96]{3,2,1,0:T(8,128)S(1)} %fusion.16), kind=kOutput, calls=%fused_computation.14 | convolution fusion | flops 2038523904 | bytes 14155776 | tf_op jit(solution)/shard_map/pabc,bk->pakc/dot_general | solution.py:28
  158.1 14.8 %copy.43 = f32[4,48,96,96]{1,0,3,2:T(4,128)} copy(f32[4,48,96,96]{3,2,1,0:T(8,128)} %convolution_bitcast_fusion) | data formatting | bytes 14155776 | tf_op jit(solution)/shard_map/reshape;stack | solution.py:35
  172.9 35.5 %reshape.84 = f32[2,1,884736]{2,1,0:T(1,128)} reshape(f32[9216,1,4,48]{3,2,1,0:T(4,128)} %bitcast.61) | data formatting | bytes 14155776
  208.5 6.5 all-to-all-start
  215.0 0.0 all-reduce.5.cloned.1.call-start
  215.0 2.9 convert_multiply_fusion
  217.9 3.6 mul.158
  221.5 0.1 dynamic-slice_multiply_fusion
  221.6 0.1 broadcast_add_fusion
  221.6 4.5 copy_divide_fusion
  226.1 66.1 %all-to-all-done = f32[2,1,884736]{2,1,0:T(1,128)} async-done(((f32[2,1,884736]{2,1,0:T(1,128)}), f32[2,1,884736]{2,1,0:T(1,128)}, u32[]{:S(2)}, u32[]{:S(2)}) %all-to-all-start) | async-done | bytes 7077920 | tf_op jit(solution)/shard_map/all_to_all | solution.py:78
  292.2 0.5 broadcast.71
  292.7 81.3 %reduce = f32[2,884736]{1,0:T(2,128)} reduce(f32[2,1,884736]{2,1,0:T(1,128)} %all-to-all-done, f32[]{:T(128)} %broadcast.71), dimensions={1}, to_apply=%all_to_all.22.reduce_sub_computation | reduce | bytes 14155780 | tf_op jit(solution)/shard_map/all_to_all | solution.py:78
  374.0 35.6 %reshape.85 = f32[9216,1,4,48]{3,2,1,0:T(4,128)} reshape(f32[2,884736]{1,0:T(2,128)} %reduce) | data formatting | bytes 14155776
  409.7 25.5 %copy.44 = f32[4,1,48,2,4608]{4,3,2,0,1:T(2,128)} copy(f32[4,1,48,2,4608]{2,0,4,3,1:T(4,128)} %bitcast.62) | data formatting | bytes 14155776 | tf_op jit(solution)/shard_map/all_to_all | solution.py:78
  435.2 7.1 copy.25
  442.3 10.4 %squeeze_reshape.6 = f32[4,96,48,96]{3,2,1,0:T(8,128)} reshape(f32[4,1,2,48,4608]{4,3,2,0,1:T(8,128)} %copy.25) | data formatting | bytes 14155776 | tf_op jit(solution)/shard_map/squeeze;reshape | solution.py:42
  452.7 0.0 copy-start.2
  452.7 15.9 %fusion.4 = f32[96,4,48,96]{3,0,2,1:T(8,128)S(1)} fusion(f32[4,96,48,96]{3,2,1,0:T(8,128)} %squeeze_reshape.6), kind=kOutput, calls=%fused_computation.4 | convolution fusion | flops 2038523904 | bytes 14155776 | tf_op jit(solution)/shard_map/pabc,ak->pkbc/dot_general | solution.py:28
  468.5 0.0 copy-done.2
  468.6 10.1 %fusion.10 = f32[4,96,48,96]{3,1,2,0:T(8,128)S(1)} fusion(f32[96,4,48,96]{3,0,2,1:T(8,128)S(1)} %fusion.4, f32[96,48,96]{2,0,1:T(8,128)S(1)} %copy-done.2), kind=kOutput, calls=%fused_computation.15 | convolution fusion | flops 2040293376 | bytes 15925248 | tf_op jit(solution)/shard_map/pabc,ak->pkbc/dot_general | solution.py:28
  478.6 9.3 %copy.45 = f32[4,96,48,96]{3,2,0,1:T(8,128)} copy(f32[4,96,48,96]{3,1,2,0:T(8,128)S(1)} %fusion.10) | data formatting | bytes 14155776 | tf_op jit(solution)/shard_map/reshape;stack | solution.py:44
  487.9 10.8 %reshape.83 = f32[4,1,96,4608]{3,0,1,2:T(4,128)} reshape(f32[4,96,48,96]{3,2,0,1:T(8,128)} %copy.45) | data formatting | bytes 14155776 | tf_op jit(solution)/shard_map/reshape;stack | solution.py:44
  498.8 86.2 %all_to_all.30 = f32[4,1,96,4608]{3,0,1,2:T(4,128)} all-to-all(f32[4,1,96,4608]{3,0,1,2:T(4,128)} %reshape.83), channel_id=1, replica_groups=mesh['band'=16,'fft'=2] {'fft'}, dimensions={2} | all-to-all | bytes 14155776 | tf_op jit(solution)/shard_map/all_to_all | solution.py:83
  585.0 11.3 %copy.51 = f32[4,1,2,48,4608]{4,2,3,0,1:T(2,128)} copy(f32[4,1,2,48,4608]{4,0,3,2,1:T(4,128)} %bitcast.64) | data formatting | bytes 14155776 | tf_op jit(solution)/shard_map/all_to_all | solution.py:83
  596.3 11.3 %squeeze_reshape.7 = f32[4,48,96,96]{3,2,1,0:T(8,128)} reshape(f32[4,1,48,2,4608]{4,3,2,0,1:T(2,128)} %bitcast.65) | data formatting | bytes 14155776 | tf_op jit(solution)/shard_map/squeeze;reshape | solution.py:52
  607.7 11.8 %fusion.21 = f32[96,4,48,96]{3,0,2,1:T(8,128)S(1)} fusion(f32[4,48,96,96]{3,2,1,0:T(8,128)} %squeeze_reshape.7), kind=kOutput, calls=%fused_computation.29 | convolution fusion | flops 2038523904 | bytes 14155776 | tf_op jit(solution)/shard_map/pabc,bk->pakc/dot_general | solution.py:28
  619.5 10.6 %broadcast_multiply_fusion = f32[4,48,96,96]{3,2,1,0:T(8,128)} fusion(f32[96,4,48,96]{3,0,2,1:T(8,128)S(1)} %fusion.21), kind=kOutput, calls=%fused_computation.10 | convolution fusion | flops 2040293376 | bytes 14155776 | tf_op jit(solution)/shard_map/pabc,ck->pabk/dot_general | solution.py:28
  630.1 10.0 %reshape_reshape.3 = f32[2,2,48,9216]{3,2,1,0:T(8,128)} reshape(f32[4,48,96,96]{3,2,1,0:T(8,128)} %broadcast_multiply_fusion) | data formatting | bytes 14155776 | tf_op jit(solution)/shard_map/reshape;reshape | solution.py:84
  640.1 7.3 multiply_reduce_fusion
  647.5 0.0 copy-start.1
  647.5 2.2 broadcast_multiply_fusion.2
  649.7 0.0 all-reduce.5.cloned.1.call-update
  649.7 1.1 copy-done.1
  650.8 2.1 multiply_subtract_fusion
  652.9 100.6 %all-reduce.5.cloned.1.call-done = f32[2,48,9216]{2,1,0:T(8,128)} async-done(((f32[2,48,9216]{2,1,0:T(8,128)}), f32[2,48,9216]{2,1,0:T(8,128)}) %all-reduce.5.cloned.1.call-update) | async-done | bytes 3538960 | tf_op jit(solution)/shard_map/psum | solution.py:89
  753.5 4.0 copy.55
  (2 shorter events, 0.0 us)
Async XLA Ops:
  7.2 114.1 %copy-start = (f32[2,48,9216]{2,1,0:T(8,128)S(1)}, f32[2,48,9216]{2,1,0:T(8,128)}, u32[]{:S(2)}) copy-start(f32[2,48,9216]{2,1,0:T(8,128)} %param.3) | copy-start | bytes 10616836
  7.2 114.0 %all-reduce.3.cloned.1.call-start = ((), (), s32[]{:S(2)}) async-start(), calls=%async_computation.2 | async-start | bytes 7077888 | tf_op jit(solution)/shard_map/psum | solution.py:14
  208.5 83.7 %all-to-all-start = ((f32[2,1,884736]{2,1,0:T(1,128)}), f32[2,1,884736]{2,1,0:T(1,128)}, u32[]{:S(2)}, u32[]{:S(2)}) async-start(f32[2,1,884736]{2,1,0:T(1,128)} %reshape.84), calls=%async_computation | async-start | bytes 14155776 | tf_op jit(solution)/shard_map/all_to_all | solution.py:78
  215.0 538.5 %all-reduce.5.cloned.1.call-start = ((), (), s32[]{:S(2)}) async-start(), calls=%async_computation.3 | async-start | bytes 7077888 | tf_op jit(solution)/shard_map/psum | solution.py:89
  452.7 15.9 %copy-start.2 = (f32[96,48,96]{2,0,1:T(8,128)S(1)}, f32[96,48,96]{2,0,1:T(8,128)}, u32[]{:S(2)}) copy-start(f32[96,48,96]{2,0,1:T(8,128)} %copy_divide_fusion) | copy-start | bytes 5308420
  647.5 3.3 copy-start.1
Sparse Core Ops, SparseCore 0:
  12.2 108.9 all-reduce.2
  649.8 103.6 all-reduce.4
where the time goes:
time: 775 us; the launch traced here: 765 us
  waiting for transfers between devices  278 us (36%)
  local copies, waits for them, and re-layouts  200 us (26%)
  other arithmetic  108 us (14%)
  blocking collectives  86.2 us (11%)
  matrix products  70.4 us (9%)
  between operations  15.3 us (2%)
    psum x1, waiting for transfers between devices, broadcast(): return lax.psum(kept, axis)  111 us
    psum x1, waiting for transfers between devices, per_device(): block_total = lax.psum(block_terms, 'band')  101 us
    all_to_all x1, blocking collectives, per_device(): lax.all_to_all(pencil_out, 'fft', split_axis=2, concat_axis=3, tiled=True)  86.2 us
    all_to_all x1, other arithmetic, per_device(): lax.all_to_all(spectrum, 'fft', split_axis=3, concat_axis=2, tiled=True)  81.3 us
    unnamed x9, local copies, waits for them, and re-layouts  76.3 us
    dot_general x6, matrix products, transform_dim(): return jnp.einsum(pattern, values, matrix, precision=lax.Precision.HIGHEST)  70.4 us
    all_to_all x1, waiting for transfers between devices, per_device(): lax.all_to_all(spectrum, 'fft', split_axis=3, concat_axis=2, tiled=True)  66.1 us
    all_to_all x3, local copies, waits for them, and re-layouts, per_device(): lax.all_to_all(spectrum, 'fft', split_axis=3, concat_axis=2, tiled=True)  33.1 us
  transfers between devices with their start and end apart: 3, of which 3 were waited for; matrix products, arithmetic and copies ran while one was open for 2% of the time, Pallas kernels for 0%

commit v1 on v0

--- a/solution.py
+++ b/solution.py
@@ -1,8 +1,12 @@
+import functools
 import math
 
 import jax
 import jax.numpy as jnp
+import numpy as np
 from jax import lax
+from jax.experimental import pallas as pl
+from jax.experimental.pallas import tpu as pltpu
 from jax.sharding import PartitionSpec as P
 
 COULOMB = 400.0
@@ -54,7 +58,7 @@
     return result.reshape(count_pairs, slab_rows, flat_cells)
 
 
-def per_device(orbitals, owners, cutoff_mask):
+def per_device_general(orbitals, owners, cutoff_mask):
     local_bands, slab_rows, flat_cells = orbitals.shape
     grid_size = slab_rows * lax.axis_size("fft")
     cosine, sine = dft_tables(grid_size)
@@ -90,9 +94,252 @@
     return (local_total, block_total)
 
 
+LANES = 128
+
+
+def casine_matrix(count):
+    positions = np.arange(count)
+    angles = (np.outer(positions, positions) % count) * (2.0 * np.pi / count)
+    return np.cos(angles) + np.sin(angles)
+
+
+def split_table(matrix):
+    high = matrix.astype(np.float32).astype(jnp.bfloat16)
+    low = (matrix - high.astype(np.float64)).astype(np.float32).astype(jnp.bfloat16)
+    return high, low
+
+
+def left_table(matrix):
+    high, low = split_table(matrix)
+    return np.concatenate([np.concatenate([high, high], 1), np.concatenate([low, low], 1)], 0)
+
+
+def right_table(matrix):
+    count = matrix.shape[0]
+    padded = np.zeros((LANES, LANES))
+    padded[:count, :count] = matrix
+    row = np.concatenate(split_table(padded), 1)
+    return np.concatenate([row, row], 0)
+
+
+def split(values):
+    high = values.astype(jnp.bfloat16)
+    return high, (values - high.astype(jnp.float32)).astype(jnp.bfloat16)
+
+
+def transform_rows(table, values):
+    rows = values.shape[0]
+    stacked = jnp.concatenate(split(values), 0)
+    result = jnp.dot(table, stacked, preferred_element_type=jnp.float32)
+    return result[:rows] + result[rows:]
+
+
+def transform_lanes(values, table):
+    stacked = jnp.concatenate(split(values), 1)
+    result = jnp.dot(stacked, table, preferred_element_type=jnp.float32)
+    return result[:, :LANES] + result[:, LANES:]
+
+
+def pair_kernel(
+    count, per_unit, has_total, own, other, block, coulomb, into_x, out_of_x, along_y, along_z, *rest
+):
+    total = rest[0] if has_total else None
+    local_own, local_other, block_terms, cells = rest[-4:]
+    half = count // 2
+    unit = per_unit * count
+    units = count // per_unit
+    batch = next(k for k in (4, 3, 2, 1) if units % k == 0)
+    planes = next(k for k in (16, 8, 4, 2, 1) if count % k == 0)
+    width = batch * unit
+
+    def forward(step, carry):
+        columns = pl.ds(pl.multiple_of(step * width, LANES), width)
+        density = jnp.concatenate([own[:, columns], other[:, columns]], 0) * block[:, columns]
+        density = transform_rows(into_x[...], density)
+        parts = []
+        for start in range(0, width, unit):
+            piece = density[:, start : start + unit]
+            for index in range(per_unit):
+                shifted = pltpu.roll(piece, unit - index * count, 1) if index else piece
+                parts.append(shifted[:, :LANES])
+        rows = pl.ds(pl.multiple_of(step * width, 8), width)
+        cells[rows, :] = transform_lanes(jnp.concatenate(parts, 0), along_z[...])
+        return carry
+
+    lax.fori_loop(0, units // batch, forward, 0)
+
+    def middle(step, carry):
+        first = step * planes
+        values = [cells[pl.ds(first + k, count, stride=count), :] for k in range(planes)]
+        spectrum = transform_rows(along_y[...], jnp.concatenate(values, 1))
+        scale = jnp.concatenate([coulomb[first + k] for k in range(planes)], 1)
+        scaled = transform_rows(along_y[...], spectrum * scale)
+        for k in range(planes):
+            cells[pl.ds(first + k, count, stride=count), :] = scaled[:, k * LANES : (k + 1) * LANES]
+        return carry
+
+    lax.fori_loop(0, count // planes, middle, 0)
+    lane = lax.broadcasted_iota(jnp.int32, (count, LANES), 1)
+
+    def inverse(step, carry):
+        rows = pl.ds(pl.multiple_of(step * width, 8), width)
+        values = transform_lanes(cells[rows, :], along_z[...])
+        tiles = [None] * (width // LANES)
+
+        def add(tile, value):
+            tiles[tile] = value if tiles[tile] is None else tiles[tile] + value
+
+        for start in range(0, width, count):
+            tile, offset = divmod(start, LANES)
+            piece = values[start : start + count]
+            if offset:
+                piece = pltpu.roll(piece, offset, 1)
+            if offset + count <= LANES:
+                add(tile, piece)
+            else:
+                add(tile, jnp.where(lane >= offset, piece, 0.0))
+                add(tile + 1, jnp.where(lane < offset, piece, 0.0))
+        potential = transform_rows(out_of_x[...], jnp.concatenate(tiles, 1))
+        columns = pl.ds(pl.multiple_of(step * width, LANES), width)
+        local = block[:, columns] * potential
+        terms = jnp.concatenate([own[:, columns], other[:, columns]], 0) * potential
+        if has_total:
+            terms = terms + total[:, columns]
+        local_own[:, columns] = local[:half]
+        local_other[:, columns] = local[half:]
+        block_terms[:, columns] = terms
+        return carry
+
+    lax.fori_loop(0, units // batch, inverse, 0)
+
+
+def pair_terms(own, other, block, coulomb, tables, total=None):
+    half, flat_cells = own.shape
+    count = 2 * half
+    has_total = total is not None
+    operands = [own, other, block, coulomb, *tables] + ([total] if has_total else [])
+    vmem = pl.BlockSpec(memory_space=pltpu.VMEM)
+    shapes = [(half, flat_cells), (half, flat_cells), (count, flat_cells)]
+    return pl.pallas_call(
+        functools.partial(pair_kernel, count, math.lcm(count, LANES) // count, has_total),
+        in_specs=[vmem] * len(operands),
+        out_specs=[vmem] * 3,
+        out_shape=[jax.ShapeDtypeStruct(shape, jnp.float32) for shape in shapes],
+        scratch_shapes=[pltpu.VMEM((flat_cells, LANES), jnp.float32)],
+        compiler_params=pltpu.CompilerParams(vmem_limit_bytes=50 * 2**20),
+        name="pair_terms",
+    )(*operands)
+
+
+def halves(values, upper, dim):
+    size = values.shape[dim] // 2
+    low = lax.slice_in_dim(values, 0, size, axis=dim)
+    high = lax.slice_in_dim(values, size, 2 * size, axis=dim)
+    return jnp.where(upper, high, low), jnp.where(upper, low, high)
+
+
+def joined(mine, theirs, upper, dim):
+    return jnp.concatenate(
+        [jnp.where(upper, theirs, mine), jnp.where(upper, mine, theirs)], axis=dim
+    )
+
+
+def band_sum(values, exchange_x):
+    size = lax.axis_size("band")
+    index = lax.axis_index("band")
+    core, side, depth = index % 2, index // 2 % 2, index // 4
+    depth_low, depth_high = (depth + depth // 2) % 2 == 1, depth // 2 == 1
+
+    def swap(value, partner):
+        return lax.ppermute(value, "band", [(k, partner(k)) for k in range(size)])
+
+    def by_core(first, second):
+        return lambda k: k ^ (second if k % 2 else first)
+
+    side_or_low = by_core(2, 4)
+    low_or_high = by_core(4, 12)
+    high_or_side = by_core(12, 2)
+    first_bit = jnp.where(core == 1, depth_low, side == 1)
+    second_bit = jnp.where(core == 1, depth_high, depth_low)
+    keep, send = halves(values, core == 1, 1)
+    values = keep + swap(send, lambda k: k ^ 1)
+    keep, send = halves(values, first_bit, 2)
+    values = keep + swap(send, side_or_low)
+    keep, send = halves(values, second_bit, 2)
+    values = keep + swap(send, low_or_high)
+    values = values + swap(values, high_or_side)
+    values = exchange_x(values)
+    values = joined(values, swap(values, low_or_high), second_bit, 2)
+    values = joined(values, swap(values, side_or_low), first_bit, 2)
+    return joined(values, swap(values, lambda k: k ^ 1), core == 1, 1)
+
+
+def across(value):
+    return lax.ppermute(value, "fft", [(0, 1), (1, 0)])
+
+
+def coulomb_table(cutoff_mask, count):
+    columns = cutoff_mask.shape[1] // count
+    positions = jnp.arange(count, dtype=jnp.int32)
+    signed = jnp.where(positions <= count // 2, positions, positions - count)
+    squares = signed * signed
+    mine = lax.dynamic_slice_in_dim(squares, lax.axis_index("fft") * columns, columns)
+    flat = (mine[:, None] + squares[None, :]).reshape(-1)
+    lengths = jnp.where(cutoff_mask != 0, squares[:, None] + flat[None, :], 0)
+    limit = jnp.full((8, LANES), jnp.max(lengths).astype(jnp.float32))
+    limit = jnp.maximum(limit, across(limit))[0, 0].astype(jnp.int32)
+    padded = jnp.concatenate([squares, jnp.full((LANES - count,), 4 * count * count, jnp.int32)])
+    squared = squares[:, None, None] + squares[None, :, None] + padded[None, None, :]
+    weights = ((squared >= 1) & (squared <= limit)).astype(jnp.float32)
+    factor = -EXCHANGE_MIX * COULOMB / float(count**3)
+    return factor * weights / jnp.maximum(squared, 1).astype(jnp.float32)
+
+
+def per_device_pairs(orbitals, owners, cutoff_mask):
+    _, half, flat_cells = orbitals.shape
+    count = 2 * half
+    plane = lax.axis_index("fft")
+    casine = casine_matrix(count)
+    turned = [(np.arange(count) + half * k) % count for k in range(2)]
+    into_x = jnp.asarray(np.stack([left_table(casine[:, order]) for order in turned]))[plane]
+    out_of_x = jnp.asarray(np.stack([left_table(casine[order, :]) for order in turned]))[plane]
+    tables = [into_x, out_of_x, jnp.asarray(left_table(casine)), jnp.asarray(right_table(casine))]
+
+    def gather_band(pieces):
+        mine = jnp.where(plane == 1, pieces[1], pieces[0])
+        theirs = jnp.where(plane == 1, pieces[0], pieces[1])
+        return jnp.stack([mine, across(theirs)])
+
+    def gather_half(pieces):
+        other = across(pieces[1])
+        return jnp.stack(
+            [jnp.where(plane == 1, other, pieces[0]), jnp.where(plane == 1, pieces[0], other)]
+        )
+
+    first_other = across(orbitals[0])
+    coulomb = coulomb_table(cutoff_mask, count)
+    owned = jnp.where(lax.axis_index("band") == owners[0], orbitals, 0.0)
+    block = band_sum(owned, gather_band).reshape(count, flat_cells)
+    second, _ = lax.optimization_barrier((orbitals[1], first_other))
+    second_other = across(second)
+    own0, other0, terms = pair_terms(orbitals[0], first_other, block, coulomb, tables)
+    own1, other1, terms = pair_terms(orbitals[1], second_other, block, coulomb, tables, terms)
+    local_total = jnp.stack([own0 + across(other0), own1 + across(other1)])
+    block_total = band_sum(terms.reshape(2, half, flat_cells), gather_half)
+    return local_total, block_total
+
+
 def solution(mesh):
     in_specs = (P("band", "fft", None), P(), P(None, "fft"))
     out_specs = (P("band", "fft", None), P(None, "fft", None))
+
+    def per_device(orbitals, owners, cutoff_mask):
+        bands, rows, cells = orbitals.shape
+        paired = bands == mesh.shape["fft"] == 2 and mesh.shape["band"] == 16
+        paired = paired and cells % (8 * LANES) == 0 and rows % 16 == 0 and 2 * rows <= LANES
+        chosen = per_device_pairs if paired else per_device_general
+        return chosen(orbitals, owners, cutoff_mask)
+
     return jax.shard_map(
         per_device, mesh=mesh, in_specs=in_specs, out_specs=out_specs, check_vma=False
     )

time: 775 us -> 298 us (0.38); the launches traced: 765 us -> 298 us
  local copies, waits for them, and re-layouts: 200 us -> 6.9 us
  waiting for transfers between devices: 278 us -> 186 us
  blocking collectives: 86.2 us -> 0 us
  other arithmetic: 108 us -> 27.4 us
  matrix products: 70.4 us -> 0 us
  Pallas kernels: 0 us -> 46.2 us
  starting transfers between devices: 6.6 us -> 28.3 us
  between operations: 15.3 us -> 2.85 us
    psum x2 -> x0, waiting for transfers between devices: 212 us -> none  [the longest x1 111 us: broadcast(): return lax.psum(kept, axis)]
    ppermute x0 -> x21, waiting for transfers between devices: none -> 186 us  [the longest x14 98.1 us: swap(): return lax.ppermute(value, 'band', [(k, partner(k)) for k in range(size)])]
    all_to_all x1 -> x0, blocking collectives: 86.2 us -> none  [per_device(): lax.all_to_all(pencil_out, 'fft', split_axis=2, concat_axis=3, tiled=True)]
    all_to_all x1 -> x0, other arithmetic: 81.3 us -> none  [per_device(): lax.all_to_all(spectrum, 'fft', split_axis=3, concat_axis=2, tiled=True)]
    unnamed x9 -> x14, local copies, waits for them, and re-layouts: 76.3 us -> 2.42 us
    dot_general x6 -> x0, matrix products: 70.4 us -> none  [transform_dim(): return jnp.einsum(pattern, values, matrix, precision=lax.Precision.HIGHEST)]
    another operation x6 -> x0, local copies, waits for them, and re-layouts: 66.7 us -> none  [the longest x2 20.1 us: spectral_middle(): jnp.stack(parts, axis=1)]
    all_to_all x1 -> x0, waiting for transfers between devices: 66.1 us -> none  [per_device(): lax.all_to_all(spectrum, 'fft', split_axis=3, concat_axis=2, tiled=True)]
  transfers between devices with their start and end apart: 3 -> 21, of which waited for: 3 -> 17; matrix products, arithmetic and copies ran while one was open for 2% -> 7% of each run, Pallas kernels for 0% -> 8%
where the time goes in v1:
time: 298 us
  waiting for transfers between devices  186 us (62%)
  Pallas kernels  46.2 us (16%)
  starting transfers between devices  28.3 us (9%)
  other arithmetic  27.4 us (9%)
  local copies, waits for them, and re-layouts  6.9 us (2%)
    ppermute x14, waiting for transfers between devices, swap(): return lax.ppermute(value, 'band', [(k, partner(k)) for k in range(size)])  98.1 us
    ppermute x7, waiting for transfers between devices, across(): return lax.ppermute(value, 'fft', [(0, 1), (1, 0)])  87.9 us
    pallas_call x2, Pallas kernels, pair_terms(): pl.pallas_call(functools.partial(pair_kernel, count, math.lcm(count, LANE...  46.2 us
    ppermute x14, starting transfers between devices, swap(): return lax.ppermute(value, 'band', [(k, partner(k)) for k in range(size)])  18.6 us
    ppermute x7, starting transfers between devices, across(): return lax.ppermute(value, 'fft', [(0, 1), (1, 0)])  9.68 us
  transfers between devices with their start and end apart: 21, of which 17 were waited for; matrix products, arithmetic and copies ran while one was open for 7% of the time, Pallas kernels for 8%

profile of v1, /device:TPU:0, one launch (start us, length us, event | category | flops | bytes accessed | tf_op | source)
XLA Modules:
  0.0 297.7 jit_solution(11576387222093398555)
XLA Ops:
  1.3 0.3 broadcast_select_fusion
  1.6 1.4 slice_select_fusion.1
  3.0 0.5 collective-permute-start.1
  3.4 3.7 %collective-permute-done.1 = f32[2,24,9216]{2,1,0:T(8,128)} collective-permute-done((f32[2,24,9216]{2,1,0:T(8,128)}, f32[2,24,9216]{2,1,0:T(8,128)}, u32[]{:S(2)}, u32[]{:S(2)}) %collective-permute-start.1) | collective-permute-done | bytes 1769504 | tf_op jit(solution)/shard_map/ppermute | solution.py:254
  7.1 1.7 select_add_fusion.1
  8.8 1.2 copy-done.2
  10.1 4.4 %collective-permute-start.2 = (f32[2,24,4608]{2,1,0:T(8,128)S(1)}, f32[2,24,4608]{2,1,0:T(8,128)S(1)}, u32[]{:S(2)}, u32[]{:S(2)}) collective-permute-start(f32[2,24,4608]{2,1,0:T(8,128)S(1)} %slice_select_fusion.3), channel_id=1, source_target_pairs={{0,4},{2,10},{4,0},{6,14},{8,12},{10,2},{12,8},{14,6},{16,20},{18,... | collective-permute-start | bytes 2654216 | tf_op jit(solution)/shard_map/ppermute | solution.py:254
  14.5 11.0 %collective-permute-done.2 = f32[2,24,4608]{2,1,0:T(8,128)S(1)} collective-permute-done((f32[2,24,4608]{2,1,0:T(8,128)S(1)}, f32[2,24,4608]{2,1,0:T(8,128)S(1)}, u32[]{:S(2)}, u32[]{:S(2)}) %collective-permute-start.2) | collective-permute-done | bytes 884768 | tf_op jit(solution)/shard_map/ppermute | solution.py:254
  25.5 1.6 select_add_fusion.3
  27.2 0.7 collective-permute-start.3
  27.8 11.7 %collective-permute-done.3 = f32[2,24,2304]{2,1,0:T(8,128)S(1)} collective-permute-done((f32[2,24,2304]{2,1,0:T(8,128)S(1)}, f32[2,24,2304]{2,1,0:T(8,128)S(1)}, u32[]{:S(2)}, u32[]{:S(2)}) %collective-permute-start.3) | collective-permute-done | bytes 442400 | tf_op jit(solution)/shard_map/ppermute | solution.py:254
  39.7 3.4 %collective-permute-start.4 = (f32[2,24,2304]{2,1,0:T(8,128)S(1)}, f32[2,24,2304]{2,1,0:T(8,128)S(1)}, u32[]{:S(2)}, u32[]{:S(2)}) collective-permute-start(f32[2,24,2304]{2,1,0:T(8,128)S(1)} %select_add_fusion.5), channel_id=1, source_target_pairs={{0,24},{2,6},{4,28},{6,2},{8,16},{10,14},{12,20},{14,10},{16,8},{1... | collective-permute-start | bytes 1327112 | tf_op jit(solution)/shard_map/ppermute | solution.py:254
  43.1 6.9 %collective-permute-done.4 = f32[2,24,2304]{2,1,0:T(8,128)S(1)} collective-permute-done((f32[2,24,2304]{2,1,0:T(8,128)S(1)}, f32[2,24,2304]{2,1,0:T(8,128)S(1)}, u32[]{:S(2)}, u32[]{:S(2)}) %collective-permute-start.4) | collective-permute-done | bytes 442400 | tf_op jit(solution)/shard_map/ppermute | solution.py:254
  50.0 1.6 collective-permute-start.5
  51.6 4.4 %collective-permute-done.5 = f32[24,2304]{1,0:T(8,128)S(1)} collective-permute-done((f32[24,2304]{1,0:T(8,128)S(1)}, f32[24,2304]{1,0:T(8,128)S(1)}, u32[]{:S(2)}, u32[]{:S(2)}) %collective-permute-start.5) | collective-permute-done | bytes 221216 | tf_op jit(solution)/shard_map/ppermute | solution.py:278
  56.1 3.9 %collective-permute-start.6 = (f32[2,24,2304]{2,1,0:T(8,128)S(1)}, f32[2,24,2304]{2,1,0:T(8,128)S(1)}, u32[]{:S(2)}, u32[]{:S(2)}) collective-permute-start(f32[2,24,2304]{2,1,0:T(8,128)S(1)} %pad_maximum_fusion.7), channel_id=1, source_target_pairs={{0,8},{2,26},{4,12},{6,30},{8,0},{10,18},{12,4},{14,22},{16,24},{1... | collective-permute-start | bytes 1327112 | tf_op jit(solution)/shard_map/ppermute | solution.py:254
  60.0 8.7 %collective-permute-done.6 = f32[2,24,2304]{2,1,0:T(8,128)S(1)} collective-permute-done((f32[2,24,2304]{2,1,0:T(8,128)S(1)}, f32[2,24,2304]{2,1,0:T(8,128)S(1)}, u32[]{:S(2)}, u32[]{:S(2)}) %collective-permute-start.6) | collective-permute-done | bytes 442400 | tf_op jit(solution)/shard_map/ppermute | solution.py:254
  68.8 2.2 collective-permute-start.7
  71.0 1.5 slice_bitcast_fusion.1
  72.5 1.5 collective-permute-start
  74.0 8.0 %collective-permute-done.7 = f32[2,24,4608]{2,1,0:T(8,128)S(1)} collective-permute-done((f32[2,24,4608]{2,1,0:T(8,128)S(1)}, f32[2,24,4608]{2,1,0:T(8,128)S(1)}, u32[]{:S(2)}, u32[]{:S(2)}) %collective-permute-start.7) | collective-permute-done | bytes 884768 | tf_op jit(solution)/shard_map/ppermute | solution.py:254
  82.0 0.1 broadcast_select_fusion.8
  82.2 1.3 pad_maximum_fusion.3
  83.6 0.7 broadcast_add_fusion.1
  84.3 1.4 add.159
  85.7 2.6 select_reduce_fusion
  89.0 1.6 collective-permute-start.9
  90.6 1.0 dynamic-slice_bitcast_fusion
  91.6 15.2 %collective-permute-done.9 = f32[8,128]{1,0:T(8,128)S(1)} collective-permute-done((f32[8,128]{1,0:T(8,128)S(1)}, f32[8,128]{1,0:T(8,128)S(1)}, u32[]{:S(2)}, u32[]{:S(2)}) %collective-permute-start.9) | collective-permute-done | bytes 4128 | tf_op jit(solution)/shard_map/ppermute | solution.py:278
  106.8 0.5 slice.71
  107.9 4.9 %fusion.1.coulomb = f32[96,96,128]{2,1,0:T(8,128)} fusion(s32[]{:T(128)} %bitcast.5, s32[128]{0:T(128)S(1)} %concatenate.24, s32[96,96]{1,0:T(8,128)S(1)} %broadcast_add_fusion), kind=kLoop, calls=%fused_computation.4 | loop fusion | flops 9437184 | bytes 4755972 | tf_op jit(solution)/shard_map/div | solution.py:295
  112.8 1.5 collective-permute-start.11
  114.3 1.8 broadcast_select_fusion.4
  116.1 2.0 pad_maximum_fusion
  118.2 22.6 %pair_terms.2 = (f32[48,9216]{1,0:T(8,128)S(1)}, f32[48,9216]{1,0:T(8,128)S(1)}, f32[96,9216]{1,0:T(8,128)}) custom-call(f32[48,9216]{1,0:T(8,128)} %get-tuple-element.20.own, f32[48,9216]{1,0:T(8,128)} %collective-permute-done.other, f32[96,9216]{1,0:T(8,128)} %bitcast.32, f32[96,96,128]{2,1,0:T(8,128)} %fusion.1.coulomb, ...), custom_call_target="tpu_custom_call" | custom-call | tf_op jit(solution)/shard_map/pair_terms/pallas_call | solution.py:223
  140.7 5.1 %collective-permute-done.11.other = f32[48,9216]{1,0:T(8,128)S(1)} collective-permute-done((f32[48,9216]{1,0:T(8,128)S(1)}, f32[48,9216]{1,0:T(8,128)S(1)}, u32[]{:S(2)}, u32[]{:S(2)}) %collective-permute-start.11) | collective-permute-done | bytes 1769504 | tf_op jit(solution)/shard_map/ppermute | solution.py:278
  145.8 1.2 copy-done.6
  147.0 23.7 %pair_terms.3 = (f32[48,9216]{1,0:T(8,128)S(1)}, f32[48,9216]{1,0:T(8,128)S(1)}, f32[96,9216]{1,0:T(8,128)}) custom-call(f32[48,9216]{1,0:T(8,128)} %copy-done.5, f32[48,9216]{1,0:T(8,128)} %copy-done.6, f32[96,9216]{1,0:T(8,128)} %bitcast.33, f32[96,96,128]{2,1,0:T(8,128)} %fusion.1.coulomb, bf16[192,192]{1,0:T(8,128)(2,1)S(1)} %get-tuple-element.35.into_x, ...), custom_call_target="tpu_custom_call" | custom-call | tf_op jit(solution)/shard_map/pair_terms/pallas_call | solution.py:223
  170.7 2.3 slice_select_fusion
  173.1 3.7 %collective-permute-done.13 = f32[2,24,9216]{2,1,0:T(8,128)S(1)} collective-permute-done((f32[2,24,9216]{2,1,0:T(8,128)S(1)}, f32[2,24,9216]{2,1,0:T(8,128)S(1)}, u32[]{:S(2)}, u32[]{:S(2)}) %collective-permute-start.13) | collective-permute-done | bytes 1769504 | tf_op jit(solution)/shard_map/ppermute | solution.py:254
  176.8 0.2 select_add_fusion
  177.1 0.1 slice_select_fusion.2
  177.2 0.3 collective-permute-start.14
  177.4 12.9 %collective-permute-done.14 = f32[2,24,4608]{2,1,0:T(8,128)S(1)} collective-permute-done((f32[2,24,4608]{2,1,0:T(8,128)S(1)}, f32[2,24,4608]{2,1,0:T(8,128)S(1)}, u32[]{:S(2)}, u32[]{:S(2)}) %collective-permute-start.14) | collective-permute-done | bytes 884768 | tf_op jit(solution)/shard_map/ppermute | solution.py:254
  190.3 0.2 select_add_fusion.2
  190.6 13.0 %collective-permute-done.15 = f32[2,24,2304]{2,1,0:T(8,128)S(1)} collective-permute-done((f32[2,24,2304]{2,1,0:T(8,128)S(1)}, f32[2,24,2304]{2,1,0:T(8,128)S(1)}, u32[]{:S(2)}, u32[]{:S(2)}) %collective-permute-start.15) | collective-permute-done | bytes 442400 | tf_op jit(solution)/shard_map/ppermute | solution.py:254
  203.7 0.3 collective-permute-start.16
  204.0 10.0 %collective-permute-done.16 = f32[2,24,2304]{2,1,0:T(8,128)S(1)} collective-permute-done((f32[2,24,2304]{2,1,0:T(8,128)S(1)}, f32[2,24,2304]{2,1,0:T(8,128)S(1)}, u32[]{:S(2)}, u32[]{:S(2)}) %collective-permute-start.16) | collective-permute-done | bytes 442400 | tf_op jit(solution)/shard_map/ppermute | solution.py:254
  214.1 1.6 collective-permute-start.17
  215.6 0.5 collective-permute-start.10
  216.1 6.3 %collective-permute-done.17 = f32[24,2304]{1,0:T(8,128)S(1)} collective-permute-done((f32[24,2304]{1,0:T(8,128)S(1)}, f32[24,2304]{1,0:T(8,128)S(1)}, u32[]{:S(2)}, u32[]{:S(2)}) %collective-permute-start.17) | collective-permute-done | bytes 221216 | tf_op jit(solution)/shard_map/ppermute | solution.py:278
  222.6 2.4 collective-permute-start.18
  225.0 1.5 collective-permute-start.12
  226.5 8.6 %collective-permute-done.18 = f32[2,24,2304]{2,1,0:T(8,128)S(1)} collective-permute-done((f32[2,24,2304]{2,1,0:T(8,128)S(1)}, f32[2,24,2304]{2,1,0:T(8,128)S(1)}, u32[]{:S(2)}, u32[]{:S(2)}) %collective-permute-start.18) | collective-permute-done | bytes 442400 | tf_op jit(solution)/shard_map/ppermute | solution.py:254
  235.2 0.4 collective-permute-start.19
  235.6 24.8 %collective-permute-done.10 = f32[48,9216]{1,0:T(8,128)S(1)} collective-permute-done((f32[48,9216]{1,0:T(8,128)S(1)}, f32[48,9216]{1,0:T(8,128)S(1)}, u32[]{:S(2)}, u32[]{:S(2)}) %collective-permute-start.10) | collective-permute-done | bytes 1769504 | tf_op jit(solution)/shard_map/ppermute | solution.py:278
  260.4 0.2 add_bitcast_fusion.1
  260.7 0.2 broadcast_select_fusion.6
  260.8 0.1 pad_maximum_fusion.4
  261.0 32.0 %collective-permute-done.12 = f32[48,9216]{1,0:T(8,128)S(1)} collective-permute-done((f32[48,9216]{1,0:T(8,128)S(1)}, f32[48,9216]{1,0:T(8,128)S(1)}, u32[]{:S(2)}, u32[]{:S(2)}) %collective-permute-start.12) | collective-permute-done | bytes 1769504 | tf_op jit(solution)/shard_map/ppermute | solution.py:278
  293.1 0.2 add_bitcast_fusion
  293.3 2.0 pad_maximum_fusion.1
  295.4 0.3 broadcast_select_fusion.2
  295.7 2.0 pad_maximum_fusion.2
  (42 shorter events, 1.3 us)
Async XLA Ops:
  3.0 4.1 %collective-permute-start.1 = (f32[2,24,9216]{2,1,0:T(8,128)}, f32[2,24,9216]{2,1,0:T(8,128)}, u32[]{:S(2)}, u32[]{:S(2)}) collective-permute-start(f32[2,24,9216]{2,1,0:T(8,128)} %slice_select_fusion.1), channel_id=1, source_target_pairs={{0,2},{2,0},{4,6},{6,4},{8,10},{10,8},{12,14},{14,12},{16,18},{18,... | collective-permute-start | bytes 5308424 | tf_op jit(solution)/shard_map/ppermute | solution.py:254
  8.8 1.2 copy-start.2
  10.1 15.4 %collective-permute-start.2 = (f32[2,24,4608]{2,1,0:T(8,128)S(1)}, f32[2,24,4608]{2,1,0:T(8,128)S(1)}, u32[]{:S(2)}, u32[]{:S(2)}) collective-permute-start(f32[2,24,4608]{2,1,0:T(8,128)S(1)} %slice_select_fusion.3), channel_id=1, source_target_pairs={{0,4},{2,10},{4,0},{6,14},{8,12},{10,2},{12,8},{14,6},{16,20},{18,... | collective-permute-start | bytes 2654216 | tf_op jit(solution)/shard_map/ppermute | solution.py:254
  27.2 12.4 %collective-permute-start.3 = (f32[2,24,2304]{2,1,0:T(8,128)S(1)}, f32[2,24,2304]{2,1,0:T(8,128)S(1)}, u32[]{:S(2)}, u32[]{:S(2)}) collective-permute-start(f32[2,24,2304]{2,1,0:T(8,128)S(1)} %slice_select_fusion.5), channel_id=1, source_target_pairs={{0,8},{2,26},{4,12},{6,30},{8,0},{10,18},{12,4},{14,22},{16,24},{1... | collective-permute-start | bytes 1327112 | tf_op jit(solution)/shard_map/ppermute | solution.py:254
  39.7 10.3 %collective-permute-start.4 = (f32[2,24,2304]{2,1,0:T(8,128)S(1)}, f32[2,24,2304]{2,1,0:T(8,128)S(1)}, u32[]{:S(2)}, u32[]{:S(2)}) collective-permute-start(f32[2,24,2304]{2,1,0:T(8,128)S(1)} %select_add_fusion.5), channel_id=1, source_target_pairs={{0,24},{2,6},{4,28},{6,2},{8,16},{10,14},{12,20},{14,10},{16,8},{1... | collective-permute-start | bytes 1327112 | tf_op jit(solution)/shard_map/ppermute | solution.py:254
  50.0 6.0 %collective-permute-start.5 = (f32[24,2304]{1,0:T(8,128)S(1)}, f32[24,2304]{1,0:T(8,128)S(1)}, u32[]{:S(2)}, u32[]{:S(2)}) collective-permute-start(f32[24,2304]{1,0:T(8,128)S(1)} %get-tuple-element.33), channel_id=1, source_target_pairs={{0,1},{1,0},{2,3},{3,2},{4,5},{5,4},{6,7},{7,6},{8,9},{9,8},{10,11... | collective-permute-start | bytes 663560 | tf_op jit(solution)/shard_map/ppermute | solution.py:278
  56.1 14.9 %copy-start.3 = (f32[2,48,9216]{2,1,0:T(8,128)S(1)}, f32[2,48,9216]{2,1,0:T(8,128)}, u32[]{:S(2)}) copy-start(f32[2,48,9216]{2,1,0:T(8,128)} %param.7) | copy-start | bytes 10616836
  56.1 12.6 %collective-permute-start.6 = (f32[2,24,2304]{2,1,0:T(8,128)S(1)}, f32[2,24,2304]{2,1,0:T(8,128)S(1)}, u32[]{:S(2)}, u32[]{:S(2)}) collective-permute-start(f32[2,24,2304]{2,1,0:T(8,128)S(1)} %pad_maximum_fusion.7), channel_id=1, source_target_pairs={{0,8},{2,26},{4,12},{6,30},{8,0},{10,18},{12,4},{14,22},{16,24},{1... | collective-permute-start | bytes 1327112 | tf_op jit(solution)/shard_map/ppermute | solution.py:254
  68.8 13.2 %collective-permute-start.7 = (f32[2,24,4608]{2,1,0:T(8,128)S(1)}, f32[2,24,4608]{2,1,0:T(8,128)S(1)}, u32[]{:S(2)}, u32[]{:S(2)}) collective-permute-start(f32[2,24,4608]{2,1,0:T(8,128)S(1)} %pad_maximum_fusion.5), channel_id=1, source_target_pairs={{0,4},{2,10},{4,0},{6,14},{8,12},{10,2},{12,8},{14,6},{16,20},{18,... | collective-permute-start | bytes 2654216 | tf_op jit(solution)/shard_map/ppermute | solution.py:254
  72.5 40.3 %copy-start.5 = (f32[48,9216]{1,0:T(8,128)}, f32[48,9216]{1,0:T(8,128)S(1)}, u32[]{:S(2)}) copy-start(f32[48,9216]{1,0:T(8,128)S(1)} %get-tuple-element.11.own) | copy-start | bytes 5308420
  72.5 40.3 %collective-permute-start = (f32[48,9216]{1,0:T(8,128)}, f32[48,9216]{1,0:T(8,128)}, u32[]{:S(2)}, u32[]{:S(2)}) collective-permute-start(f32[48,9216]{1,0:T(8,128)} %get-tuple-element.20.own), channel_id=1, source_target_pairs={{0,1},{1,0},{2,3},{3,2},{4,5},{5,4},{6,7},{7,6},{8,9},{9,8},{10,11... | collective-permute-start | bytes 5308424 | tf_op jit(solution)/shard_map/ppermute | solution.py:278
  83.5 30.8 %collective-permute-start.8 = (f32[2,24,9216]{2,1,0:T(8,128)}, f32[2,24,9216]{2,1,0:T(8,128)}, u32[]{:S(2)}, u32[]{:S(2)}) collective-permute-start(f32[2,24,9216]{2,1,0:T(8,128)} %pad_maximum_fusion.3), channel_id=1, source_target_pairs={{0,2},{2,0},{4,6},{6,4},{8,10},{10,8},{12,14},{14,12},{16,18},{18,... | collective-permute-start | bytes 5308424 | tf_op jit(solution)/shard_map/ppermute | solution.py:254
  89.0 17.8 %collective-permute-start.9 = (f32[8,128]{1,0:T(8,128)S(1)}, f32[8,128]{1,0:T(8,128)S(1)}, u32[]{:S(2)}, u32[]{:S(2)}) collective-permute-start(f32[8,128]{1,0:T(8,128)S(1)} %broadcast_in_dim.8), channel_id=1, source_target_pairs={{0,1},{1,0},{2,3},{3,2},{4,5},{5,4},{6,7},{7,6},{8,9},{9,8},{10,11... | collective-permute-start | bytes 12296 | tf_op jit(solution)/shard_map/ppermute | solution.py:278
  112.8 33.0 %collective-permute-start.11 = (f32[48,9216]{1,0:T(8,128)S(1)}, f32[48,9216]{1,0:T(8,128)S(1)}, u32[]{:S(2)}, u32[]{:S(2)}) collective-permute-start(f32[48,9216]{1,0:T(8,128)S(1)} %get-tuple-element.11.own), channel_id=1, source_target_pairs={{0,1},{1,0},{2,3},{3,2},{4,5},{5,4},{6,7},{7,6},{8,9},{9,8},{10,11... | collective-permute-start | bytes 5308424 | tf_op jit(solution)/shard_map/ppermute | solution.py:278
  116.1 2.1 copy-start
  116.1 2.1 copy-start.1
  145.8 1.2 copy-start.6
  170.7 6.1 %copy-start.4 = (f32[96,9216]{1,0:T(8,128)S(1)}, f32[96,9216]{1,0:T(8,128)}, u32[]{:S(2)}) copy-start(f32[96,9216]{1,0:T(8,128)} %get-tuple-element.15) | copy-start | bytes 10616836
  173.1 3.8 %collective-permute-start.13 = (f32[2,24,9216]{2,1,0:T(8,128)S(1)}, f32[2,24,9216]{2,1,0:T(8,128)S(1)}, u32[]{:S(2)}, u32[]{:S(2)}) collective-permute-start(f32[2,24,9216]{2,1,0:T(8,128)S(1)} %slice_select_fusion), channel_id=1, source_target_pairs={{0,2},{2,0},{4,6},{6,4},{8,10},{10,8},{12,14},{14,12},{16,18},{18,... | collective-permute-start | bytes 5308424 | tf_op jit(solution)/shard_map/ppermute | solution.py:254
  177.2 13.1 %collective-permute-start.14 = (f32[2,24,4608]{2,1,0:T(8,128)S(1)}, f32[2,24,4608]{2,1,0:T(8,128)S(1)}, u32[]{:S(2)}, u32[]{:S(2)}) collective-permute-start(f32[2,24,4608]{2,1,0:T(8,128)S(1)} %slice_select_fusion.2), channel_id=1, source_target_pairs={{0,4},{2,10},{4,0},{6,14},{8,12},{10,2},{12,8},{14,6},{16,20},{18,... | collective-permute-start | bytes 2654216 | tf_op jit(solution)/shard_map/ppermute | solution.py:254
  190.5 13.1 %collective-permute-start.15 = (f32[2,24,2304]{2,1,0:T(8,128)S(1)}, f32[2,24,2304]{2,1,0:T(8,128)S(1)}, u32[]{:S(2)}, u32[]{:S(2)}) collective-permute-start(f32[2,24,2304]{2,1,0:T(8,128)S(1)} %slice_select_fusion.4), channel_id=1, source_target_pairs={{0,8},{2,26},{4,12},{6,30},{8,0},{10,18},{12,4},{14,22},{16,24},{1... | collective-permute-start | bytes 1327112 | tf_op jit(solution)/shard_map/ppermute | solution.py:254
  203.7 10.3 %collective-permute-start.16 = (f32[2,24,2304]{2,1,0:T(8,128)S(1)}, f32[2,24,2304]{2,1,0:T(8,128)S(1)}, u32[]{:S(2)}, u32[]{:S(2)}) collective-permute-start(f32[2,24,2304]{2,1,0:T(8,128)S(1)} %select_add_fusion.4), channel_id=1, source_target_pairs={{0,24},{2,6},{4,28},{6,2},{8,16},{10,14},{12,20},{14,10},{16,8},{1... | collective-permute-start | bytes 1327112 | tf_op jit(solution)/shard_map/ppermute | solution.py:254
  214.1 8.4 %collective-permute-start.17 = (f32[24,2304]{1,0:T(8,128)S(1)}, f32[24,2304]{1,0:T(8,128)S(1)}, u32[]{:S(2)}, u32[]{:S(2)}) collective-permute-start(f32[24,2304]{1,0:T(8,128)S(1)} %slice_bitcast_fusion.3), channel_id=1, source_target_pairs={{0,1},{1,0},{2,3},{3,2},{4,5},{5,4},{6,7},{7,6},{8,9},{9,8},{10,11... | collective-permute-start | bytes 663560 | tf_op jit(solution)/shard_map/ppermute | solution.py:278
  215.6 44.8 %collective-permute-start.10 = (f32[48,9216]{1,0:T(8,128)S(1)}, f32[48,9216]{1,0:T(8,128)S(1)}, u32[]{:S(2)}, u32[]{:S(2)}) collective-permute-start(f32[48,9216]{1,0:T(8,128)S(1)} %get-tuple-element.10), channel_id=1, source_target_pairs={{0,1},{1,0},{2,3},{3,2},{4,5},{5,4},{6,7},{7,6},{8,9},{9,8},{10,11... | collective-permute-start | bytes 5308424 | tf_op jit(solution)/shard_map/ppermute | solution.py:278
  222.6 12.5 %collective-permute-start.18 = (f32[2,24,2304]{2,1,0:T(8,128)S(1)}, f32[2,24,2304]{2,1,0:T(8,128)S(1)}, u32[]{:S(2)}, u32[]{:S(2)}) collective-permute-start(f32[2,24,2304]{2,1,0:T(8,128)S(1)} %pad_maximum_fusion.8), channel_id=1, source_target_pairs={{0,8},{2,26},{4,12},{6,30},{8,0},{10,18},{12,4},{14,22},{16,24},{1... | collective-permute-start | bytes 1327112 | tf_op jit(solution)/shard_map/ppermute | solution.py:254
  225.0 68.1 %collective-permute-start.12 = (f32[48,9216]{1,0:T(8,128)S(1)}, f32[48,9216]{1,0:T(8,128)S(1)}, u32[]{:S(2)}, u32[]{:S(2)}) collective-permute-start(f32[48,9216]{1,0:T(8,128)S(1)} %get-tuple-element.14), channel_id=1, source_target_pairs={{0,1},{1,0},{2,3},{3,2},{4,5},{5,4},{6,7},{7,6},{8,9},{9,8},{10,11... | collective-permute-start | bytes 5308424 | tf_op jit(solution)/shard_map/ppermute | solution.py:278
  235.2 25.4 %collective-permute-start.19 = (f32[2,24,4608]{2,1,0:T(8,128)S(1)}, f32[2,24,4608]{2,1,0:T(8,128)S(1)}, u32[]{:S(2)}, u32[]{:S(2)}) collective-permute-start(f32[2,24,4608]{2,1,0:T(8,128)S(1)} %pad_maximum_fusion.6), channel_id=1, source_target_pairs={{0,4},{2,10},{4,0},{6,14},{8,12},{10,2},{12,8},{14,6},{16,20},{18,... | collective-permute-start | bytes 2654216 | tf_op jit(solution)/shard_map/ppermute | solution.py:254
  261.0 34.4 %collective-permute-start.20 = (f32[2,24,9216]{2,1,0:T(8,128)S(1)}, f32[2,24,9216]{2,1,0:T(8,128)S(1)}, u32[]{:S(2)}, u32[]{:S(2)}) collective-permute-start(f32[2,24,9216]{2,1,0:T(8,128)S(1)} %pad_maximum_fusion.4), channel_id=1, source_target_pairs={{0,2},{2,0},{4,6},{6,4},{8,10},{10,8},{12,14},{14,12},{16,18},{18,... | collective-permute-start | bytes 5308424 | tf_op jit(solution)/shard_map/ppermute | solution.py:254

commit v2 on v1

--- a/solution.py
+++ b/solution.py
@@ -140,42 +140,85 @@
     return result[:, :LANES] + result[:, LANES:]
 
 
-def pair_kernel(
-    count, per_unit, has_total, own, other, block, coulomb, into_x, out_of_x, along_y, along_z, *rest
-):
-    total = rest[0] if has_total else None
-    local_own, local_other, block_terms, cells = rest[-4:]
-    half = count // 2
-    unit = per_unit * count
-    units = count // per_unit
-    batch = next(k for k in (4, 3, 2, 1) if units % k == 0)
-    planes = next(k for k in (16, 8, 4, 2, 1) if count % k == 0)
+def divisor(total, limit):
+    return max(k for k in range(1, limit + 1) if total % k == 0)
+
+
+def pair_kernel(count, unit, batch, planes, band, has_total, sizes, core_ref, *refs):
+    into_x, out_of_x, along_y, along_z, *refs = refs
+    in_rows, out_rows = sizes
+    half, quarter = count // 2, count // 4
+    n_in = 6 + len(in_rows) + (4 if has_total else 0)
+    n_out = 5 + len(out_rows)
+    orbitals, coulomb_in, *others = refs[:n_in]
+    block_in, totals_in, others = others[:4], others[4 + len(in_rows) :], others[4 : 4 + len(in_rows)]
+    local_out, *backs = refs[n_in : n_in + n_out]
+    terms_out, backs = backs[:4], backs[4:]
+    first, second, coulomb, total, local, terms, cells, in_sems, out_sems, wide_sem = refs[n_in + n_out :]
     width = batch * unit
+    steps = count * count // width
+    mine, theirs = core_ref[0] * quarter, quarter - core_ref[0] * quarter
+
+    def spans(buffer, pieces):
+        result = []
+        for ref, start, rows in pieces:
+            start = start if isinstance(start, int) else pl.multiple_of(start, 8)
+            result.append((ref, buffer.at[pl.ds(start, rows)]))
+        return result
+
+    def by_core(buffer, parts):
+        starts = [k * half + start for k in range(2) for start in (mine, theirs)]
+        return spans(buffer, [(ref, start, quarter) for ref, start in zip(parts, starts)])
+
+    def by_size(buffer, own, rest, rows):
+        starts = [half + sum(rows[:k]) for k in range(len(rows))]
+        return spans(buffer, [(own, 0, half)] + list(zip(rest, starts, rows)))
+
+    loads = by_size(first, orbitals.at[band], others, in_rows) + by_core(second, block_in)
+    late = by_core(total, totals_in) if has_total else []
+    stores = by_size(local, local_out, backs, out_rows) + by_core(terms, terms_out)
+
+    def copies(pairs, sems, step, offset, outward):
+        columns = pl.ds(pl.multiple_of(step * width, LANES), width)
+        for k, (outside, inside) in enumerate(pairs):
+            ends = (outside.at[:, columns], inside.at[:, columns])
+            yield pltpu.make_async_copy(*(ends[::-1] if outward else ends), sems.at[offset + k, step])
+
+    wide = pltpu.make_async_copy(coulomb_in, coulomb, wide_sem)
+    for step in range(steps):
+        for copy in copies(loads, in_sems, step, 0, False):
+            copy.start()
+    wide.start()
+    for step in range(steps):
+        for copy in copies(late, in_sems, step, len(loads), False):
+            copy.start()
 
     def forward(step, carry):
+        for copy in copies(loads, in_sems, step, 0, False):
+            copy.wait()
         columns = pl.ds(pl.multiple_of(step * width, LANES), width)
-        density = jnp.concatenate([own[:, columns], other[:, columns]], 0) * block[:, columns]
-        density = transform_rows(into_x[...], density)
+        density = transform_rows(into_x[...], first[:, columns] * second[:, columns])
         parts = []
         for start in range(0, width, unit):
             piece = density[:, start : start + unit]
-            for index in range(per_unit):
-                shifted = pltpu.roll(piece, unit - index * count, 1) if index else piece
+            for offset in range(0, unit, count):
+                shifted = pltpu.roll(piece, unit - offset, 1) if offset else piece
                 parts.append(shifted[:, :LANES])
         rows = pl.ds(pl.multiple_of(step * width, 8), width)
         cells[rows, :] = transform_lanes(jnp.concatenate(parts, 0), along_z[...])
         return carry
 
-    lax.fori_loop(0, units // batch, forward, 0)
+    lax.fori_loop(0, steps, forward, 0)
+    wide.wait()
 
     def middle(step, carry):
-        first = step * planes
-        values = [cells[pl.ds(first + k, count, stride=count), :] for k in range(planes)]
+        start = step * planes
+        values = [cells[pl.ds(start + k, count, stride=count), :] for k in range(planes)]
         spectrum = transform_rows(along_y[...], jnp.concatenate(values, 1))
-        scale = jnp.concatenate([coulomb[first + k] for k in range(planes)], 1)
+        scale = jnp.concatenate([coulomb[start + k] for k in range(planes)], 1)
         scaled = transform_rows(along_y[...], spectrum * scale)
         for k in range(planes):
-            cells[pl.ds(first + k, count, stride=count), :] = scaled[:, k * LANES : (k + 1) * LANES]
+            cells[pl.ds(start + k, count, stride=count), :] = scaled[:, k * LANES : (k + 1) * LANES]
         return carry
 
     lax.fori_loop(0, count // planes, middle, 0)
@@ -200,35 +243,65 @@
                 add(tile, jnp.where(lane >= offset, piece, 0.0))
                 add(tile + 1, jnp.where(lane < offset, piece, 0.0))
         potential = transform_rows(out_of_x[...], jnp.concatenate(tiles, 1))
+        for copy in copies(late, in_sems, step, len(loads), False):
+            copy.wait()
         columns = pl.ds(pl.multiple_of(step * width, LANES), width)
-        local = block[:, columns] * potential
-        terms = jnp.concatenate([own[:, columns], other[:, columns]], 0) * potential
+        local[:, columns] = second[:, columns] * potential
+        result = first[:, columns] * potential
         if has_total:
-            terms = terms + total[:, columns]
-        local_own[:, columns] = local[:half]
-        local_other[:, columns] = local[half:]
-        block_terms[:, columns] = terms
+            result = result + total[:, columns]
+        terms[:, columns] = result
+        for copy in copies(stores, out_sems, step, 0, True):
+            copy.start()
         return carry
 
-    lax.fori_loop(0, units // batch, inverse, 0)
-
-
-def pair_terms(own, other, block, coulomb, tables, total=None):
-    half, flat_cells = own.shape
-    count = 2 * half
-    has_total = total is not None
-    operands = [own, other, block, coulomb, *tables] + ([total] if has_total else [])
+    lax.fori_loop(0, steps, inverse, 0)
+    for step in range(steps):
+        for copy in copies(stores, out_sems, step, 0, True):
+            copy.wait()
+
+
+def pair_terms(orbitals, band, others, block, coulomb, core, tables, back_rows, totals=()):
+    _, half, flat_cells = orbitals.shape
+    count, quarter = 2 * half, half // 2
+    unit = math.lcm(count, LANES)
+    batch = divisor(flat_cells // unit, 8)
+    planes = divisor(count, 16)
+    steps = flat_cells // (batch * unit)
+    in_rows, out_rows = tuple(v.shape[0] for v in others), tuple(back_rows)
+    operands = [orbitals, coulomb, *block, *others, *totals]
     vmem = pl.BlockSpec(memory_space=pltpu.VMEM)
-    shapes = [(half, flat_cells), (half, flat_cells), (count, flat_cells)]
+    anywhere = pl.BlockSpec(memory_space=pl.ANY)
+    shapes = [(half, flat_cells)] + [(quarter, flat_cells)] * 4
+    shapes += [(rows, flat_cells) for rows in out_rows]
+    whole = pltpu.VMEM((count, flat_cells), jnp.float32)
+    moved = 4 * sum(math.prod(s) for s in shapes + [v.shape for v in operands])
+    sizes = (in_rows, out_rows)
     return pl.pallas_call(
-        functools.partial(pair_kernel, count, math.lcm(count, LANES) // count, has_total),
-        in_specs=[vmem] * len(operands),
-        out_specs=[vmem] * 3,
+        functools.partial(pair_kernel, count, unit, batch, planes, band, bool(totals), sizes),
+        in_specs=[pl.BlockSpec(memory_space=pltpu.SMEM)]
+        + [vmem] * len(tables)
+        + [anywhere] * len(operands),
+        out_specs=[anywhere] * len(shapes),
         out_shape=[jax.ShapeDtypeStruct(shape, jnp.float32) for shape in shapes],
-        scratch_shapes=[pltpu.VMEM((flat_cells, LANES), jnp.float32)],
-        compiler_params=pltpu.CompilerParams(vmem_limit_bytes=50 * 2**20),
+        scratch_shapes=[
+            whole,
+            whole,
+            pltpu.VMEM(coulomb.shape, jnp.float32),
+            whole if totals else pltpu.VMEM((8, LANES), jnp.float32),
+            whole,
+            whole,
+            pltpu.VMEM((flat_cells, LANES), jnp.float32),
+            pltpu.SemaphoreType.DMA((9 + len(in_rows), steps)),
+            pltpu.SemaphoreType.DMA((5 + len(out_rows), steps)),
+            pltpu.SemaphoreType.DMA,
+        ],
+        compiler_params=pltpu.CompilerParams(vmem_limit_bytes=60 * 2**20),
+        cost_estimate=pl.CostEstimate(
+            flops=6 * flat_cells * count * 16 * LANES, bytes_accessed=moved, transcendentals=0
+        ),
         name="pair_terms",
-    )(*operands)
+    )(core, *tables, *operands)
 
 
 def halves(values, upper, dim):
@@ -244,41 +317,15 @@
     )
 
 
-def band_sum(values, exchange_x):
-    size = lax.axis_size("band")
-    index = lax.axis_index("band")
-    core, side, depth = index % 2, index // 2 % 2, index // 4
-    depth_low, depth_high = (depth + depth // 2) % 2 == 1, depth // 2 == 1
-
-    def swap(value, partner):
-        return lax.ppermute(value, "band", [(k, partner(k)) for k in range(size)])
-
-    def by_core(first, second):
-        return lambda k: k ^ (second if k % 2 else first)
-
-    side_or_low = by_core(2, 4)
-    low_or_high = by_core(4, 12)
-    high_or_side = by_core(12, 2)
-    first_bit = jnp.where(core == 1, depth_low, side == 1)
-    second_bit = jnp.where(core == 1, depth_high, depth_low)
-    keep, send = halves(values, core == 1, 1)
-    values = keep + swap(send, lambda k: k ^ 1)
-    keep, send = halves(values, first_bit, 2)
-    values = keep + swap(send, side_or_low)
-    keep, send = halves(values, second_bit, 2)
-    values = keep + swap(send, low_or_high)
-    values = values + swap(values, high_or_side)
-    values = exchange_x(values)
-    values = joined(values, swap(values, low_or_high), second_bit, 2)
-    values = joined(values, swap(values, side_or_low), first_bit, 2)
-    return joined(values, swap(values, lambda k: k ^ 1), core == 1, 1)
-
-
 def across(value):
     return lax.ppermute(value, "fft", [(0, 1), (1, 0)])
 
 
-def coulomb_table(cutoff_mask, count):
+def tied(*values):
+    return lax.optimization_barrier(values)
+
+
+def largest_length(cutoff_mask, count):
     columns = cutoff_mask.shape[1] // count
     positions = jnp.arange(count, dtype=jnp.int32)
     signed = jnp.where(positions <= count // 2, positions, positions - count)
@@ -286,8 +333,13 @@
     mine = lax.dynamic_slice_in_dim(squares, lax.axis_index("fft") * columns, columns)
     flat = (mine[:, None] + squares[None, :]).reshape(-1)
     lengths = jnp.where(cutoff_mask != 0, squares[:, None] + flat[None, :], 0)
-    limit = jnp.full((8, LANES), jnp.max(lengths).astype(jnp.float32))
-    limit = jnp.maximum(limit, across(limit))[0, 0].astype(jnp.int32)
+    return jnp.full((8, LANES), jnp.max(lengths).astype(jnp.float32))
+
+
+def coulomb_table(limit, count):
+    positions = jnp.arange(count, dtype=jnp.int32)
+    signed = jnp.where(positions <= count // 2, positions, positions - count)
+    squares = signed * signed
     padded = jnp.concatenate([squares, jnp.full((LANES - count,), 4 * count * count, jnp.int32)])
     squared = squares[:, None, None] + squares[None, :, None] + padded[None, None, :]
     weights = ((squared >= 1) & (squared <= limit)).astype(jnp.float32)
@@ -295,37 +347,144 @@
     return factor * weights / jnp.maximum(squared, 1).astype(jnp.float32)
 
 
+class Beside:
+    def __init__(self, sends, needed=()):
+        self.sends = sends
+        self.needed = dict(needed)
+        self.results = {}
+        self.arrived = {}
+
+    def open(self, step, *values):
+        self.arrived[step] = None
+        if step in self.sends:
+            *values, send = tied(*values, self.sends[step])
+            self.arrived[step] = across(send)
+        return values
+
+    def close(self, step, value):
+        if step in self.sends:
+            value, self.arrived[step] = tied(value, self.arrived[step])
+        if step in self.needed:
+            value, self.results[step] = tied(value, self.needed[step](self.results))
+        return value
+
+    def pieces(self, *steps):
+        return [self.arrived[step] for step in steps]
+
+
+def band_sum(parts, exchange, beside, flip):
+    size, planes = lax.axis_size("band"), lax.axis_size("fft")
+    index, plane = lax.axis_index("band"), lax.axis_index("fft")
+    core, side, depth = index % 2, index // 2 % 2, index // 4
+    depth_low, depth_high = (depth + depth // 2) % 2 == 1, depth // 2 == 1
+
+    def swap(step, value, partner, kept=None):
+        kept, value = beside.open(step, value if kept is None else kept, value)
+        ends = [(k, f, partner(k, f)) for k in range(size) for f in range(planes)]
+        pairs = [(k * planes + f, end * planes + f) for k, f, end in ends]
+        arrived = lax.ppermute(value, ("band", "fft"), pairs)
+        return kept, beside.close(step, arrived)
+
+    def added(step, value, partner, kept=None):
+        kept, arrived = swap(step, value, partner, kept)
+        return kept + arrived
+
+    def across_cores(k, f):
+        return k ^ 1
+
+    def axes(which, flipped):
+        def by_core(first, second):
+            return lambda k, f: k ^ (second if (k + which + flipped * f) % 2 else first)
+
+        turned = (core + which + flipped * plane) % 2 == 1
+        bits = jnp.where(turned, depth_low, side == 1), jnp.where(turned, depth_high, depth_low)
+        return bits, (by_core(2, 4), by_core(4, 12), by_core(12, 2))
+
+    def down(which):
+        bits, partners = axes(which, flip)
+        keep, send = parts[which]
+        value = added((which, "core"), send, across_cores, keep)
+        keep, send = halves(value, bits[0], 1)
+        value = added((which, "first"), send, partners[0], keep)
+        keep, send = halves(value, bits[1], 1)
+        value = added((which, "second"), send, partners[1], keep)
+        return added((which, "third"), value, partners[2])
+
+    def up(which, value):
+        bits, partners = axes(which, 0)
+        value = joined(*swap((which, "up_second"), value, partners[1]), bits[1], 1)
+        value = joined(*swap((which, "up_first"), value, partners[0]), bits[0], 1)
+        return swap((which, "core_back"), value, across_cores)
+
+    pieces = exchange(down(0), down(1))
+    return [up(which, piece) for which, piece in enumerate(pieces)]
+
+
 def per_device_pairs(orbitals, owners, cutoff_mask):
     _, half, flat_cells = orbitals.shape
     count = 2 * half
     plane = lax.axis_index("fft")
+    core = lax.axis_index("band") % 2
+    core_scalar = jnp.full((1,), core, jnp.int32)
     casine = casine_matrix(count)
-    turned = [(np.arange(count) + half * k) % count for k in range(2)]
-    into_x = jnp.asarray(np.stack([left_table(casine[:, order]) for order in turned]))[plane]
-    out_of_x = jnp.asarray(np.stack([left_table(casine[order, :]) for order in turned]))[plane]
-    tables = [into_x, out_of_x, jnp.asarray(left_table(casine)), jnp.asarray(right_table(casine))]
-
-    def gather_band(pieces):
-        mine = jnp.where(plane == 1, pieces[1], pieces[0])
-        theirs = jnp.where(plane == 1, pieces[0], pieces[1])
-        return jnp.stack([mine, across(theirs)])
-
-    def gather_half(pieces):
-        other = across(pieces[1])
-        return jnp.stack(
-            [jnp.where(plane == 1, other, pieces[0]), jnp.where(plane == 1, pieces[0], other)]
-        )
-
-    first_other = across(orbitals[0])
-    coulomb = coulomb_table(cutoff_mask, count)
+    orders = [np.roll(np.arange(count), -half * k) for k in range(2)]
+    into_x = jnp.asarray(np.stack([left_table(casine[:, order]) for order in orders]))[plane]
+    out_of_x = jnp.asarray(np.stack([left_table(casine[order, :]) for order in orders]))[plane]
+    along_y, along_z = jnp.asarray(left_table(casine)), jnp.asarray(right_table(casine))
+    length = largest_length(cutoff_mask, count)
+
+    def gather_band(first, second):
+        mine, theirs = jnp.where(plane == 1, second, first), jnp.where(plane == 1, first, second)
+        return mine, across(theirs)
+
+    def gather_half(own, other):
+        return own, across(other)
+
+    sixth = half // 6
+    cut = lambda band, start, rows: orbitals[band, sixth * start : sixth * (start + rows)]
+    steps = [(0, "core")]
+    steps += [(k, name) for name in ("first", "second", "third", "up_second") for k in range(2)]
+    places = [(0, k) for k in range(6)] + [(1, k) for k in range(3)]
+    beside = Beside(
+        {step: cut(*place, 1) for step, place in zip(steps, places)},
+        {
+            (0, "first"): lambda got: (length, into_x, out_of_x),
+            (0, "third"): lambda got: jnp.maximum(
+                got[0, "first"][0], across(got[0, "first"][0])
+            ),
+            (1, "up_second"): lambda got: coulomb_table(
+                got[0, "third"][0, 0].astype(jnp.int32), count
+            ),
+        },
+    )
     owned = jnp.where(lax.axis_index("band") == owners[0], orbitals, 0.0)
-    block = band_sum(owned, gather_band).reshape(count, flat_cells)
-    second, _ = lax.optimization_barrier((orbitals[1], first_other))
-    second_other = across(second)
-    own0, other0, terms = pair_terms(orbitals[0], first_other, block, coulomb, tables)
-    own1, other1, terms = pair_terms(orbitals[1], second_other, block, coulomb, tables, terms)
-    local_total = jnp.stack([own0 + across(other0), own1 + across(other1)])
-    block_total = band_sum(terms.reshape(2, half, flat_cells), gather_half)
+    block = band_sum([halves(v, core == 1, 0) for v in owned], gather_band, beside, 1)
+    tables = (*beside.results[0, "first"][1:], along_y, along_z)
+    coulomb = beside.results[1, "up_second"]
+    block = [*block[0], *block[1]]
+    arrived = beside.pieces(*steps)
+    block[0], last = tied(block[0], cut(1, 3, 3))
+    last = across(last)
+    own0, *rest = pair_terms(
+        orbitals, 0, arrived[:6], block, coulomb, core_scalar, tables, [3 * sixth] + [sixth] * 3
+    )
+    terms, backs0 = rest[:4], rest[4:]
+    back0 = across(backs0[0])
+    own1, *rest = pair_terms(
+        orbitals, 1, arrived[6:] + [last], block, coulomb, core_scalar, tables, [sixth] * 6, terms
+    )
+    terms, backs1 = rest[:4], rest[4:]
+    *terms, back0 = tied(*terms, back0)
+    beside = Beside(dict(zip(steps, backs0[1:] + backs1)))
+    sums = band_sum([terms[:2], terms[2:]], gather_half, beside, 0)
+    own_band, other_band = [joined(*parts, core == 1, 0) for parts in sums]
+    block_total = jnp.stack(
+        [jnp.where(plane == 1, other_band, own_band), jnp.where(plane == 1, own_band, other_band)]
+    )
+    arrived = beside.pieces(*steps)
+    back0 = jnp.concatenate([back0] + arrived[:3], 0)
+    back1 = jnp.concatenate(arrived[3:], 0)
+    local_total = jnp.stack([own0 + back0, own1 + back1])
     return local_total, block_total
 
 

time: 298 us -> 223 us (0.75)
  waiting for transfers between devices: 186 us -> 90.6 us
  starting transfers between devices: 28.3 us -> 58.5 us
  Pallas kernels: 46.2 us -> 38.8 us
  other arithmetic: 27.4 us -> 21 us
  local copies, waits for them, and re-layouts: 6.9 us -> 10.6 us
    ppermute x14 -> x28, waiting for transfers between devices: 98.1 us -> 38.1 us  [swap(): arrived = lax.ppermute(value, ('band', 'fft'), pairs)]
    ppermute x7 -> x23, waiting for transfers between devices: 87.9 us -> 52.5 us  [across(): return lax.ppermute(value, 'fft', [(0, 1), (1, 0)])]
    ppermute x7 -> x23, starting transfers between devices: 9.68 us -> 25.6 us  [across(): return lax.ppermute(value, 'fft', [(0, 1), (1, 0)])]
    ppermute x14 -> x28, starting transfers between devices: 18.6 us -> 33 us  [swap(): arrived = lax.ppermute(value, ('band', 'fft'), pairs)]
    pallas_call x2, Pallas kernels: 46.2 us -> 38.8 us  [pair_terms(): pl.pallas_call(functools.partial(pair_kernel, count, unit, batch, planes,...]
    concatenate x6 -> x10, other arithmetic: 5.64 us -> 0.6 us  [joined(): jnp.concatenate([jnp.where(upper, theirs, mine), jnp.where(upper, mine, t...]
    squeeze x3, local copies, waits for them, and re-layouts: 2.47 us -> 6.2 us  [the longest x2 4.56 us: per_device_pairs(): orbitals[band, sixth * start:sixth * (start + rows)]]
  transfers between devices with their start and end apart: 21 -> 51, of which waited for: 17 -> 29; matrix products, arithmetic and copies ran while one was open for 7% -> 10% of each run, Pallas kernels for 8% -> 17%
where the time goes in v2:
time: 223 us
  waiting for transfers between devices  90.6 us (41%)
  starting transfers between devices  58.5 us (26%)
  Pallas kernels  38.8 us (17%)
  other arithmetic  21 us (9%)
  local copies, waits for them, and re-layouts  10.6 us (5%)
  between operations  3.3 us (1%)
    ppermute x23, waiting for transfers between devices, across(): return lax.ppermute(value, 'fft', [(0, 1), (1, 0)])  52.5 us
    pallas_call x2, Pallas kernels, pair_terms(): pl.pallas_call(functools.partial(pair_kernel, count, unit, batch, planes,...  38.8 us
    ppermute x28, waiting for transfers between devices, swap(): arrived = lax.ppermute(value, ('band', 'fft'), pairs)  38.1 us
    ppermute x28, starting transfers between devices, swap(): arrived = lax.ppermute(value, ('band', 'fft'), pairs)  33 us
    ppermute x23, starting transfers between devices, across(): return lax.ppermute(value, 'fft', [(0, 1), (1, 0)])  25.6 us
    div x1, other arithmetic, coulomb_table(): return factor * weights / jnp.maximum(squared, 1).astype(jnp.float32)  4.69 us
    add x14, other arithmetic, added(): return kept + arrived  4.59 us
    squeeze x2, local copies, waits for them, and re-layouts, per_device_pairs(): orbitals[band, sixth * start:sixth * (start + rows)]  4.56 us
  transfers between devices with their start and end apart: 51, of which 29 were waited for; matrix products, arithmetic and copies ran while one was open for 10% of the time, Pallas kernels for 17%

profile of v2, /device:TPU:0, one launch (start us, length us, event | category | flops | bytes accessed | tf_op | source)
XLA Modules:
  0.0 222.9 jit_solution(1200126358786859697)
XLA Ops:
  1.3 3.3 %slice_bitcast_fusion.1 = (f32[8,9216]{1,0:T(8,128)}, f32[8,9216]{1,0:T(8,128)}, f32[8,9216]{1,0:T(8,128)}, f32[8,9216]{1,0:T(8,128)}, f32[8,9216]{1,0:T(8,128)}...) fusion(f32[2,48,9216]{2,1,0:T(8,128)} %refs_4_.3), kind=kLoop, calls=%fused_computation.42 | loop fusion | bytes 5308416 | tf_op jit(solution)/shard_map/squeeze | solution.py:444
  5.0 1.6 select_bitcast_fusion.4
  7.0 2.5 %collective-permute-start.1 = (f32[8,9216]{1,0:T(8,128)}, f32[8,9216]{1,0:T(8,128)}, u32[]{:S(2)}, u32[]{:S(2)}) collective-permute-start(f32[8,9216]{1,0:T(8,128)} %get-tuple-element.129), channel_id=1, source_target_pairs={{0,1},{1,0},{2,3},{3,2},{4,5},{5,4},{6,7},{7,6},{8,9},{9,8},{10,11... | collective-permute-start | bytes 884744 | tf_op jit(solution)/shard_map/ppermute | solution.py:321
  10.5 1.4 add.205
  11.9 2.6 %select_reduce_fusion = s32[]{:T(128)} fusion(s32[96,4608]{1,0:T(8,128)} %param.9, s32[4608]{0:T(1024)} %add.205, s32[96]{0:T(128)S(1)} %fusion.6), kind=kLoop, calls=%fused_computation.13 | loop fusion | flops 1769471 | bytes 1788292 | tf_op jit(solution)/shard_map/reduce_max | solution.py:336
  15.2 1.6 dynamic-slice_bitcast_fusion
  17.5 1.5 add.199
  19.1 1.8 collective-permute-start.3
  20.9 1.5 collective-permute-start.2
  22.5 1.3 bitcast_add_fusion
  25.3 1.0 collective-permute-start.10
  26.3 2.8 %collective-permute-done.3.refs_11_ = f32[8,9216]{1,0:T(8,128)S(1)} collective-permute-done((f32[8,9216]{1,0:T(8,128)S(1)}, f32[8,9216]{1,0:T(8,128)S(1)}, u32[]{:S(2)}, u32[]{:S(2)}) %collective-permute-start.3) | collective-permute-done | bytes 294944 | tf_op jit(solution)/shard_map/ppermute | solution.py:321
  29.1 2.6 %collective-permute-done.2 = f32[24,4608]{1,0:T(8,128)S(1)} collective-permute-done((f32[24,4608]{1,0:T(8,128)S(1)}, f32[24,4608]{1,0:T(8,128)S(1)}, u32[]{:S(2)}, u32[]{:S(2)}) %collective-permute-start.2) | collective-permute-done | bytes 442400 | tf_op jit(solution)/shard_map/ppermute | solution.py:385
  31.9 3.5 %collective-permute-done.11.refs_12_ = f32[8,9216]{1,0:T(8,128)S(1)} collective-permute-done((f32[8,9216]{1,0:T(8,128)S(1)}, f32[8,9216]{1,0:T(8,128)S(1)}, u32[]{:S(2)}, u32[]{:S(2)}) %collective-permute-start.11) | collective-permute-done | bytes 294944 | tf_op jit(solution)/shard_map/ppermute | solution.py:321
  35.5 1.8 collective-permute-start.13
  37.4 1.6 collective-permute-start.4
  39.0 2.5 %collective-permute-start.12 = (f32[24,2304]{1,0:T(8,128)S(1)}, f32[24,2304]{1,0:T(8,128)S(1)}, u32[]{:S(2)}, u32[]{:S(2)}) collective-permute-start(f32[24,2304]{1,0:T(8,128)S(1)} %get-tuple-element.153), channel_id=1, source_target_pairs={{0,24},{1,9},{2,10},{3,27},{4,28},{5,13},{6,14},{7,31},{8,16},{9,1... | collective-permute-start | bytes 663560 | tf_op jit(solution)/shard_map/ppermute | solution.py:385
  41.4 4.9 %collective-permute-done.4 = f32[24,2304]{1,0:T(8,128)S(1)} collective-permute-done((f32[24,2304]{1,0:T(8,128)S(1)}, f32[24,2304]{1,0:T(8,128)S(1)}, u32[]{:S(2)}, u32[]{:S(2)}) %collective-permute-start.4) | collective-permute-done | bytes 221216 | tf_op jit(solution)/shard_map/ppermute | solution.py:385
  46.4 1.7 collective-permute-start.7
  48.7 1.6 collective-permute-start.15
  50.8 3.5 %collective-permute-start.6 = (f32[24,2304]{1,0:T(8,128)S(1)}, f32[24,2304]{1,0:T(8,128)S(1)}, u32[]{:S(2)}, u32[]{:S(2)}) collective-permute-start(f32[24,2304]{1,0:T(8,128)S(1)} %add.210), channel_id=1, source_target_pairs={{0,24},{1,5},{2,6},{3,27},{4,28},{5,1},{6,2},{7,31},{8,16},{9,13},... | collective-permute-start | bytes 663560 | tf_op jit(solution)/shard_map/ppermute | solution.py:385
  54.3 1.5 collective-permute-start.14
  56.0 3.8 %collective-permute-done.8 = f32[8,128]{1,0:T(8,128)S(1)} collective-permute-done((f32[8,128]{1,0:T(8,128)S(1)}, f32[8,128]{1,0:T(8,128)S(1)}, u32[]{:S(2)}, u32[]{:S(2)}) %collective-permute-start.8) | collective-permute-done | bytes 4128 | tf_op jit(solution)/shard_map/ppermute | solution.py:321
  61.1 4.1 %collective-permute-start.19 = (f32[24,2304]{1,0:T(8,128)S(1)}, f32[24,2304]{1,0:T(8,128)S(1)}, u32[]{:S(2)}, u32[]{:S(2)}) collective-permute-start(f32[24,2304]{1,0:T(8,128)S(1)} %get-tuple-element.168), channel_id=1, source_target_pairs={{0,8},{1,9},{2,26},{3,27},{4,12},{5,13},{6,30},{7,31},{8,0},{9,1},... | collective-permute-start | bytes 663560 | tf_op jit(solution)/shard_map/ppermute | solution.py:385
  65.2 2.0 collective-permute-start.20
  67.2 4.7 %fusion.1.refs_5_ = f32[96,96,128]{2,1,0:T(8,128)} fusion(s32[]{:T(128)} %bitcast.16, s32[128]{0:T(128)S(1)} %concatenate.75, s32[96,96]{1,0:T(8,128)S(1)} %broadcast_add_fusion), kind=kLoop, calls=%fused_computation.4 | loop fusion | flops 9437184 | bytes 4755972 | tf_op jit(solution)/shard_map/div | solution.py:347
  71.9 1.6 collective-permute-done.16
  73.5 1.1 collective-permute-start.17
  75.5 4.3 %collective-permute-done.20.refs_11_ = f32[8,9216]{1,0:T(8,128)S(1)} collective-permute-done((f32[8,9216]{1,0:T(8,128)S(1)}, f32[8,9216]{1,0:T(8,128)S(1)}, u32[]{:S(2)}, u32[]{:S(2)}) %collective-permute-start.20) | collective-permute-done | bytes 294944 | tf_op jit(solution)/shard_map/ppermute | solution.py:321
  80.5 2.7 %collective-permute-done.17 = f32[24,2304]{1,0:T(8,128)S(1)} collective-permute-done((f32[24,2304]{1,0:T(8,128)S(1)}, f32[24,2304]{1,0:T(8,128)S(1)}, u32[]{:S(2)}, u32[]{:S(2)}) %collective-permute-start.17) | collective-permute-done | bytes 221216 | tf_op jit(solution)/shard_map/ppermute | solution.py:385
  84.2 6.9 %collective-permute-done.21 = f32[24,4608]{1,0:T(8,128)S(1)} collective-permute-done((f32[24,4608]{1,0:T(8,128)S(1)}, f32[24,4608]{1,0:T(8,128)S(1)}, u32[]{:S(2)}, u32[]{:S(2)}) %collective-permute-start.21) | collective-permute-done | bytes 442400 | tf_op jit(solution)/shard_map/ppermute | solution.py:385
  93.1 1.2 slice_bitcast_fusion
  94.3 1.5 collective-permute-start.25
  97.0 18.6 %pair_terms.2 = (f32[48,9216]{1,0:T(8,128)}, f32[24,9216]{1,0:T(8,128)}, f32[24,9216]{1,0:T(8,128)}, f32[24,9216]{1,0:T(8,128)}, f32[24,9216]{1,0:T(8,128)}, /*i...) custom-call(s32[1]{0:T(128)} %bitcast.core_ref, ...), custom_call_target="tpu_custom_call" | custom-call | flops 10871635968 | bytes 20643840 | tf_op jit(solution)/shard_map/pair_terms/pallas_call | solution.py:280
  116.3 20.2 %pair_terms.3 = (f32[48,9216]{1,0:T(8,128)}, f32[24,9216]{1,0:T(8,128)}, f32[24,9216]{1,0:T(8,128)}, f32[24,9216]{1,0:T(8,128)}, f32[24,9216]{1,0:T(8,128)}, /*i...) custom-call(s32[1]{0:T(128)} %bitcast.core_ref, ...), custom_call_target="tpu_custom_call" | custom-call | flops 10871635968 | bytes 24182784 | tf_op jit(solution)/shard_map/pair_terms/pallas_call | solution.py:280
  138.4 8.4 %collective-permute-done.28 = f32[8,9216]{1,0:T(8,128)S(1)} collective-permute-done((f32[8,9216]{1,0:T(8,128)S(1)}, f32[8,9216]{1,0:T(8,128)S(1)}, u32[]{:S(2)}, u32[]{:S(2)}) %collective-permute-start.28) | collective-permute-done | bytes 294944 | tf_op jit(solution)/shard_map/ppermute | solution.py:321
  146.9 1.3 add.227
  149.0 1.1 collective-permute-start.29
  150.3 1.3 collective-permute-start.33
  152.0 6.2 %collective-permute-done.30 = f32[8,9216]{1,0:T(8,128)S(1)} collective-permute-done((f32[8,9216]{1,0:T(8,128)S(1)}, f32[8,9216]{1,0:T(8,128)S(1)}, u32[]{:S(2)}, u32[]{:S(2)}) %collective-permute-start.30) | collective-permute-done | bytes 294944 | tf_op jit(solution)/shard_map/ppermute | solution.py:321
  158.2 3.6 %collective-permute-done.29 = f32[24,4608]{1,0:T(8,128)S(1)} collective-permute-done((f32[24,4608]{1,0:T(8,128)S(1)}, f32[24,4608]{1,0:T(8,128)S(1)}, u32[]{:S(2)}, u32[]{:S(2)}) %collective-permute-start.29) | collective-permute-done | bytes 442400 | tf_op jit(solution)/shard_map/ppermute | solution.py:385
  162.0 0.9 collective-permute-start.35
  162.9 1.6 collective-permute-done.33
  164.6 1.8 collective-permute-start.36
  166.4 1.1 collective-permute-start.37
  167.9 1.6 collective-permute-done.34
  169.4 2.6 %collective-permute-done.35 = f32[8,9216]{1,0:T(8,128)S(1)} collective-permute-done((f32[8,9216]{1,0:T(8,128)S(1)}, f32[8,9216]{1,0:T(8,128)S(1)}, u32[]{:S(2)}, u32[]{:S(2)}) %collective-permute-start.35) | collective-permute-done | bytes 294944 | tf_op jit(solution)/shard_map/ppermute | solution.py:321
  172.0 3.4 %collective-permute-start.38 = (f32[24,2304]{1,0:T(8,128)S(1)}, f32[24,2304]{1,0:T(8,128)S(1)}, u32[]{:S(2)}, u32[]{:S(2)}) collective-permute-start(f32[24,2304]{1,0:T(8,128)S(1)} %add.232), channel_id=1, source_target_pairs={{0,24},{1,25},{2,6},{3,7},{4,28},{5,29},{6,2},{7,3},{8,16},{9,17},... | collective-permute-start | bytes 663560 | tf_op jit(solution)/shard_map/ppermute | solution.py:385
  176.3 2.0 collective-permute-done.37
  178.4 1.2 collective-permute-start.40
  179.5 1.3 collective-permute-start.41
  180.8 1.0 collective-permute-done.38
  181.9 3.5 %collective-permute-done.39 = f32[8,9216]{1,0:T(8,128)S(1)} collective-permute-done((f32[8,9216]{1,0:T(8,128)S(1)}, f32[8,9216]{1,0:T(8,128)S(1)}, u32[]{:S(2)}, u32[]{:S(2)}) %collective-permute-start.39) | collective-permute-done | bytes 294944 | tf_op jit(solution)/shard_map/ppermute | solution.py:321
  185.4 4.1 %collective-permute-start.42 = (f32[24,2304]{1,0:T(8,128)S(1)}, f32[24,2304]{1,0:T(8,128)S(1)}, u32[]{:S(2)}, u32[]{:S(2)}) collective-permute-start(f32[24,2304]{1,0:T(8,128)S(1)} %add.234), channel_id=1, source_target_pairs={{0,8},{1,9},{2,26},{3,27},{4,12},{5,13},{6,30},{7,31},{8,0},{9,1},... | collective-permute-start | bytes 663560 | tf_op jit(solution)/shard_map/ppermute | solution.py:385
  190.5 1.2 collective-permute-done.41
  191.7 0.9 collective-permute-start.44
  192.7 8.7 %collective-permute-done.44 = f32[24,2304]{1,0:T(8,128)S(1)} collective-permute-done((f32[24,2304]{1,0:T(8,128)S(1)}, f32[24,2304]{1,0:T(8,128)S(1)}, u32[]{:S(2)}, u32[]{:S(2)}) %collective-permute-start.44) | collective-permute-done | bytes 221216 | tf_op jit(solution)/shard_map/ppermute | solution.py:321
  202.5 1.5 collective-permute-start.49
  204.0 5.3 %collective-permute-done.45 = f32[24,2304]{1,0:T(8,128)S(1)} collective-permute-done((f32[24,2304]{1,0:T(8,128)S(1)}, f32[24,2304]{1,0:T(8,128)S(1)}, u32[]{:S(2)}, u32[]{:S(2)}) %collective-permute-start.45) | collective-permute-done | bytes 221216 | tf_op jit(solution)/shard_map/ppermute | solution.py:385
  209.8 2.0 pad_maximum_fusion
  211.8 2.9 %collective-permute-done.49 = f32[24,4608]{1,0:T(8,128)S(1)} collective-permute-done((f32[24,4608]{1,0:T(8,128)S(1)}, f32[24,4608]{1,0:T(8,128)S(1)}, u32[]{:S(2)}, u32[]{:S(2)}) %collective-permute-start.49) | collective-permute-done | bytes 442400 | tf_op jit(solution)/shard_map/ppermute | solution.py:385
  214.9 2.8 %collective-permute-done.47 = f32[24,4608]{1,0:T(8,128)S(1)} collective-permute-done((f32[24,4608]{1,0:T(8,128)S(1)}, f32[24,4608]{1,0:T(8,128)S(1)}, u32[]{:S(2)}, u32[]{:S(2)}) %collective-permute-start.47) | collective-permute-done | bytes 442400 | tf_op jit(solution)/shard_map/ppermute | solution.py:385
  218.1 2.3 %collective-permute-done.48 = f32[24,9216]{1,0:T(8,128)S(1)} collective-permute-done((f32[24,9216]{1,0:T(8,128)S(1)}, f32[24,9216]{1,0:T(8,128)S(1)}, u32[]{:S(2)}, u32[]{:S(2)}) %collective-permute-start.48) | collective-permute-done | bytes 884768 | tf_op jit(solution)/shard_map/ppermute | solution.py:385
  220.8 2.0 pad_maximum_fusion.1
  (170 shorter events, 20.6 us)
Async XLA Ops:
  6.6 10.9 %collective-permute-start = (f32[24,9216]{1,0:T(8,128)}, f32[24,9216]{1,0:T(8,128)}, u32[]{:S(2)}, u32[]{:S(2)}) collective-permute-start(f32[24,9216]{1,0:T(8,128)} %get-tuple-element.128), channel_id=1, source_target_pairs={{0,2},{1,3},{2,0},{3,1},{4,6},{5,7},{6,4},{7,5},{8,10},{9,11},{10,... | collective-permute-start | bytes 2654216 | tf_op jit(solution)/shard_map/ppermute | solution.py:385
  7.0 10.5 %collective-permute-start.1 = (f32[8,9216]{1,0:T(8,128)}, f32[8,9216]{1,0:T(8,128)}, u32[]{:S(2)}, u32[]{:S(2)}) collective-permute-start(f32[8,9216]{1,0:T(8,128)} %get-tuple-element.129), channel_id=1, source_target_pairs={{0,1},{1,0},{2,3},{3,2},{4,5},{5,4},{6,7},{7,6},{8,9},{9,8},{10,11... | collective-permute-start | bytes 884744 | tf_op jit(solution)/shard_map/ppermute | solution.py:321
  9.5 12.9 %collective-permute-start.9 = (f32[24,9216]{1,0:T(8,128)}, f32[24,9216]{1,0:T(8,128)}, u32[]{:S(2)}, u32[]{:S(2)}) collective-permute-start(f32[24,9216]{1,0:T(8,128)} %get-tuple-element.263), channel_id=1, source_target_pairs={{0,2},{1,3},{2,0},{3,1},{4,6},{5,7},{6,4},{7,5},{8,10},{9,11},{10,... | collective-permute-start | bytes 2654216 | tf_op jit(solution)/shard_map/ppermute | solution.py:385
  19.1 9.9 %collective-permute-start.3 = (f32[8,9216]{1,0:T(8,128)S(1)}, f32[8,9216]{1,0:T(8,128)S(1)}, u32[]{:S(2)}, u32[]{:S(2)}) collective-permute-start(f32[8,9216]{1,0:T(8,128)S(1)} %copy-done.13), channel_id=1, source_target_pairs={{0,1},{1,0},{2,3},{3,2},{4,5},{5,4},{6,7},{7,6},{8,9},{9,8},{10,11... | collective-permute-start | bytes 884744 | tf_op jit(solution)/shard_map/ppermute | solution.py:321
  20.9 10.8 %collective-permute-start.2 = (f32[24,4608]{1,0:T(8,128)S(1)}, f32[24,4608]{1,0:T(8,128)S(1)}, u32[]{:S(2)}, u32[]{:S(2)}) collective-permute-start(f32[24,4608]{1,0:T(8,128)S(1)} %get-tuple-element.131), channel_id=1, source_target_pairs={{0,4},{1,9},{2,10},{3,7},{4,0},{5,13},{6,14},{7,3},{8,12},{9,1},{1... | collective-permute-start | bytes 1327112 | tf_op jit(solution)/shard_map/ppermute | solution.py:385
  24.7 10.7 %collective-permute-start.11 = (f32[8,9216]{1,0:T(8,128)S(1)}, f32[8,9216]{1,0:T(8,128)S(1)}, u32[]{:S(2)}, u32[]{:S(2)}) collective-permute-start(f32[8,9216]{1,0:T(8,128)S(1)} %copy-done.12), channel_id=1, source_target_pairs={{0,1},{1,0},{2,3},{3,2},{4,5},{5,4},{6,7},{7,6},{8,9},{9,8},{10,11... | collective-permute-start | bytes 884744 | tf_op jit(solution)/shard_map/ppermute | solution.py:321
  25.3 10.1 %collective-permute-start.10 = (f32[24,4608]{1,0:T(8,128)S(1)}, f32[24,4608]{1,0:T(8,128)S(1)}, u32[]{:S(2)}, u32[]{:S(2)}) collective-permute-start(f32[24,4608]{1,0:T(8,128)S(1)} %get-tuple-element.149), channel_id=1, source_target_pairs={{0,8},{1,5},{2,6},{3,11},{4,12},{5,1},{6,2},{7,15},{8,0},{9,13},{1... | collective-permute-start | bytes 1327112 | tf_op jit(solution)/shard_map/ppermute | solution.py:385
  31.7 14.6 %copy-start.9 = (f32[8,9216]{1,0:T(8,128)S(1)}, f32[8,9216]{1,0:T(8,128)}, u32[]{:S(2)}) copy-start(f32[8,9216]{1,0:T(8,128)} %get-tuple-element.144) | copy-start | bytes 884740
  31.8 16.9 %copy-start.8 = (f32[8,9216]{1,0:T(8,128)S(1)}, f32[8,9216]{1,0:T(8,128)}, u32[]{:S(2)}) copy-start(f32[8,9216]{1,0:T(8,128)} %get-tuple-element.158) | copy-start | bytes 884740
  31.8 14.5 %collective-permute-start.5 = (f32[8,9216]{1,0:T(8,128)S(1)}, f32[8,9216]{1,0:T(8,128)}, u32[]{:S(2)}, u32[]{:S(2)}) collective-permute-start(f32[8,9216]{1,0:T(8,128)S(1)} %copy-done.11), channel_id=1, source_target_pairs={{0,1},{1,0},{2,3},{3,2},{4,5},{5,4},{6,7},{7,6},{8,9},{9,8},{10,11... | collective-permute-start | bytes 884744 | tf_op jit(solution)/shard_map/ppermute | solution.py:321
  35.4 13.3 %copy-start.17 = (f32[8,9216]{1,0:T(8,128)}, f32[8,9216]{1,0:T(8,128)S(1)}, u32[]{:S(2)}) copy-start(f32[8,9216]{1,0:T(8,128)S(1)} %collective-permute-done.11.refs_12_) | copy-start | bytes 884740
  35.5 29.7 %copy-start.7 = (f32[8,9216]{1,0:T(8,128)S(1)}, f32[8,9216]{1,0:T(8,128)}, u32[]{:S(2)}) copy-start(f32[8,9216]{1,0:T(8,128)} %get-tuple-element.166) | copy-start | bytes 884740
  35.5 13.2 %collective-permute-start.13 = (f32[8,9216]{1,0:T(8,128)S(1)}, f32[8,9216]{1,0:T(8,128)}, u32[]{:S(2)}, u32[]{:S(2)}) collective-permute-start(f32[8,9216]{1,0:T(8,128)S(1)} %copy-done.10), channel_id=1, source_target_pairs={{0,1},{1,0},{2,3},{3,2},{4,5},{5,4},{6,7},{7,6},{8,9},{9,8},{10,11... | collective-permute-start | bytes 884744 | tf_op jit(solution)/shard_map/ppermute | solution.py:321
  37.4 9.0 %collective-permute-start.4 = (f32[24,2304]{1,0:T(8,128)S(1)}, f32[24,2304]{1,0:T(8,128)S(1)}, u32[]{:S(2)}, u32[]{:S(2)}) collective-permute-start(f32[24,2304]{1,0:T(8,128)S(1)} %get-tuple-element.139), channel_id=1, source_target_pairs={{0,8},{1,25},{2,26},{3,11},{4,12},{5,29},{6,30},{7,15},{8,0},{9,17... | collective-permute-start | bytes 663560 | tf_op jit(solution)/shard_map/ppermute | solution.py:385
  39.0 9.7 %collective-permute-start.12 = (f32[24,2304]{1,0:T(8,128)S(1)}, f32[24,2304]{1,0:T(8,128)S(1)}, u32[]{:S(2)}, u32[]{:S(2)}) collective-permute-start(f32[24,2304]{1,0:T(8,128)S(1)} %get-tuple-element.153), channel_id=1, source_target_pairs={{0,24},{1,9},{2,10},{3,27},{4,28},{5,13},{6,14},{7,31},{8,16},{9,1... | collective-permute-start | bytes 663560 | tf_op jit(solution)/shard_map/ppermute | solution.py:385
  46.4 13.4 %collective-permute-start.7 = (f32[8,9216]{1,0:T(8,128)S(1)}, f32[8,9216]{1,0:T(8,128)S(1)}, u32[]{:S(2)}, u32[]{:S(2)}) collective-permute-start(f32[8,9216]{1,0:T(8,128)S(1)} %copy-done.9), channel_id=1, source_target_pairs={{0,1},{1,0},{2,3},{3,2},{4,5},{5,4},{6,7},{7,6},{8,9},{9,8},{10,11... | collective-permute-start | bytes 884744 | tf_op jit(solution)/shard_map/ppermute | solution.py:321
  48.7 12.2 %collective-permute-start.15 = (f32[8,9216]{1,0:T(8,128)S(1)}, f32[8,9216]{1,0:T(8,128)S(1)}, u32[]{:S(2)}, u32[]{:S(2)}) collective-permute-start(f32[8,9216]{1,0:T(8,128)S(1)} %copy-done.8), channel_id=1, source_target_pairs={{0,1},{1,0},{2,3},{3,2},{4,5},{5,4},{6,7},{7,6},{8,9},{9,8},{10,11... | collective-permute-start | bytes 884744 | tf_op jit(solution)/shard_map/ppermute | solution.py:321
  50.4 9.4 %collective-permute-start.8 = (f32[8,128]{1,0:T(8,128)S(1)}, f32[8,128]{1,0:T(8,128)S(1)}, u32[]{:S(2)}, u32[]{:S(2)}) collective-permute-start(f32[8,128]{1,0:T(8,128)S(1)} %broadcast_in_dim.12), channel_id=1, source_target_pairs={{0,1},{1,0},{2,3},{3,2},{4,5},{5,4},{6,7},{7,6},{8,9},{9,8},{10,11... | collective-permute-start | bytes 12296 | tf_op jit(solution)/shard_map/ppermute | solution.py:321
  50.8 8.9 %collective-permute-start.6 = (f32[24,2304]{1,0:T(8,128)S(1)}, f32[24,2304]{1,0:T(8,128)S(1)}, u32[]{:S(2)}, u32[]{:S(2)}) collective-permute-start(f32[24,2304]{1,0:T(8,128)S(1)} %add.210), channel_id=1, source_target_pairs={{0,24},{1,5},{2,6},{3,27},{4,28},{5,1},{6,2},{7,31},{8,16},{9,13},... | collective-permute-start | bytes 663560 | tf_op jit(solution)/shard_map/ppermute | solution.py:385
  54.3 6.6 %collective-permute-start.14 = (f32[24,2304]{1,0:T(8,128)S(1)}, f32[24,2304]{1,0:T(8,128)S(1)}, u32[]{:S(2)}, u32[]{:S(2)}) collective-permute-start(f32[24,2304]{1,0:T(8,128)S(1)} %add.217), channel_id=1, source_target_pairs={{0,4},{1,25},{2,26},{3,7},{4,0},{5,29},{6,30},{7,3},{8,12},{9,17},... | collective-permute-start | bytes 663560 | tf_op jit(solution)/shard_map/ppermute | solution.py:385
  59.7 12.1 %copy-start.20 = (f32[8,9216]{1,0:T(8,128)}, f32[8,9216]{1,0:T(8,128)S(1)}, u32[]{:S(2)}) copy-start(f32[8,9216]{1,0:T(8,128)S(1)} %collective-permute-done.7.refs_15_) | copy-start | bytes 884740
  61.0 10.9 %copy-start.18 = (f32[8,9216]{1,0:T(8,128)}, f32[8,9216]{1,0:T(8,128)S(1)}, u32[]{:S(2)}) copy-start(f32[8,9216]{1,0:T(8,128)S(1)} %collective-permute-done.15.refs_10_) | copy-start | bytes 884740
  61.1 14.5 %collective-permute-start.19 = (f32[24,2304]{1,0:T(8,128)S(1)}, f32[24,2304]{1,0:T(8,128)S(1)}, u32[]{:S(2)}, u32[]{:S(2)}) collective-permute-start(f32[24,2304]{1,0:T(8,128)S(1)} %get-tuple-element.168), channel_id=1, source_target_pairs={{0,8},{1,9},{2,26},{3,27},{4,12},{5,13},{6,30},{7,31},{8,0},{9,1},... | collective-permute-start | bytes 663560 | tf_op jit(solution)/shard_map/ppermute | solution.py:385
  65.2 8.4 %collective-permute-start.16 = (f32[24,2304]{1,0:T(8,128)S(1)}, f32[24,2304]{1,0:T(8,128)S(1)}, u32[]{:S(2)}, u32[]{:S(2)}) collective-permute-start(f32[24,2304]{1,0:T(8,128)S(1)} %get-tuple-element.283), channel_id=1, source_target_pairs={{0,1},{1,0},{2,3},{3,2},{4,5},{5,4},{6,7},{7,6},{8,9},{9,8},{10,11... | collective-permute-start | bytes 663560 | tf_op jit(solution)/shard_map/ppermute | solution.py:321
  65.2 14.7 %collective-permute-start.20 = (f32[8,9216]{1,0:T(8,128)S(1)}, f32[8,9216]{1,0:T(8,128)S(1)}, u32[]{:S(2)}, u32[]{:S(2)}) collective-permute-start(f32[8,9216]{1,0:T(8,128)S(1)} %copy-done.7), channel_id=1, source_target_pairs={{0,1},{1,0},{2,3},{3,2},{4,5},{5,4},{6,7},{7,6},{8,9},{9,8},{10,11... | collective-permute-start | bytes 884744 | tf_op jit(solution)/shard_map/ppermute | solution.py:321
  73.5 9.7 %collective-permute-start.17 = (f32[24,2304]{1,0:T(8,128)S(1)}, f32[24,2304]{1,0:T(8,128)S(1)}, u32[]{:S(2)}, u32[]{:S(2)}) collective-permute-start(f32[24,2304]{1,0:T(8,128)S(1)} %collective-permute-done.16), channel_id=1, source_target_pairs={{0,24},{1,25},{2,10},{3,11},{4,28},{5,29},{6,14},{7,15},{8,16},{9,... | collective-permute-start | bytes 663560 | tf_op jit(solution)/shard_map/ppermute | solution.py:385
  74.7 9.1 %collective-permute-start.18 = (f32[8,9216]{1,0:T(8,128)S(1)}, f32[8,9216]{1,0:T(8,128)S(1)}, u32[]{:S(2)}, u32[]{:S(2)}) collective-permute-start(f32[8,9216]{1,0:T(8,128)S(1)} %copy-done.6), channel_id=1, source_target_pairs={{0,1},{1,0},{2,3},{3,2},{4,5},{5,4},{6,7},{7,6},{8,9},{9,8},{10,11... | collective-permute-start | bytes 884744 | tf_op jit(solution)/shard_map/ppermute | solution.py:321
  79.9 11.2 %collective-permute-start.21 = (f32[24,4608]{1,0:T(8,128)S(1)}, f32[24,4608]{1,0:T(8,128)S(1)}, u32[]{:S(2)}, u32[]{:S(2)}) collective-permute-start(f32[24,4608]{1,0:T(8,128)S(1)} %pad_maximum_fusion.8), channel_id=1, source_target_pairs={{0,4},{1,5},{2,10},{3,11},{4,0},{5,1},{6,14},{7,15},{8,12},{9,13},... | collective-permute-start | bytes 1327112 | tf_op jit(solution)/shard_map/ppermute | solution.py:385
  83.9 8.4 %collective-permute-start.23 = (f32[24,4608]{1,0:T(8,128)S(1)}, f32[24,4608]{1,0:T(8,128)S(1)}, u32[]{:S(2)}, u32[]{:S(2)}) collective-permute-start(f32[24,4608]{1,0:T(8,128)S(1)} %pad_maximum_fusion.9), channel_id=1, source_target_pairs={{0,8},{1,9},{2,6},{3,7},{4,12},{5,13},{6,2},{7,3},{8,0},{9,1},{10,... | collective-permute-start | bytes 1327112 | tf_op jit(solution)/shard_map/ppermute | solution.py:385
  91.2 4.5 %collective-permute-start.22 = (f32[24,9216]{1,0:T(8,128)S(1)}, f32[24,9216]{1,0:T(8,128)S(1)}, u32[]{:S(2)}, u32[]{:S(2)}) collective-permute-start(f32[24,9216]{1,0:T(8,128)S(1)} %pad_maximum_fusion.4.refs_6_), channel_id=1, source_target_pairs={{0,2},{1,3},{2,0},{3,1},{4,6},{5,7},{6,4},{7,5},{8,10},{9,11},{10,... | collective-permute-start | bytes 2654216 | tf_op jit(solution)/shard_map/ppermute | solution.py:385
  92.4 3.4 %collective-permute-start.24 = (f32[24,9216]{1,0:T(8,128)S(1)}, f32[24,9216]{1,0:T(8,128)S(1)}, u32[]{:S(2)}, u32[]{:S(2)}) collective-permute-start(f32[24,9216]{1,0:T(8,128)S(1)} %pad_maximum_fusion.5.refs_8_), channel_id=1, source_target_pairs={{0,2},{1,3},{2,0},{3,1},{4,6},{5,7},{6,4},{7,5},{8,10},{9,11},{10,... | collective-permute-start | bytes 2654216 | tf_op jit(solution)/shard_map/ppermute | solution.py:385
  94.3 22.0 %collective-permute-start.25 = (f32[24,9216]{1,0:T(8,128)S(1)}, f32[24,9216]{1,0:T(8,128)}, u32[]{:S(2)}, u32[]{:S(2)}) collective-permute-start(f32[24,9216]{1,0:T(8,128)S(1)} %slice_bitcast_fusion), channel_id=1, source_target_pairs={{0,1},{1,0},{2,3},{3,2},{4,5},{5,4},{6,7},{7,6},{8,9},{9,8},{10,11... | collective-permute-start | bytes 2654216 | tf_op jit(solution)/shard_map/ppermute | solution.py:321
  115.6 21.8 %collective-permute-start.26 = (f32[24,9216]{1,0:T(8,128)}, f32[24,9216]{1,0:T(8,128)S(1)}, u32[]{:S(2)}, u32[]{:S(2)}) collective-permute-start(f32[24,9216]{1,0:T(8,128)} %get-tuple-element.191), channel_id=1, source_target_pairs={{0,1},{1,0},{2,3},{3,2},{4,5},{5,4},{6,7},{7,6},{8,9},{9,8},{10,11... | collective-permute-start | bytes 2654216 | tf_op jit(solution)/shard_map/ppermute | solution.py:321
  116.3 21.1 %copy-start.30 = (f32[8,9216]{1,0:T(8,128)S(1)}, f32[8,9216]{1,0:T(8,128)}, u32[]{:S(2)}) copy-start(f32[8,9216]{1,0:T(8,128)} %get-tuple-element.197) | copy-start | bytes 884740
  137.4 10.8 %copy-start.29 = (f32[8,9216]{1,0:T(8,128)S(1)}, f32[8,9216]{1,0:T(8,128)}, u32[]{:S(2)}) copy-start(f32[8,9216]{1,0:T(8,128)} %get-tuple-element.203) | copy-start | bytes 884740
  137.4 12.7 %copy-start.5 = (f32[24,9216]{1,0:T(8,128)S(1)}, f32[24,9216]{1,0:T(8,128)}, u32[]{:S(2)}) copy-start(f32[24,9216]{1,0:T(8,128)} %get-tuple-element.205) | copy-start | bytes 2654212
  137.4 9.4 %collective-permute-start.27 = (f32[24,9216]{1,0:T(8,128)}, f32[24,9216]{1,0:T(8,128)S(1)}, u32[]{:S(2)}, u32[]{:S(2)}) collective-permute-start(f32[24,9216]{1,0:T(8,128)} %get-tuple-element.196), channel_id=1, source_target_pairs={{0,2},{1,3},{2,0},{3,1},{4,6},{5,7},{6,4},{7,5},{8,10},{9,11},{10,... | collective-permute-start | bytes 2654216 | tf_op jit(solution)/shard_map/ppermute | solution.py:385
  137.4 9.4 %collective-permute-start.28 = (f32[8,9216]{1,0:T(8,128)S(1)}, f32[8,9216]{1,0:T(8,128)S(1)}, u32[]{:S(2)}, u32[]{:S(2)}) collective-permute-start(f32[8,9216]{1,0:T(8,128)S(1)} %copy-done.30), channel_id=1, source_target_pairs={{0,1},{1,0},{2,3},{3,2},{4,5},{5,4},{6,7},{7,6},{8,9},{9,8},{10,11... | collective-permute-start | bytes 884744 | tf_op jit(solution)/shard_map/ppermute | solution.py:321
  138.2 11.9 %collective-permute-start.31 = (f32[24,9216]{1,0:T(8,128)}, f32[24,9216]{1,0:T(8,128)S(1)}, u32[]{:S(2)}, u32[]{:S(2)}) collective-permute-start(f32[24,9216]{1,0:T(8,128)} %get-tuple-element.206), channel_id=1, source_target_pairs={{0,2},{1,3},{2,0},{3,1},{4,6},{5,7},{6,4},{7,5},{8,10},{9,11},{10,... | collective-permute-start | bytes 2654216 | tf_op jit(solution)/shard_map/ppermute | solution.py:385
  148.2 10.0 %collective-permute-start.30 = (f32[8,9216]{1,0:T(8,128)S(1)}, f32[8,9216]{1,0:T(8,128)S(1)}, u32[]{:S(2)}, u32[]{:S(2)}) collective-permute-start(f32[8,9216]{1,0:T(8,128)S(1)} %copy-done.29), channel_id=1, source_target_pairs={{0,1},{1,0},{2,3},{3,2},{4,5},{5,4},{6,7},{7,6},{8,9},{9,8},{10,11... | collective-permute-start | bytes 884744 | tf_op jit(solution)/shard_map/ppermute | solution.py:321
  149.0 12.7 %collective-permute-start.29 = (f32[24,4608]{1,0:T(8,128)S(1)}, f32[24,4608]{1,0:T(8,128)S(1)}, u32[]{:S(2)}, u32[]{:S(2)}) collective-permute-start(f32[24,4608]{1,0:T(8,128)S(1)} %get-tuple-element.202), channel_id=1, source_target_pairs={{0,4},{1,5},{2,10},{3,11},{4,0},{5,1},{6,14},{7,15},{8,12},{9,13},... | collective-permute-start | bytes 1327112 | tf_op jit(solution)/shard_map/ppermute | solution.py:385
  150.2 11.7 %copy-start.25 = (f32[8,9216]{1,0:T(8,128)S(1)}, f32[8,9216]{1,0:T(8,128)}, u32[]{:S(2)}) copy-start(f32[8,9216]{1,0:T(8,128)} %get-tuple-element.216) | copy-start | bytes 884740
  150.3 14.2 %collective-permute-start.33 = (f32[8,9216]{1,0:T(8,128)S(1)}, f32[8,9216]{1,0:T(8,128)S(1)}, u32[]{:S(2)}, u32[]{:S(2)}) collective-permute-start(f32[8,9216]{1,0:T(8,128)S(1)} %copy-done.27), channel_id=1, source_target_pairs={{0,1},{1,0},{2,3},{3,2},{4,5},{5,4},{6,7},{7,6},{8,9},{9,8},{10,11... | collective-permute-start | bytes 884744 | tf_op jit(solution)/shard_map/ppermute | solution.py:321
  151.6 12.9 %collective-permute-start.32 = (f32[24,4608]{1,0:T(8,128)S(1)}, f32[24,4608]{1,0:T(8,128)S(1)}, u32[]{:S(2)}, u32[]{:S(2)}) collective-permute-start(f32[24,4608]{1,0:T(8,128)S(1)} %get-tuple-element.208), channel_id=1, source_target_pairs={{0,8},{1,9},{2,6},{3,7},{4,12},{5,13},{6,2},{7,3},{8,0},{9,1},{10,... | collective-permute-start | bytes 1327112 | tf_op jit(solution)/shard_map/ppermute | solution.py:385
  161.9 7.5 %collective-permute-start.34 = (f32[24,2304]{1,0:T(8,128)S(1)}, f32[24,2304]{1,0:T(8,128)S(1)}, u32[]{:S(2)}, u32[]{:S(2)}) collective-permute-start(f32[24,2304]{1,0:T(8,128)S(1)} %get-tuple-element.215), channel_id=1, source_target_pairs={{0,8},{1,9},{2,26},{3,27},{4,12},{5,13},{6,30},{7,31},{8,0},{9,1},... | collective-permute-start | bytes 663560 | tf_op jit(solution)/shard_map/ppermute | solution.py:385
  162.0 10.0 %collective-permute-start.35 = (f32[8,9216]{1,0:T(8,128)S(1)}, f32[8,9216]{1,0:T(8,128)S(1)}, u32[]{:S(2)}, u32[]{:S(2)}) collective-permute-start(f32[8,9216]{1,0:T(8,128)S(1)} %copy-done.25), channel_id=1, source_target_pairs={{0,1},{1,0},{2,3},{3,2},{4,5},{5,4},{6,7},{7,6},{8,9},{9,8},{10,11... | collective-permute-start | bytes 884744 | tf_op jit(solution)/shard_map/ppermute | solution.py:321
  164.6 11.7 %collective-permute-start.36 = (f32[24,2304]{1,0:T(8,128)S(1)}, f32[24,2304]{1,0:T(8,128)S(1)}, u32[]{:S(2)}, u32[]{:S(2)}) collective-permute-start(f32[24,2304]{1,0:T(8,128)S(1)} %get-tuple-element.221), channel_id=1, source_target_pairs={{0,24},{1,25},{2,10},{3,11},{4,28},{5,29},{6,14},{7,15},{8,16},{9,... | collective-permute-start | bytes 663560 | tf_op jit(solution)/shard_map/ppermute | solution.py:385
  166.4 11.9 %collective-permute-start.37 = (f32[8,9216]{1,0:T(8,128)S(1)}, f32[8,9216]{1,0:T(8,128)S(1)}, u32[]{:S(2)}, u32[]{:S(2)}) collective-permute-start(f32[8,9216]{1,0:T(8,128)S(1)} %copy-done.24), channel_id=1, source_target_pairs={{0,1},{1,0},{2,3},{3,2},{4,5},{5,4},{6,7},{7,6},{8,9},{9,8},{10,11... | collective-permute-start | bytes 884744 | tf_op jit(solution)/shard_map/ppermute | solution.py:321
  167.6 11.9 %copy-start.22 = (f32[8,9216]{1,0:T(8,128)S(1)}, f32[8,9216]{1,0:T(8,128)}, u32[]{:S(2)}) copy-start(f32[8,9216]{1,0:T(8,128)} %get-tuple-element.234) | copy-start | bytes 884740
  167.9 21.7 %copy-start.21 = (f32[8,9216]{1,0:T(8,128)S(1)}, f32[8,9216]{1,0:T(8,128)}, u32[]{:S(2)}) copy-start(f32[8,9216]{1,0:T(8,128)} %get-tuple-element.240) | copy-start | bytes 884740
  172.0 9.9 %collective-permute-start.38 = (f32[24,2304]{1,0:T(8,128)S(1)}, f32[24,2304]{1,0:T(8,128)S(1)}, u32[]{:S(2)}, u32[]{:S(2)}) collective-permute-start(f32[24,2304]{1,0:T(8,128)S(1)} %add.232), channel_id=1, source_target_pairs={{0,24},{1,25},{2,6},{3,7},{4,28},{5,29},{6,2},{7,3},{8,16},{9,17},... | collective-permute-start | bytes 663560 | tf_op jit(solution)/shard_map/ppermute | solution.py:385
  175.4 9.9 %collective-permute-start.39 = (f32[8,9216]{1,0:T(8,128)S(1)}, f32[8,9216]{1,0:T(8,128)S(1)}, u32[]{:S(2)}, u32[]{:S(2)}) collective-permute-start(f32[8,9216]{1,0:T(8,128)S(1)} %copy-done.23), channel_id=1, source_target_pairs={{0,1},{1,0},{2,3},{3,2},{4,5},{5,4},{6,7},{7,6},{8,9},{9,8},{10,11... | collective-permute-start | bytes 884744 | tf_op jit(solution)/shard_map/ppermute | solution.py:321
  178.3 23.1 %copy-start.19 = (f32[8,9216]{1,0:T(8,128)S(1)}, f32[8,9216]{1,0:T(8,128)}, u32[]{:S(2)}) copy-start(f32[8,9216]{1,0:T(8,128)} %get-tuple-element.246) | copy-start | bytes 884740
  178.4 12.1 %collective-permute-start.40 = (f32[24,2304]{1,0:T(8,128)S(1)}, f32[24,2304]{1,0:T(8,128)S(1)}, u32[]{:S(2)}, u32[]{:S(2)}) collective-permute-start(f32[24,2304]{1,0:T(8,128)S(1)} %add.233), channel_id=1, source_target_pairs={{0,4},{1,5},{2,26},{3,27},{4,0},{5,1},{6,30},{7,31},{8,12},{9,13},... | collective-permute-start | bytes 663560 | tf_op jit(solution)/shard_map/ppermute | solution.py:385
  179.5 12.2 %collective-permute-start.41 = (f32[8,9216]{1,0:T(8,128)S(1)}, f32[8,9216]{1,0:T(8,128)S(1)}, u32[]{:S(2)}, u32[]{:S(2)}) collective-permute-start(f32[8,9216]{1,0:T(8,128)S(1)} %copy-done.22), channel_id=1, source_target_pairs={{0,1},{1,0},{2,3},{3,2},{4,5},{5,4},{6,7},{7,6},{8,9},{9,8},{10,11... | collective-permute-start | bytes 884744 | tf_op jit(solution)/shard_map/ppermute | solution.py:321
  185.4 17.0 %collective-permute-start.42 = (f32[24,2304]{1,0:T(8,128)S(1)}, f32[24,2304]{1,0:T(8,128)S(1)}, u32[]{:S(2)}, u32[]{:S(2)}) collective-permute-start(f32[24,2304]{1,0:T(8,128)S(1)} %add.234), channel_id=1, source_target_pairs={{0,8},{1,9},{2,26},{3,27},{4,12},{5,13},{6,30},{7,31},{8,0},{9,1},... | collective-permute-start | bytes 663560 | tf_op jit(solution)/shard_map/ppermute | solution.py:385
  189.6 12.8 %collective-permute-start.43 = (f32[8,9216]{1,0:T(8,128)S(1)}, f32[8,9216]{1,0:T(8,128)S(1)}, u32[]{:S(2)}, u32[]{:S(2)}) collective-permute-start(f32[8,9216]{1,0:T(8,128)S(1)} %copy-done.21), channel_id=1, source_target_pairs={{0,1},{1,0},{2,3},{3,2},{4,5},{5,4},{6,7},{7,6},{8,9},{9,8},{10,11... | collective-permute-start | bytes 884744 | tf_op jit(solution)/shard_map/ppermute | solution.py:321
  191.7 9.7 %collective-permute-start.44 = (f32[24,2304]{1,0:T(8,128)S(1)}, f32[24,2304]{1,0:T(8,128)S(1)}, u32[]{:S(2)}, u32[]{:S(2)}) collective-permute-start(f32[24,2304]{1,0:T(8,128)S(1)} %add.235), channel_id=1, source_target_pairs={{0,1},{1,0},{2,3},{3,2},{4,5},{5,4},{6,7},{7,6},{8,9},{9,8},{10,11... | collective-permute-start | bytes 663560 | tf_op jit(solution)/shard_map/ppermute | solution.py:321
  201.5 7.8 %collective-permute-start.45 = (f32[24,2304]{1,0:T(8,128)S(1)}, f32[24,2304]{1,0:T(8,128)S(1)}, u32[]{:S(2)}, u32[]{:S(2)}) collective-permute-start(f32[24,2304]{1,0:T(8,128)S(1)} %collective-permute-done.44), channel_id=1, source_target_pairs={{0,24},{1,25},{2,10},{3,11},{4,28},{5,29},{6,14},{7,15},{8,16},{9,... | collective-permute-start | bytes 663560 | tf_op jit(solution)/shard_map/ppermute | solution.py:385
  201.5 7.8 %collective-permute-start.46 = (f32[8,9216]{1,0:T(8,128)S(1)}, f32[8,9216]{1,0:T(8,128)S(1)}, u32[]{:S(2)}, u32[]{:S(2)}) collective-permute-start(f32[8,9216]{1,0:T(8,128)S(1)} %copy-done.19), channel_id=1, source_target_pairs={{0,1},{1,0},{2,3},{3,2},{4,5},{5,4},{6,7},{7,6},{8,9},{9,8},{10,11... | collective-permute-start | bytes 884744 | tf_op jit(solution)/shard_map/ppermute | solution.py:321
  202.5 12.2 %collective-permute-start.49 = (f32[24,4608]{1,0:T(8,128)S(1)}, f32[24,4608]{1,0:T(8,128)S(1)}, u32[]{:S(2)}, u32[]{:S(2)}) collective-permute-start(f32[24,4608]{1,0:T(8,128)S(1)} %pad_maximum_fusion.11), channel_id=1, source_target_pairs={{0,4},{1,5},{2,10},{3,11},{4,0},{5,1},{6,14},{7,15},{8,12},{9,13},... | collective-permute-start | bytes 1327112 | tf_op jit(solution)/shard_map/ppermute | solution.py:385
  209.4 8.4 %collective-permute-start.47 = (f32[24,4608]{1,0:T(8,128)S(1)}, f32[24,4608]{1,0:T(8,128)S(1)}, u32[]{:S(2)}, u32[]{:S(2)}) collective-permute-start(f32[24,4608]{1,0:T(8,128)S(1)} %pad_maximum_fusion.10), channel_id=1, source_target_pairs={{0,8},{1,9},{2,6},{3,7},{4,12},{5,13},{6,2},{7,3},{8,0},{9,1},{10,... | collective-permute-start | bytes 1327112 | tf_op jit(solution)/shard_map/ppermute | solution.py:385
  214.9 3.1 %collective-permute-start.50 = (f32[24,9216]{1,0:T(8,128)S(1)}, f32[24,9216]{1,0:T(8,128)S(1)}, u32[]{:S(2)}, u32[]{:S(2)}) collective-permute-start(f32[24,9216]{1,0:T(8,128)S(1)} %pad_maximum_fusion.7), channel_id=1, source_target_pairs={{0,2},{1,3},{2,0},{3,1},{4,6},{5,7},{6,4},{7,5},{8,10},{9,11},{10,... | collective-permute-start | bytes 2654216 | tf_op jit(solution)/shard_map/ppermute | solution.py:385
  217.9 2.5 %collective-permute-start.48 = (f32[24,9216]{1,0:T(8,128)S(1)}, f32[24,9216]{1,0:T(8,128)S(1)}, u32[]{:S(2)}, u32[]{:S(2)}) collective-permute-start(f32[24,9216]{1,0:T(8,128)S(1)} %pad_maximum_fusion.6), channel_id=1, source_target_pairs={{0,2},{1,3},{2,0},{3,1},{4,6},{5,7},{6,4},{7,5},{8,10},{9,11},{10,... | collective-permute-start | bytes 2654216 | tf_op jit(solution)/shard_map/ppermute | solution.py:385
  (18 other events, 77.8 us)

commit v3 on v2

--- a/solution.py
+++ b/solution.py
@@ -144,39 +144,43 @@
     return max(k for k in range(1, limit + 1) if total % k == 0)
 
 
-def pair_kernel(count, unit, batch, planes, band, has_total, sizes, core_ref, *refs):
-    into_x, out_of_x, along_y, along_z, *refs = refs
-    in_rows, out_rows = sizes
+def pair_kernel(count, unit, batch, planes, specs, has_total, place_ref, *refs):
+    in_specs, out_specs = specs
+    forth, along_z, *refs = refs
     half, quarter = count // 2, count // 4
-    n_in = 6 + len(in_rows) + (4 if has_total else 0)
-    n_out = 5 + len(out_rows)
-    orbitals, coulomb_in, *others = refs[:n_in]
-    block_in, totals_in, others = others[:4], others[4 + len(in_rows) :], others[4 : 4 + len(in_rows)]
-    local_out, *backs = refs[n_in : n_in + n_out]
-    terms_out, backs = backs[:4], backs[4:]
+    n_in = 5 + len(in_specs) + (4 if has_total else 0)
+    n_out = 4 + len(out_specs)
+    coulomb_in, *others = refs[:n_in]
+    block_in, orbital_in, totals_in = others[:4], others[4 : 4 + len(in_specs)], others[4 + len(in_specs) :]
+    terms_out, local_out = refs[n_in : n_in + 4], refs[n_in + 4 : n_in + n_out]
     first, second, coulomb, total, local, terms, cells, in_sems, out_sems, wide_sem = refs[n_in + n_out :]
     width = batch * unit
     steps = count * count // width
-    mine, theirs = core_ref[0] * quarter, quarter - core_ref[0] * quarter
-
-    def spans(buffer, pieces):
+    plane, core = place_ref[0], place_ref[1]
+    starts = (plane * half, half - plane * half)
+    parts = (core * quarter, quarter - core * quarter)
+
+    def span(ref, buffer, start, rows):
+        start = start if isinstance(start, int) else pl.multiple_of(start, 8)
+        return ref, buffer.at[pl.ds(start, rows)]
+
+    def by_core(buffer, arrays):
+        places = [start + part for start in starts for part in parts]
+        return [span(ref, buffer, start, quarter) for ref, start in zip(arrays, places)]
+
+    def by_spec(buffer, arrays, given):
         result = []
-        for ref, start, rows in pieces:
-            start = start if isinstance(start, int) else pl.multiple_of(start, 8)
-            result.append((ref, buffer.at[pl.ds(start, rows)]))
+        for ref, (index, which, row, rows) in zip(arrays, given):
+            ref = ref if index is None else ref.at[index]
+            if which is None:
+                result += [span(ref.at[k], buffer, k * half, half) for k in range(2)]
+            else:
+                result.append(span(ref, buffer, starts[which] + row, rows))
         return result
 
-    def by_core(buffer, parts):
-        starts = [k * half + start for k in range(2) for start in (mine, theirs)]
-        return spans(buffer, [(ref, start, quarter) for ref, start in zip(parts, starts)])
-
-    def by_size(buffer, own, rest, rows):
-        starts = [half + sum(rows[:k]) for k in range(len(rows))]
-        return spans(buffer, [(own, 0, half)] + list(zip(rest, starts, rows)))
-
-    loads = by_size(first, orbitals.at[band], others, in_rows) + by_core(second, block_in)
+    loads = by_spec(first, orbital_in, in_specs) + by_core(second, block_in)
     late = by_core(total, totals_in) if has_total else []
-    stores = by_size(local, local_out, backs, out_rows) + by_core(terms, terms_out)
+    stores = by_core(terms, terms_out) + by_spec(local, local_out, out_specs)
 
     def copies(pairs, sems, step, offset, outward):
         columns = pl.ds(pl.multiple_of(step * width, LANES), width)
@@ -189,36 +193,37 @@
         for copy in copies(loads, in_sems, step, 0, False):
             copy.start()
     wide.start()
-    for step in range(steps):
-        for copy in copies(late, in_sems, step, len(loads), False):
-            copy.start()
 
     def forward(step, carry):
         for copy in copies(loads, in_sems, step, 0, False):
             copy.wait()
         columns = pl.ds(pl.multiple_of(step * width, LANES), width)
-        density = transform_rows(into_x[...], first[:, columns] * second[:, columns])
-        parts = []
+        density = transform_rows(forth[...], first[:, columns] * second[:, columns])
+        pieces = []
         for start in range(0, width, unit):
             piece = density[:, start : start + unit]
             for offset in range(0, unit, count):
                 shifted = pltpu.roll(piece, unit - offset, 1) if offset else piece
-                parts.append(shifted[:, :LANES])
+                pieces.append(shifted[:, :LANES])
         rows = pl.ds(pl.multiple_of(step * width, 8), width)
-        cells[rows, :] = transform_lanes(jnp.concatenate(parts, 0), along_z[...])
+        cells[pl.ds(step * (width // count), width // count)] = transform_lanes(jnp.concatenate(pieces, 0), along_z[...]).reshape(width // count, count, LANES)
         return carry
 
     lax.fori_loop(0, steps, forward, 0)
+    for step in range(steps):
+        for copy in copies(late, in_sems, step, len(loads), False):
+            copy.start()
     wide.wait()
 
     def middle(step, carry):
         start = step * planes
-        values = [cells[pl.ds(start + k, count, stride=count), :] for k in range(planes)]
-        spectrum = transform_rows(along_y[...], jnp.concatenate(values, 1))
+        cube = jnp.swapaxes(cells[:, pl.ds(pl.multiple_of(start, 8), planes), :], 0, 1)
+        values = [cube[k] for k in range(planes)]
+        spectrum = transform_rows(forth[...], jnp.concatenate(values, 1))
         scale = jnp.concatenate([coulomb[start + k] for k in range(planes)], 1)
-        scaled = transform_rows(along_y[...], spectrum * scale)
-        for k in range(planes):
-            cells[pl.ds(start + k, count, stride=count), :] = scaled[:, k * LANES : (k + 1) * LANES]
+        scaled = transform_rows(forth[...], spectrum * scale)
+        cube = jnp.stack([scaled[:, k * LANES : (k + 1) * LANES] for k in range(planes)], 0)
+        cells[:, pl.ds(pl.multiple_of(start, 8), planes), :] = jnp.swapaxes(cube, 0, 1)
         return carry
 
     lax.fori_loop(0, count // planes, middle, 0)
@@ -226,7 +231,7 @@
 
     def inverse(step, carry):
         rows = pl.ds(pl.multiple_of(step * width, 8), width)
-        values = transform_lanes(cells[rows, :], along_z[...])
+        values = transform_lanes(cells[pl.ds(step * (width // count), width // count)].reshape(width, LANES), along_z[...])
         tiles = [None] * (width // LANES)
 
         def add(tile, value):
@@ -242,7 +247,7 @@
             else:
                 add(tile, jnp.where(lane >= offset, piece, 0.0))
                 add(tile + 1, jnp.where(lane < offset, piece, 0.0))
-        potential = transform_rows(out_of_x[...], jnp.concatenate(tiles, 1))
+        potential = transform_rows(forth[...], jnp.concatenate(tiles, 1))
         for copy in copies(late, in_sems, step, len(loads), False):
             copy.wait()
         columns = pl.ds(pl.multiple_of(step * width, LANES), width)
@@ -261,24 +266,25 @@
             copy.wait()
 
 
-def pair_terms(orbitals, band, others, block, coulomb, core, tables, back_rows, totals=()):
-    _, half, flat_cells = orbitals.shape
-    count, quarter = 2 * half, half // 2
+def pair_terms(orbital, block, coulomb, place, tables, out_specs, totals=()):
+    arrays, in_specs = zip(*orbital)
+    quarter, flat_cells = block[0].shape
+    count = 4 * quarter
     unit = math.lcm(count, LANES)
-    batch = divisor(flat_cells // unit, 8)
+    batch = divisor(flat_cells // unit, 12)
     planes = divisor(count, 16)
     steps = flat_cells // (batch * unit)
-    in_rows, out_rows = tuple(v.shape[0] for v in others), tuple(back_rows)
-    operands = [orbitals, coulomb, *block, *others, *totals]
+    operands = [coulomb, *block, *arrays, *totals]
     vmem = pl.BlockSpec(memory_space=pltpu.VMEM)
     anywhere = pl.BlockSpec(memory_space=pl.ANY)
-    shapes = [(half, flat_cells)] + [(quarter, flat_cells)] * 4
-    shapes += [(rows, flat_cells) for rows in out_rows]
+    shapes = [(quarter, flat_cells)] * 4
+    for _, which, _, rows in out_specs:
+        shapes.append((2, 2 * quarter, flat_cells) if which is None else (rows, flat_cells))
     whole = pltpu.VMEM((count, flat_cells), jnp.float32)
     moved = 4 * sum(math.prod(s) for s in shapes + [v.shape for v in operands])
-    sizes = (in_rows, out_rows)
+    specs = (tuple(in_specs), tuple(out_specs))
     return pl.pallas_call(
-        functools.partial(pair_kernel, count, unit, batch, planes, band, bool(totals), sizes),
+        functools.partial(pair_kernel, count, unit, batch, planes, specs, bool(totals)),
         in_specs=[pl.BlockSpec(memory_space=pltpu.SMEM)]
         + [vmem] * len(tables)
         + [anywhere] * len(operands),
@@ -291,9 +297,9 @@
             whole if totals else pltpu.VMEM((8, LANES), jnp.float32),
             whole,
             whole,
-            pltpu.VMEM((flat_cells, LANES), jnp.float32),
-            pltpu.SemaphoreType.DMA((9 + len(in_rows), steps)),
-            pltpu.SemaphoreType.DMA((5 + len(out_rows), steps)),
+            pltpu.VMEM((count, count, LANES), jnp.float32),
+            pltpu.SemaphoreType.DMA((10 + len(in_specs), steps)),
+            pltpu.SemaphoreType.DMA((6 + len(out_specs), steps)),
             pltpu.SemaphoreType.DMA,
         ],
         compiler_params=pltpu.CompilerParams(vmem_limit_bytes=60 * 2**20),
@@ -301,7 +307,7 @@
             flops=6 * flat_cells * count * 16 * LANES, bytes_accessed=moved, transcendentals=0
         ),
         name="pair_terms",
-    )(core, *tables, *operands)
+    )(place, *tables, *operands)
 
 
 def halves(values, upper, dim):
@@ -325,26 +331,33 @@
     return lax.optimization_barrier(values)
 
 
+def squared_components(count):
+    positions = np.arange(count)
+    return np.where(positions <= count // 2, positions, positions - count).astype(np.int32) ** 2
+
+
 def largest_length(cutoff_mask, count):
-    columns = cutoff_mask.shape[1] // count
-    positions = jnp.arange(count, dtype=jnp.int32)
-    signed = jnp.where(positions <= count // 2, positions, positions - count)
-    squares = signed * signed
-    mine = lax.dynamic_slice_in_dim(squares, lax.axis_index("fft") * columns, columns)
-    flat = (mine[:, None] + squares[None, :]).reshape(-1)
-    lengths = jnp.where(cutoff_mask != 0, squares[:, None] + flat[None, :], 0)
+    squares = squared_components(count)
+    flat = (squares[:, None] + squares[None, :]).reshape(-1, cutoff_mask.shape[1])
+    mine = jnp.asarray(flat)[lax.axis_index("fft")]
+    lengths = jnp.where(cutoff_mask != 0, squares[:, None] + mine[None, :], 0)
     return jnp.full((8, LANES), jnp.max(lengths).astype(jnp.float32))
 
 
 def coulomb_table(limit, count):
-    positions = jnp.arange(count, dtype=jnp.int32)
-    signed = jnp.where(positions <= count // 2, positions, positions - count)
-    squares = signed * signed
-    padded = jnp.concatenate([squares, jnp.full((LANES - count,), 4 * count * count, jnp.int32)])
-    squared = squares[:, None, None] + squares[None, :, None] + padded[None, None, :]
+    def squares(dim):
+        position = lax.broadcasted_iota(jnp.int32, (count, count, LANES), dim)
+        signed = jnp.where(position <= count // 2, position, position - count)
+        return signed * signed
+
+    squared = squares(0) + squares(1) + squares(2)
     weights = ((squared >= 1) & (squared <= limit)).astype(jnp.float32)
     factor = -EXCHANGE_MIX * COULOMB / float(count**3)
     return factor * weights / jnp.maximum(squared, 1).astype(jnp.float32)
+
+
+def rows_of(array, index, start, rows):
+    return array[index, start : start + rows]
 
 
 class Beside:
@@ -355,21 +368,21 @@
         self.arrived = {}
 
     def open(self, step, *values):
-        self.arrived[step] = None
         if step in self.sends:
-            *values, send = tied(*values, self.sends[step])
-            self.arrived[step] = across(send)
+            array, *cut = self.sends[step]
+            *values, array = tied(*values, array)
+            self.arrived[step] = across(rows_of(array, *cut))
+        if step in self.needed:
+            array, function = self.needed[step]
+            *values, array = tied(*values, array)
+            self.results[step] = function(array, self.results)
         return values
 
     def close(self, step, value):
-        if step in self.sends:
-            value, self.arrived[step] = tied(value, self.arrived[step])
-        if step in self.needed:
-            value, self.results[step] = tied(value, self.needed[step](self.results))
+        for found in (self.arrived, self.results):
+            if step in found:
+                value, found[step] = tied(value, found[step])
         return value
-
-    def pieces(self, *steps):
-        return [self.arrived[step] for step in steps]
 
 
 def band_sum(parts, exchange, beside, flip):
@@ -400,24 +413,37 @@
         bits = jnp.where(turned, depth_low, side == 1), jnp.where(turned, depth_high, depth_low)
         return bits, (by_core(2, 4), by_core(4, 12), by_core(12, 2))
 
-    def down(which):
-        bits, partners = axes(which, flip)
-        keep, send = parts[which]
-        value = added((which, "core"), send, across_cores, keep)
-        keep, send = halves(value, bits[0], 1)
-        value = added((which, "first"), send, partners[0], keep)
-        keep, send = halves(value, bits[1], 1)
-        value = added((which, "second"), send, partners[1], keep)
-        return added((which, "third"), value, partners[2])
-
-    def up(which, value):
-        bits, partners = axes(which, 0)
-        value = joined(*swap((which, "up_second"), value, partners[1]), bits[1], 1)
-        value = joined(*swap((which, "up_first"), value, partners[0]), bits[0], 1)
-        return swap((which, "core_back"), value, across_cores)
-
-    pieces = exchange(down(0), down(1))
-    return [up(which, piece) for which, piece in enumerate(pieces)]
+    def after(value, other):
+        return value
+
+    values = [None, None]
+    earlier = [None, None]
+    for which, (keep, send) in enumerate(parts):
+        values[which] = added((which, "core"), send, across_cores, keep)
+    for number, name in enumerate(("first", "second", "third")):
+        results = []
+        for which in range(2):
+            bits, partners = axes(which, flip)
+            value = after(values[which], earlier[1 - which])
+            if number < 2:
+                keep, send = halves(value, bits[number], 1)
+                results.append(added((which, name), send, partners[number], keep))
+            else:
+                results.append(added((which, name), value, partners[number]))
+        earlier, values = values, results
+    values = exchange(*values)
+    earlier = [None, None]
+    for number, name in ((1, "up_second"), (0, "up_first")):
+        results = []
+        for which in range(2):
+            bits, partners = axes(which, 0)
+            value = after(values[which], earlier[1 - which])
+            results.append(joined(*swap((which, name), value, partners[number]), bits[number], 1))
+        earlier, values = values, results
+    return [
+        swap((which, "core_back"), after(values[which], earlier[1 - which]), across_cores)
+        for which in range(2)
+    ]
 
 
 def per_device_pairs(orbitals, owners, cutoff_mask):
@@ -425,13 +451,10 @@
     count = 2 * half
     plane = lax.axis_index("fft")
     core = lax.axis_index("band") % 2
-    core_scalar = jnp.full((1,), core, jnp.int32)
+    place = jnp.stack([plane, core]).astype(jnp.int32)
     casine = casine_matrix(count)
-    orders = [np.roll(np.arange(count), -half * k) for k in range(2)]
-    into_x = jnp.asarray(np.stack([left_table(casine[:, order]) for order in orders]))[plane]
-    out_of_x = jnp.asarray(np.stack([left_table(casine[order, :]) for order in orders]))[plane]
-    along_y, along_z = jnp.asarray(left_table(casine)), jnp.asarray(right_table(casine))
-    length = largest_length(cutoff_mask, count)
+    tables = (jnp.asarray(left_table(casine)), jnp.asarray(right_table(casine)))
+    sixth = half // 6
 
     def gather_band(first, second):
         mine, theirs = jnp.where(plane == 1, second, first), jnp.where(plane == 1, first, second)
@@ -440,52 +463,67 @@
     def gather_half(own, other):
         return own, across(other)
 
-    sixth = half // 6
-    cut = lambda band, start, rows: orbitals[band, sixth * start : sixth * (start + rows)]
-    steps = [(0, "core")]
-    steps += [(k, name) for name in ("first", "second", "third", "up_second") for k in range(2)]
-    places = [(0, k) for k in range(6)] + [(1, k) for k in range(3)]
+    def pieces(sizes):
+        return [(None, 1, sixth * sum(sizes[:k]), sixth * size) for k, size in enumerate(sizes)]
+
+    def sent(names, band, sizes):
+        rows = pieces(sizes)
+        return {(1, name): (orbitals, band, *spec[2:]) for name, spec in zip(names, rows)}
+
+    steps = ("first", "second", "third", "up_second", "up_first")
+    names = [(k, name) for name in steps for k in range(2)]
+    sizes = ((1,) * 6, (1, 1, 1, 1, 2))
+    rows = [(orbitals, band, *spec[2:]) for band in range(2) for spec in pieces(sizes[band])]
     beside = Beside(
-        {step: cut(*place, 1) for step, place in zip(steps, places)},
+        dict(zip(names, rows)),
         {
-            (0, "first"): lambda got: (length, into_x, out_of_x),
-            (0, "third"): lambda got: jnp.maximum(
-                got[0, "first"][0], across(got[0, "first"][0])
+            (0, "first"): (cutoff_mask, lambda mask, got: largest_length(mask, count)),
+            (0, "second"): (
+                cutoff_mask,
+                lambda _, got: jnp.maximum(got[0, "first"], across(got[0, "first"])),
             ),
-            (1, "up_second"): lambda got: coulomb_table(
-                got[0, "third"][0, 0].astype(jnp.int32), count
+            (0, "up_first"): (
+                cutoff_mask,
+                lambda _, got: coulomb_table(got[0, "second"][0, 0].astype(jnp.int32), count),
             ),
         },
     )
-    owned = jnp.where(lax.axis_index("band") == owners[0], orbitals, 0.0)
-    block = band_sum([halves(v, core == 1, 0) for v in owned], gather_band, beside, 1)
-    tables = (*beside.results[0, "first"][1:], along_y, along_z)
-    coulomb = beside.results[1, "up_second"]
+    owner = lax.axis_index("band") == owners[0]
+    owned = [
+        [jnp.where(owner, part, 0.0) for part in halves(orbitals[band], core == 1, 0)]
+        for band in range(2)
+    ]
+    block = band_sum(owned, gather_band, beside, 1)
+    coulomb = beside.results[0, "up_first"]
     block = [*block[0], *block[1]]
-    arrived = beside.pieces(*steps)
-    block[0], last = tied(block[0], cut(1, 3, 3))
-    last = across(last)
-    own0, *rest = pair_terms(
-        orbitals, 0, arrived[:6], block, coulomb, core_scalar, tables, [3 * sixth] + [sixth] * 3
-    )
-    terms, backs0 = rest[:4], rest[4:]
-    back0 = across(backs0[0])
-    own1, *rest = pair_terms(
-        orbitals, 1, arrived[6:] + [last], block, coulomb, core_scalar, tables, [sixth] * 6, terms
-    )
-    terms, backs1 = rest[:4], rest[4:]
-    *terms, back0 = tied(*terms, back0)
-    beside = Beside(dict(zip(steps, backs0[1:] + backs1)))
+    block[0], later = tied(block[0], orbitals)
+    last = across(rows_of(later, *rows[-1][1:]))
+    arrived = [beside.arrived[name] for name in names] + [last]
+    orbital = [(orbitals, (0, 0, 0, half)), *zip(arrived[:6], pieces(sizes[0]))]
+    back_sizes = ((2, 1, 1, 1, 1), (1,) * 6)
+    out_specs = [(None, 0, 0, half), *pieces(back_sizes[0])]
+    *terms, own0, back0, back1, back2, back3, back4 = pair_terms(
+        orbital, block, coulomb, place, tables, out_specs
+    )
+    back0 = across(back0)
+    orbital = [(orbitals, (1, 0, 0, half)), *zip(arrived[6:], pieces(sizes[1]))]
+    out_specs = [(None, 0, 0, half), *pieces(back_sizes[1])]
+    results = pair_terms(orbital, block, coulomb, place, tables, out_specs, terms)
+    *terms, back0 = tied(*results[:4], back0)
+    own1 = results[4]
+    backs = [back1, back2, back3, back4, *results[5:]]
+    beside = Beside(
+        {name: (back[None], 0, 0, back.shape[0]) for name, back in zip(names, backs)}
+    )
     sums = band_sum([terms[:2], terms[2:]], gather_half, beside, 0)
     own_band, other_band = [joined(*parts, core == 1, 0) for parts in sums]
     block_total = jnp.stack(
         [jnp.where(plane == 1, other_band, own_band), jnp.where(plane == 1, own_band, other_band)]
     )
-    arrived = beside.pieces(*steps)
-    back0 = jnp.concatenate([back0] + arrived[:3], 0)
-    back1 = jnp.concatenate(arrived[3:], 0)
-    local_total = jnp.stack([own0 + back0, own1 + back1])
-    return local_total, block_total
+    arrived = [beside.arrived[name] for name in names]
+    back0 = jnp.concatenate([back0] + arrived[:4], 0)
+    back1 = jnp.concatenate(arrived[4:], 0)
+    return jnp.stack([own0 + back0, own1 + back1]), block_total
 
 
 def solution(mesh):

time: 223 us -> 208 us (0.933)
  waiting for transfers between devices: 90.6 us -> 81.9 us
  Pallas kernels: 38.8 us -> 31.5 us
  starting transfers between devices: 58.5 us -> 62.2 us
  local copies, waits for them, and re-layouts: 10.6 us -> 7.14 us
    ppermute x28, waiting for transfers between devices: 38.1 us -> 20 us  [swap(): arrived = lax.ppermute(value, ('band', 'fft'), pairs)]
    ppermute x23 -> x25, waiting for transfers between devices: 52.5 us -> 61.9 us  [across(): return lax.ppermute(value, 'fft', [(0, 1), (1, 0)])]
    pallas_call x2, Pallas kernels: 38.8 us -> 31.5 us  [pair_terms(): pl.pallas_call(functools.partial(pair_kernel, count, unit, batch, planes,...]
    ppermute x23 -> x25, starting transfers between devices: 25.6 us -> 30.8 us  [across(): return lax.ppermute(value, 'fft', [(0, 1), (1, 0)])]
    squeeze x3 -> x11, local copies, waits for them, and re-layouts: 6.2 us -> 1.68 us  [rows_of(): return array[index, start:start + rows]]
    select_n x2, other arithmetic: 0.37 us -> 3.57 us  [the longest x1 3.5 us: per_device_pairs(): jnp.where(owner, part, 0.0)]
    add x14 -> x13, other arithmetic: 4.59 us -> 3.37 us  [added(): return kept + arrived]
  transfers between devices with their start and end apart: 51 -> 53, of which waited for: 29 -> 27; matrix products, arithmetic and copies ran while one was open for 10% -> 7% of each run, Pallas kernels for 17% -> 15%
where the time goes in v3:
time: 208 us; the launch traced here: 207 us
  waiting for transfers between devices  81.9 us (39%)
  starting transfers between devices  62.2 us (30%)
  Pallas kernels  31.5 us (15%)
  other arithmetic  20.9 us (10%)
  local copies, waits for them, and re-layouts  7.14 us (3%)
  between operations  3.36 us (2%)
    ppermute x25, waiting for transfers between devices, across(): return lax.ppermute(value, 'fft', [(0, 1), (1, 0)])  61.9 us
    pallas_call x2, Pallas kernels, pair_terms(): pl.pallas_call(functools.partial(pair_kernel, count, unit, batch, planes,...  31.5 us
    ppermute x28, starting transfers between devices, swap(): arrived = lax.ppermute(value, ('band', 'fft'), pairs)  31.4 us
    ppermute x25, starting transfers between devices, across(): return lax.ppermute(value, 'fft', [(0, 1), (1, 0)])  30.8 us
    ppermute x28, waiting for transfers between devices, swap(): arrived = lax.ppermute(value, ('band', 'fft'), pairs)  20 us
    div x1, other arithmetic, coulomb_table(): return factor * weights / jnp.maximum(squared, 1).astype(jnp.float32)  4.63 us
  transfers between devices with their start and end apart: 53, of which 27 were waited for; matrix products, arithmetic and copies ran while one was open for 7% of the time, Pallas kernels for 15%

profile of v3, /device:TPU:0, one launch (start us, length us, event | category | flops | bytes accessed | tf_op | source)
XLA Modules:
  0.0 207.1 jit_solution(15150859402020616779)
XLA Ops:
  1.3 3.5 %select_bitcast_fusion.5 = (f32[24,9216]{1,0:T(8,128)}, f32[24,9216]{1,0:T(8,128)}) fusion(f32[2,48,9216]{2,1,0:T(8,128)} %refs_7_.3, pred[]{:T(512)S(6)} %eq.88, pred[]{:T(512)S(6)} %eq.87), kind=kLoop, calls=%fused_computation.25 | loop fusion | flops 884736 | bytes 5308418 | tf_op jit(solution)/shard_map/jit(_where)/select_n | solution.py:493
  7.7 1.3 collective-permute-done.7
  8.9 1.7 bitcast_add_fusion.1
  10.6 1.3 slice_select_fusion.4
  12.6 2.9 %collective-permute-start.2 = (f32[8,9216]{1,0:T(8,128)}, f32[8,9216]{1,0:T(8,128)}, u32[]{:S(2)}, u32[]{:S(2)}) collective-permute-start(f32[8,9216]{1,0:T(8,128)} %slice_bitcast_fusion.10), channel_id=1, source_target_pairs={{0,1},{1,0},{2,3},{3,2},{4,5},{5,4},{6,7},{7,6},{8,9},{9,8},{10,11... | collective-permute-start | bytes 884744 | tf_op jit(solution)/shard_map/ppermute | solution.py:327
  15.5 1.6 collective-permute-start.1
  17.8 1.3 select_reduce_fusion
  20.3 1.1 collective-permute-start.8
  21.4 2.2 %collective-permute-done.2.refs_9_ = f32[8,9216]{1,0:T(8,128)} collective-permute-done((f32[8,9216]{1,0:T(8,128)}, f32[8,9216]{1,0:T(8,128)}, u32[]{:S(2)}, u32[]{:S(2)}) %collective-permute-start.2) | collective-permute-done | bytes 294944 | tf_op jit(solution)/shard_map/ppermute | solution.py:327
  23.6 2.0 collective-permute-done.1
  25.6 1.2 add.166
  26.8 3.9 %collective-permute-start.3 = (f32[24,2304]{1,0:T(8,128)S(1)}, f32[24,2304]{1,0:T(8,128)S(1)}, u32[]{:S(2)}, u32[]{:S(2)}) collective-permute-start(f32[24,2304]{1,0:T(8,128)S(1)} %get-tuple-element.148), channel_id=1, source_target_pairs={{0,24},{1,9},{2,10},{3,27},{4,28},{5,13},{6,14},{7,31},{8,16},{9,1... | collective-permute-start | bytes 663560 | tf_op jit(solution)/shard_map/ppermute | solution.py:398
  31.7 2.1 collective-permute-start.12
  34.4 2.6 %collective-permute-start.11 = (f32[8,9216]{1,0:T(8,128)S(1)}, f32[8,9216]{1,0:T(8,128)S(1)}, u32[]{:S(2)}, u32[]{:S(2)}) collective-permute-start(f32[8,9216]{1,0:T(8,128)S(1)} %slice_bitcast_fusion.6), channel_id=1, source_target_pairs={{0,1},{1,0},{2,3},{3,2},{4,5},{5,4},{6,7},{7,6},{8,9},{9,8},{10,11... | collective-permute-start | bytes 884744 | tf_op jit(solution)/shard_map/ppermute | solution.py:327
  37.0 1.2 collective-permute-done.12
  38.2 3.4 %collective-permute-start.5 = (f32[24,2304]{1,0:T(8,128)S(1)}, f32[24,2304]{1,0:T(8,128)S(1)}, u32[]{:S(2)}, u32[]{:S(2)}) collective-permute-start(f32[24,2304]{1,0:T(8,128)S(1)} %add.167), channel_id=1, source_target_pairs={{0,4},{1,25},{2,26},{3,7},{4,0},{5,29},{6,30},{7,3},{8,12},{9,17},... | collective-permute-start | bytes 663560 | tf_op jit(solution)/shard_map/ppermute | solution.py:398
  42.1 2.8 %collective-permute-done.11.refs_10_ = f32[8,9216]{1,0:T(8,128)S(1)} collective-permute-done((f32[8,9216]{1,0:T(8,128)S(1)}, f32[8,9216]{1,0:T(8,128)S(1)}, u32[]{:S(2)}, u32[]{:S(2)}) %collective-permute-start.11) | collective-permute-done | bytes 294944 | tf_op jit(solution)/shard_map/ppermute | solution.py:327
  46.1 2.4 %collective-permute-start.13 = (f32[24,2304]{1,0:T(8,128)S(1)}, f32[24,2304]{1,0:T(8,128)S(1)}, u32[]{:S(2)}, u32[]{:S(2)}) collective-permute-start(f32[24,2304]{1,0:T(8,128)S(1)} %add.179), channel_id=1, source_target_pairs={{0,24},{1,5},{2,6},{3,27},{4,28},{5,1},{6,2},{7,31},{8,16},{9,13},... | collective-permute-start | bytes 663560 | tf_op jit(solution)/shard_map/ppermute | solution.py:398
  48.5 1.3 collective-permute-start.14
  49.8 4.6 %convert_divide_fusion.refs_2_ = f32[96,96,128]{2,1,0:T(8,128)} fusion(s32[]{:T(128)} %bitcast.15, s32[128]{0:T(128)S(1)} %iota_add_fusion, s32[96]{0:T(128)S(1)} %iota_add_fusion.1, pred[96]{0:T(512)(128)(4,1)S(1)} %iota_compare_fusion.1, pred[128]{0:T(512)(128)(4,1)S(1)} %iota_compare_fusion), kind=kLoop, calls=%fused_computation | loop fusion | flops 17694720 | bytes 4719716 | tf_op jit(solution)/shard_map/div | solution.py:356
  54.5 2.1 collective-permute-done.14.refs_12_
  56.6 2.6 %collective-permute-start.15 = (f32[24,2304]{1,0:T(8,128)S(1)}, f32[24,2304]{1,0:T(8,128)S(1)}, u32[]{:S(2)}, u32[]{:S(2)}) collective-permute-start(f32[24,2304]{1,0:T(8,128)S(1)} %get-tuple-element.178), channel_id=1, source_target_pairs={{0,8},{1,9},{2,26},{3,27},{4,12},{5,13},{6,30},{7,31},{8,0},{9,1},... | collective-permute-start | bytes 663560 | tf_op jit(solution)/shard_map/ppermute | solution.py:398
  59.2 2.1 %collective-permute-start.16 = (f32[8,9216]{1,0:T(8,128)S(1)}, f32[8,9216]{1,0:T(8,128)}, u32[]{:S(2)}, u32[]{:S(2)}) collective-permute-start(f32[8,9216]{1,0:T(8,128)S(1)} %slice_bitcast_fusion.4), channel_id=1, source_target_pairs={{0,1},{1,0},{2,3},{3,2},{4,5},{5,4},{6,7},{7,6},{8,9},{9,8},{10,11... | collective-permute-start | bytes 884744 | tf_op jit(solution)/shard_map/ppermute | solution.py:327
  61.3 6.3 %collective-permute-done.20 = f32[24,2304]{1,0:T(8,128)S(1)} collective-permute-done((f32[24,2304]{1,0:T(8,128)S(1)}, f32[24,2304]{1,0:T(8,128)S(1)}, u32[]{:S(2)}, u32[]{:S(2)}) %collective-permute-start.20) | collective-permute-done | bytes 221216 | tf_op jit(solution)/shard_map/ppermute | solution.py:327
  67.9 1.2 collective-permute-start.22
  69.1 4.9 %collective-permute-done.16.refs_8_ = f32[8,9216]{1,0:T(8,128)} collective-permute-done((f32[8,9216]{1,0:T(8,128)S(1)}, f32[8,9216]{1,0:T(8,128)}, u32[]{:S(2)}, u32[]{:S(2)}) %collective-permute-start.16) | collective-permute-done | bytes 294944 | tf_op jit(solution)/shard_map/ppermute | solution.py:327
  74.5 3.1 %collective-permute-done.21 = f32[24,2304]{1,0:T(8,128)S(1)} collective-permute-done((f32[24,2304]{1,0:T(8,128)S(1)}, f32[24,2304]{1,0:T(8,128)S(1)}, u32[]{:S(2)}, u32[]{:S(2)}) %collective-permute-start.21) | collective-permute-done | bytes 221216 | tf_op jit(solution)/shard_map/ppermute | solution.py:398
  77.6 2.6 %collective-permute-done.22.refs_9_ = f32[8,9216]{1,0:T(8,128)S(1)} collective-permute-done((f32[8,9216]{1,0:T(8,128)S(1)}, f32[8,9216]{1,0:T(8,128)S(1)}, u32[]{:S(2)}, u32[]{:S(2)}) %collective-permute-start.22) | collective-permute-done | bytes 294944 | tf_op jit(solution)/shard_map/ppermute | solution.py:327
  80.5 5.9 %collective-permute-done.18.refs_10_ = f32[8,9216]{1,0:T(8,128)S(1)} collective-permute-done((f32[8,9216]{1,0:T(8,128)S(1)}, f32[8,9216]{1,0:T(8,128)S(1)}, u32[]{:S(2)}, u32[]{:S(2)}) %collective-permute-start.18) | collective-permute-done | bytes 294944 | tf_op jit(solution)/shard_map/ppermute | solution.py:327
  87.4 2.2 %collective-permute-done.24.refs_11_ = f32[8,9216]{1,0:T(8,128)S(1)} collective-permute-done((f32[8,9216]{1,0:T(8,128)S(1)}, f32[8,9216]{1,0:T(8,128)S(1)}, u32[]{:S(2)}, u32[]{:S(2)}) %collective-permute-start.24) | collective-permute-done | bytes 294944 | tf_op jit(solution)/shard_map/ppermute | solution.py:327
  90.4 1.7 collective-permute-start.26
  93.0 15.4 %pair_terms.2 = (f32[24,9216]{1,0:T(8,128)}, f32[24,9216]{1,0:T(8,128)}, f32[24,9216]{1,0:T(8,128)}, f32[24,9216]{1,0:T(8,128)}, f32[48,9216]{1,0:T(8,128)}, /*i...) custom-call(s32[2]{0:T(128)} %pad_add_fusion.place_ref, ...), custom_call_target="tpu_custom_call" | custom-call | flops 10871635968 | bytes 20643840 | tf_op jit(solution)/shard_map/pair_terms/pallas_call | solution.py:286
  108.4 1.6 collective-permute-start.27
  110.8 16.2 %pair_terms.3 = (f32[24,9216]{1,0:T(8,128)}, f32[24,9216]{1,0:T(8,128)}, f32[24,9216]{1,0:T(8,128)}, f32[24,9216]{1,0:T(8,128)}, f32[48,9216]{1,0:T(8,128)}, /*i...) custom-call(s32[2]{0:T(128)} %pad_add_fusion.place_ref, ...), custom_call_target="tpu_custom_call" | custom-call | flops 10871635968 | bytes 24182784 | tf_op jit(solution)/shard_map/pair_terms/pallas_call | solution.py:286
  127.6 2.1 collective-permute-done.28
  130.4 1.5 collective-permute-start.29
  132.2 1.5 collective-permute-start.33
  133.7 6.1 %collective-permute-done.30 = f32[8,9216]{1,0:T(8,128)S(1)} collective-permute-done((f32[8,9216]{1,0:T(8,128)S(1)}, f32[8,9216]{1,0:T(8,128)S(1)}, u32[]{:S(2)}, u32[]{:S(2)}) %collective-permute-start.30) | collective-permute-done | bytes 294944 | tf_op jit(solution)/shard_map/ppermute | solution.py:327
  139.8 3.4 %collective-permute-done.29 = f32[24,4608]{1,0:T(8,128)S(1)} collective-permute-done((f32[24,4608]{1,0:T(8,128)S(1)}, f32[24,4608]{1,0:T(8,128)S(1)}, u32[]{:S(2)}, u32[]{:S(2)}) %collective-permute-start.29) | collective-permute-done | bytes 442400 | tf_op jit(solution)/shard_map/ppermute | solution.py:398
  143.4 1.7 collective-permute-start.35
  145.1 1.0 collective-permute-done.33
  146.3 1.5 collective-permute-start.37
  147.9 3.4 %collective-permute-done.34 = f32[24,2304]{1,0:T(8,128)S(1)} collective-permute-done((f32[24,2304]{1,0:T(8,128)S(1)}, f32[24,2304]{1,0:T(8,128)S(1)}, u32[]{:S(2)}, u32[]{:S(2)}) %collective-permute-start.34) | collective-permute-done | bytes 221216 | tf_op jit(solution)/shard_map/ppermute | solution.py:398
  151.2 2.2 %collective-permute-done.35 = f32[8,9216]{1,0:T(8,128)S(1)} collective-permute-done((f32[8,9216]{1,0:T(8,128)S(1)}, f32[8,9216]{1,0:T(8,128)S(1)}, u32[]{:S(2)}, u32[]{:S(2)}) %collective-permute-start.35) | collective-permute-done | bytes 294944 | tf_op jit(solution)/shard_map/ppermute | solution.py:327
  153.4 2.0 collective-permute-start.38
  155.6 4.1 %collective-permute-done.37 = f32[8,9216]{1,0:T(8,128)S(1)} collective-permute-done((f32[8,9216]{1,0:T(8,128)S(1)}, f32[8,9216]{1,0:T(8,128)S(1)}, u32[]{:S(2)}, u32[]{:S(2)}) %collective-permute-start.37) | collective-permute-done | bytes 294944 | tf_op jit(solution)/shard_map/ppermute | solution.py:327
  159.7 1.6 collective-permute-start.40
  161.3 1.7 collective-permute-start.41
  163.3 2.7 %collective-permute-done.39 = f32[8,9216]{1,0:T(8,128)S(1)} collective-permute-done((f32[8,9216]{1,0:T(8,128)S(1)}, f32[8,9216]{1,0:T(8,128)S(1)}, u32[]{:S(2)}, u32[]{:S(2)}) %collective-permute-start.39) | collective-permute-done | bytes 294944 | tf_op jit(solution)/shard_map/ppermute | solution.py:327
  166.1 4.5 %collective-permute-start.42 = (f32[24,2304]{1,0:T(8,128)S(1)}, f32[24,2304]{1,0:T(8,128)S(1)}, u32[]{:S(2)}, u32[]{:S(2)}) collective-permute-start(f32[24,2304]{1,0:T(8,128)S(1)} %add.191), channel_id=1, source_target_pairs={{0,8},{1,9},{2,26},{3,27},{4,12},{5,13},{6,30},{7,31},{8,0},{9,1},... | collective-permute-start | bytes 663560 | tf_op jit(solution)/shard_map/ppermute | solution.py:398
  170.6 2.0 collective-permute-start.43
  172.6 1.5 collective-permute-start.44
  174.2 7.8 %collective-permute-done.44 = f32[24,2304]{1,0:T(8,128)S(1)} collective-permute-done((f32[24,2304]{1,0:T(8,128)S(1)}, f32[24,2304]{1,0:T(8,128)S(1)}, u32[]{:S(2)}, u32[]{:S(2)}) %collective-permute-start.44) | collective-permute-done | bytes 221216 | tf_op jit(solution)/shard_map/ppermute | solution.py:327
  182.2 1.2 collective-permute-start.46
  184.4 2.7 %collective-permute-start.47 = (f32[24,4608]{1,0:T(8,128)S(1)}, f32[24,4608]{1,0:T(8,128)S(1)}, u32[]{:S(2)}, u32[]{:S(2)}) collective-permute-start(f32[24,4608]{1,0:T(8,128)S(1)} %pad_maximum_fusion.10), channel_id=1, source_target_pairs={{0,4},{1,5},{2,10},{3,11},{4,0},{5,1},{6,14},{7,15},{8,12},{9,13},... | collective-permute-start | bytes 1327112 | tf_op jit(solution)/shard_map/ppermute | solution.py:398
  187.2 2.7 %collective-permute-done.45 = f32[24,2304]{1,0:T(8,128)S(1)} collective-permute-done((f32[24,2304]{1,0:T(8,128)S(1)}, f32[24,2304]{1,0:T(8,128)S(1)}, u32[]{:S(2)}, u32[]{:S(2)}) %collective-permute-start.45) | collective-permute-done | bytes 221216 | tf_op jit(solution)/shard_map/ppermute | solution.py:398
  189.8 2.3 %collective-permute-done.46 = f32[8,9216]{1,0:T(8,128)S(1)} collective-permute-done((f32[8,9216]{1,0:T(8,128)S(1)}, f32[8,9216]{1,0:T(8,128)S(1)}, u32[]{:S(2)}, u32[]{:S(2)}) %collective-permute-start.46) | collective-permute-done | bytes 294944 | tf_op jit(solution)/shard_map/ppermute | solution.py:327
  192.3 1.3 collective-permute-start.50
  193.5 1.1 collective-permute-start.49
  194.7 2.8 %collective-permute-done.48 = f32[8,9216]{1,0:T(8,128)S(1)} collective-permute-done((f32[8,9216]{1,0:T(8,128)S(1)}, f32[8,9216]{1,0:T(8,128)S(1)}, u32[]{:S(2)}, u32[]{:S(2)}) %collective-permute-start.48) | collective-permute-done | bytes 294944 | tf_op jit(solution)/shard_map/ppermute | solution.py:327
  197.7 2.9 %collective-permute-done.50 = f32[8,9216]{1,0:T(8,128)S(1)} collective-permute-done((f32[8,9216]{1,0:T(8,128)S(1)}, f32[8,9216]{1,0:T(8,128)S(1)}, u32[]{:S(2)}, u32[]{:S(2)}) %collective-permute-start.50) | collective-permute-done | bytes 294944 | tf_op jit(solution)/shard_map/ppermute | solution.py:327
  200.6 1.2 collective-permute-done.49
  202.3 2.2 %pad_maximum_fusion = f32[2,48,9216]{2,1,0:T(8,128)} fusion(f32[1,48,9216]{2,1,0:T(8,128)S(1)} %add_bitcast_fusion, f32[1,48,9216]{2,1,0:T(8,128)S(1)} %add_bitcast_fusion.1), kind=kLoop, calls=%fused_computation.5 | loop fusion | flops 884736 | bytes 7077888 | tf_op jit(solution)/shard_map/stack | solution.py:526
  205.0 2.0 pad_maximum_fusion.1
  (182 shorter events, 17.3 us)
Async XLA Ops:
  4.8 2.8 %collective-permute-start = (f32[24,9216]{1,0:T(8,128)}, f32[24,9216]{1,0:T(8,128)}, u32[]{:S(2)}, u32[]{:S(2)}) collective-permute-start(f32[24,9216]{1,0:T(8,128)} %get-tuple-element.288), channel_id=1, source_target_pairs={{0,2},{1,3},{2,0},{3,1},{4,6},{5,7},{6,4},{7,5},{8,10},{9,11},{10,... | collective-permute-start | bytes 2654216 | tf_op jit(solution)/shard_map/ppermute | solution.py:398
  5.3 3.7 %collective-permute-start.7 = (f32[24,9216]{1,0:T(8,128)}, f32[24,9216]{1,0:T(8,128)}, u32[]{:S(2)}, u32[]{:S(2)}) collective-permute-start(f32[24,9216]{1,0:T(8,128)} %get-tuple-element.289), channel_id=1, source_target_pairs={{0,2},{1,3},{2,0},{3,1},{4,6},{5,7},{6,4},{7,5},{8,10},{9,11},{10,... | collective-permute-start | bytes 2654216 | tf_op jit(solution)/shard_map/ppermute | solution.py:398
  12.6 11.0 %collective-permute-start.2 = (f32[8,9216]{1,0:T(8,128)}, f32[8,9216]{1,0:T(8,128)}, u32[]{:S(2)}, u32[]{:S(2)}) collective-permute-start(f32[8,9216]{1,0:T(8,128)} %slice_bitcast_fusion.10), channel_id=1, source_target_pairs={{0,1},{1,0},{2,3},{3,2},{4,5},{5,4},{6,7},{7,6},{8,9},{9,8},{10,11... | collective-permute-start | bytes 884744 | tf_op jit(solution)/shard_map/ppermute | solution.py:327
  15.5 10.1 %collective-permute-start.1 = (f32[24,4608]{1,0:T(8,128)}, f32[24,4608]{1,0:T(8,128)}, u32[]{:S(2)}, u32[]{:S(2)}) collective-permute-start(f32[24,4608]{1,0:T(8,128)} %get-tuple-element.144), channel_id=1, source_target_pairs={{0,8},{1,5},{2,6},{3,11},{4,12},{5,1},{6,2},{7,15},{8,0},{9,13},{1... | collective-permute-start | bytes 1327112 | tf_op jit(solution)/shard_map/ppermute | solution.py:398
  19.7 11.8 %copy-start.4 = (f32[24,4608]{1,0:T(8,128)S(1)}, f32[24,4608]{1,0:T(8,128)}, u32[]{:S(2)}) copy-start(f32[24,4608]{1,0:T(8,128)} %get-tuple-element.157) | copy-start | bytes 1327108
  19.7 11.1 %collective-permute-start.9 = (f32[8,9216]{1,0:T(8,128)}, f32[8,9216]{1,0:T(8,128)S(1)}, u32[]{:S(2)}, u32[]{:S(2)}) collective-permute-start(f32[8,9216]{1,0:T(8,128)} %slice_bitcast_fusion.7), channel_id=1, source_target_pairs={{0,1},{1,0},{2,3},{3,2},{4,5},{5,4},{6,7},{7,6},{8,9},{9,8},{10,11... | collective-permute-start | bytes 884744 | tf_op jit(solution)/shard_map/ppermute | solution.py:327
  20.3 11.3 %collective-permute-start.8 = (f32[24,4608]{1,0:T(8,128)}, f32[24,4608]{1,0:T(8,128)S(1)}, u32[]{:S(2)}, u32[]{:S(2)}) collective-permute-start(f32[24,4608]{1,0:T(8,128)} %get-tuple-element.158), channel_id=1, source_target_pairs={{0,4},{1,9},{2,10},{3,7},{4,0},{5,13},{6,14},{7,3},{8,12},{9,1},{1... | collective-permute-start | bytes 1327112 | tf_op jit(solution)/shard_map/ppermute | solution.py:398
  26.8 11.3 %collective-permute-start.3 = (f32[24,2304]{1,0:T(8,128)S(1)}, f32[24,2304]{1,0:T(8,128)S(1)}, u32[]{:S(2)}, u32[]{:S(2)}) collective-permute-start(f32[24,2304]{1,0:T(8,128)S(1)} %get-tuple-element.148), channel_id=1, source_target_pairs={{0,24},{1,9},{2,10},{3,27},{4,28},{5,13},{6,14},{7,31},{8,16},{9,1... | collective-permute-start | bytes 663560 | tf_op jit(solution)/shard_map/ppermute | solution.py:398
  30.8 7.4 %collective-permute-start.4 = (f32[8,9216]{1,0:T(8,128)S(1)}, f32[8,9216]{1,0:T(8,128)S(1)}, u32[]{:S(2)}, u32[]{:S(2)}) collective-permute-start(f32[8,9216]{1,0:T(8,128)S(1)} %slice_bitcast_fusion.9), channel_id=1, source_target_pairs={{0,1},{1,0},{2,3},{3,2},{4,5},{5,4},{6,7},{7,6},{8,9},{9,8},{10,11... | collective-permute-start | bytes 884744 | tf_op jit(solution)/shard_map/ppermute | solution.py:327
  31.7 6.5 %collective-permute-start.12 = (f32[8,128]{1,0:T(8,128)S(1)}, f32[8,128]{1,0:T(8,128)S(1)}, u32[]{:S(2)}, u32[]{:S(2)}) collective-permute-start(f32[8,128]{1,0:T(8,128)S(1)} %broadcast_in_dim.43), channel_id=1, source_target_pairs={{0,1},{1,0},{2,3},{3,2},{4,5},{5,4},{6,7},{7,6},{8,9},{9,8},{10,11... | collective-permute-start | bytes 12296 | tf_op jit(solution)/shard_map/ppermute | solution.py:327
  33.7 8.4 %collective-permute-start.10 = (f32[24,2304]{1,0:T(8,128)S(1)}, f32[24,2304]{1,0:T(8,128)S(1)}, u32[]{:S(2)}, u32[]{:S(2)}) collective-permute-start(f32[24,2304]{1,0:T(8,128)S(1)} %get-tuple-element.166), channel_id=1, source_target_pairs={{0,8},{1,25},{2,26},{3,11},{4,12},{5,29},{6,30},{7,15},{8,0},{9,17... | collective-permute-start | bytes 663560 | tf_op jit(solution)/shard_map/ppermute | solution.py:398
  34.4 10.5 %collective-permute-start.11 = (f32[8,9216]{1,0:T(8,128)S(1)}, f32[8,9216]{1,0:T(8,128)S(1)}, u32[]{:S(2)}, u32[]{:S(2)}) collective-permute-start(f32[8,9216]{1,0:T(8,128)S(1)} %slice_bitcast_fusion.6), channel_id=1, source_target_pairs={{0,1},{1,0},{2,3},{3,2},{4,5},{5,4},{6,7},{7,6},{8,9},{9,8},{10,11... | collective-permute-start | bytes 884744 | tf_op jit(solution)/shard_map/ppermute | solution.py:327
  38.2 11.7 %copy-start.16 = (f32[8,9216]{1,0:T(8,128)}, f32[8,9216]{1,0:T(8,128)S(1)}, u32[]{:S(2)}) copy-start(f32[8,9216]{1,0:T(8,128)S(1)} %collective-permute-done.4.refs_11_) | copy-start | bytes 884740
  38.2 16.3 %collective-permute-start.5 = (f32[24,2304]{1,0:T(8,128)S(1)}, f32[24,2304]{1,0:T(8,128)S(1)}, u32[]{:S(2)}, u32[]{:S(2)}) collective-permute-start(f32[24,2304]{1,0:T(8,128)S(1)} %add.167), channel_id=1, source_target_pairs={{0,4},{1,25},{2,26},{3,7},{4,0},{5,29},{6,30},{7,3},{8,12},{9,17},... | collective-permute-start | bytes 663560 | tf_op jit(solution)/shard_map/ppermute | solution.py:398
  41.6 12.9 %collective-permute-start.6 = (f32[8,9216]{1,0:T(8,128)S(1)}, f32[8,9216]{1,0:T(8,128)S(1)}, u32[]{:S(2)}, u32[]{:S(2)}) collective-permute-start(f32[8,9216]{1,0:T(8,128)S(1)} %slice_bitcast_fusion.8), channel_id=1, source_target_pairs={{0,1},{1,0},{2,3},{3,2},{4,5},{5,4},{6,7},{7,6},{8,9},{9,8},{10,11... | collective-permute-start | bytes 884744 | tf_op jit(solution)/shard_map/ppermute | solution.py:327
  46.1 8.4 %collective-permute-start.13 = (f32[24,2304]{1,0:T(8,128)S(1)}, f32[24,2304]{1,0:T(8,128)S(1)}, u32[]{:S(2)}, u32[]{:S(2)}) collective-permute-start(f32[24,2304]{1,0:T(8,128)S(1)} %add.179), channel_id=1, source_target_pairs={{0,24},{1,5},{2,6},{3,27},{4,28},{5,1},{6,2},{7,31},{8,16},{9,13},... | collective-permute-start | bytes 663560 | tf_op jit(solution)/shard_map/ppermute | solution.py:398
  48.5 8.0 %collective-permute-start.14 = (f32[8,9216]{1,0:T(8,128)S(1)}, f32[8,9216]{1,0:T(8,128)S(1)}, u32[]{:S(2)}, u32[]{:S(2)}) collective-permute-start(f32[8,9216]{1,0:T(8,128)S(1)} %slice_bitcast_fusion.5), channel_id=1, source_target_pairs={{0,1},{1,0},{2,3},{3,2},{4,5},{5,4},{6,7},{7,6},{8,9},{9,8},{10,11... | collective-permute-start | bytes 884744 | tf_op jit(solution)/shard_map/ppermute | solution.py:327
  54.5 19.6 %copy-start.20 = (f32[8,9216]{1,0:T(8,128)}, f32[8,9216]{1,0:T(8,128)S(1)}, u32[]{:S(2)}) copy-start(f32[8,9216]{1,0:T(8,128)S(1)} %collective-permute-done.6.refs_13_) | copy-start | bytes 884740
  56.6 17.5 %copy-start.23 = (f32[8,9216]{1,0:T(8,128)}, f32[8,9216]{1,0:T(8,128)S(1)}, u32[]{:S(2)}) copy-start(f32[8,9216]{1,0:T(8,128)S(1)} %collective-permute-done.14.refs_12_) | copy-start | bytes 884740
  56.6 12.5 %collective-permute-start.15 = (f32[24,2304]{1,0:T(8,128)S(1)}, f32[24,2304]{1,0:T(8,128)S(1)}, u32[]{:S(2)}, u32[]{:S(2)}) collective-permute-start(f32[24,2304]{1,0:T(8,128)S(1)} %get-tuple-element.178), channel_id=1, source_target_pairs={{0,8},{1,9},{2,26},{3,27},{4,12},{5,13},{6,30},{7,31},{8,0},{9,1},... | collective-permute-start | bytes 663560 | tf_op jit(solution)/shard_map/ppermute | solution.py:398
  59.2 8.4 %collective-permute-start.20 = (f32[24,2304]{1,0:T(8,128)S(1)}, f32[24,2304]{1,0:T(8,128)S(1)}, u32[]{:S(2)}, u32[]{:S(2)}) collective-permute-start(f32[24,2304]{1,0:T(8,128)S(1)} %get-tuple-element.304), channel_id=1, source_target_pairs={{0,1},{1,0},{2,3},{3,2},{4,5},{5,4},{6,7},{7,6},{8,9},{9,8},{10,11... | collective-permute-start | bytes 663560 | tf_op jit(solution)/shard_map/ppermute | solution.py:327
  59.2 14.8 %collective-permute-start.16 = (f32[8,9216]{1,0:T(8,128)S(1)}, f32[8,9216]{1,0:T(8,128)}, u32[]{:S(2)}, u32[]{:S(2)}) collective-permute-start(f32[8,9216]{1,0:T(8,128)S(1)} %slice_bitcast_fusion.4), channel_id=1, source_target_pairs={{0,1},{1,0},{2,3},{3,2},{4,5},{5,4},{6,7},{7,6},{8,9},{9,8},{10,11... | collective-permute-start | bytes 884744 | tf_op jit(solution)/shard_map/ppermute | solution.py:327
  67.6 10.1 %collective-permute-start.21 = (f32[24,2304]{1,0:T(8,128)S(1)}, f32[24,2304]{1,0:T(8,128)S(1)}, u32[]{:S(2)}, u32[]{:S(2)}) collective-permute-start(f32[24,2304]{1,0:T(8,128)S(1)} %collective-permute-done.20), channel_id=1, source_target_pairs={{0,24},{1,25},{2,10},{3,11},{4,28},{5,29},{6,14},{7,15},{8,16},{9,... | collective-permute-start | bytes 663560 | tf_op jit(solution)/shard_map/ppermute | solution.py:398
  67.9 12.3 %collective-permute-start.22 = (f32[8,9216]{1,0:T(8,128)S(1)}, f32[8,9216]{1,0:T(8,128)S(1)}, u32[]{:S(2)}, u32[]{:S(2)}) collective-permute-start(f32[8,9216]{1,0:T(8,128)S(1)} %slice_bitcast_fusion.2), channel_id=1, source_target_pairs={{0,1},{1,0},{2,3},{3,2},{4,5},{5,4},{6,7},{7,6},{8,9},{9,8},{10,11... | collective-permute-start | bytes 884744 | tf_op jit(solution)/shard_map/ppermute | solution.py:327
  74.1 12.3 %collective-permute-start.18 = (f32[8,9216]{1,0:T(8,128)S(1)}, f32[8,9216]{1,0:T(8,128)S(1)}, u32[]{:S(2)}, u32[]{:S(2)}) collective-permute-start(f32[8,9216]{1,0:T(8,128)S(1)} %slice_bitcast_fusion.3), channel_id=1, source_target_pairs={{0,1},{1,0},{2,3},{3,2},{4,5},{5,4},{6,7},{7,6},{8,9},{9,8},{10,11... | collective-permute-start | bytes 884744 | tf_op jit(solution)/shard_map/ppermute | solution.py:327
  74.2 13.0 %collective-permute-start.17 = (f32[24,4608]{1,0:T(8,128)S(1)}, f32[24,4608]{1,0:T(8,128)S(1)}, u32[]{:S(2)}, u32[]{:S(2)}) collective-permute-start(f32[24,4608]{1,0:T(8,128)S(1)} %pad_maximum_fusion.8), channel_id=1, source_target_pairs={{0,4},{1,5},{2,10},{3,11},{4,0},{5,1},{6,14},{7,15},{8,12},{9,13},... | collective-permute-start | bytes 1327112 | tf_op jit(solution)/shard_map/ppermute | solution.py:398
  80.3 9.3 %collective-permute-start.24 = (f32[8,9216]{1,0:T(8,128)S(1)}, f32[8,9216]{1,0:T(8,128)S(1)}, u32[]{:S(2)}, u32[]{:S(2)}) collective-permute-start(f32[8,9216]{1,0:T(8,128)S(1)} %slice_bitcast_fusion.1), channel_id=1, source_target_pairs={{0,1},{1,0},{2,3},{3,2},{4,5},{5,4},{6,7},{7,6},{8,9},{9,8},{10,11... | collective-permute-start | bytes 884744 | tf_op jit(solution)/shard_map/ppermute | solution.py:327
  80.4 9.2 %collective-permute-start.23 = (f32[24,4608]{1,0:T(8,128)S(1)}, f32[24,4608]{1,0:T(8,128)S(1)}, u32[]{:S(2)}, u32[]{:S(2)}) collective-permute-start(f32[24,4608]{1,0:T(8,128)S(1)} %pad_maximum_fusion.9), channel_id=1, source_target_pairs={{0,8},{1,9},{2,6},{3,7},{4,12},{5,13},{6,2},{7,3},{8,0},{9,1},{10,... | collective-permute-start | bytes 1327112 | tf_op jit(solution)/shard_map/ppermute | solution.py:398
  87.3 4.7 %collective-permute-start.19 = (f32[24,9216]{1,0:T(8,128)S(1)}, f32[24,9216]{1,0:T(8,128)S(1)}, u32[]{:S(2)}, u32[]{:S(2)}) collective-permute-start(f32[24,9216]{1,0:T(8,128)S(1)} %pad_maximum_fusion.4.refs_3_), channel_id=1, source_target_pairs={{0,2},{1,3},{2,0},{3,1},{4,6},{5,7},{6,4},{7,5},{8,10},{9,11},{10,... | collective-permute-start | bytes 2654216 | tf_op jit(solution)/shard_map/ppermute | solution.py:398
  90.3 2.7 %collective-permute-start.25 = (f32[24,9216]{1,0:T(8,128)S(1)}, f32[24,9216]{1,0:T(8,128)}, u32[]{:S(2)}, u32[]{:S(2)}) collective-permute-start(f32[24,9216]{1,0:T(8,128)S(1)} %pad_maximum_fusion.5.refs_5_), channel_id=1, source_target_pairs={{0,2},{1,3},{2,0},{3,1},{4,6},{5,7},{6,4},{7,5},{8,10},{9,11},{10,... | collective-permute-start | bytes 2654216 | tf_op jit(solution)/shard_map/ppermute | solution.py:398
  90.4 19.6 %collective-permute-start.26 = (f32[16,9216]{1,0:T(8,128)S(1)}, f32[16,9216]{1,0:T(8,128)S(1)}, u32[]{:S(2)}, u32[]{:S(2)}) collective-permute-start(f32[16,9216]{1,0:T(8,128)S(1)} %slice_bitcast_fusion), channel_id=1, source_target_pairs={{0,1},{1,0},{2,3},{3,2},{4,5},{5,4},{6,7},{7,6},{8,9},{9,8},{10,11... | collective-permute-start | bytes 1769480 | tf_op jit(solution)/shard_map/ppermute | solution.py:327
  108.4 18.6 %collective-permute-start.27 = (f32[16,9216]{1,0:T(8,128)}, f32[16,9216]{1,0:T(8,128)S(1)}, u32[]{:S(2)}, u32[]{:S(2)}) collective-permute-start(f32[16,9216]{1,0:T(8,128)} %get-tuple-element.217), channel_id=1, source_target_pairs={{0,1},{1,0},{2,3},{3,2},{4,5},{5,4},{6,7},{7,6},{8,9},{9,8},{10,11... | collective-permute-start | bytes 1769480 | tf_op jit(solution)/shard_map/ppermute | solution.py:327
  127.0 2.7 %collective-permute-start.28 = (f32[24,9216]{1,0:T(8,128)}, f32[24,9216]{1,0:T(8,128)S(1)}, u32[]{:S(2)}, u32[]{:S(2)}) collective-permute-start(f32[24,9216]{1,0:T(8,128)} %get-tuple-element.220), channel_id=1, source_target_pairs={{0,2},{1,3},{2,0},{3,1},{4,6},{5,7},{6,4},{7,5},{8,10},{9,11},{10,... | collective-permute-start | bytes 2654216 | tf_op jit(solution)/shard_map/ppermute | solution.py:398
  127.1 4.9 %collective-permute-start.31 = (f32[24,9216]{1,0:T(8,128)}, f32[24,9216]{1,0:T(8,128)S(1)}, u32[]{:S(2)}, u32[]{:S(2)}) collective-permute-start(f32[24,9216]{1,0:T(8,128)} %get-tuple-element.226), channel_id=1, source_target_pairs={{0,2},{1,3},{2,0},{3,1},{4,6},{5,7},{6,4},{7,5},{8,10},{9,11},{10,... | collective-permute-start | bytes 2654216 | tf_op jit(solution)/shard_map/ppermute | solution.py:398
  129.9 9.9 %collective-permute-start.30 = (f32[8,9216]{1,0:T(8,128)S(1)}, f32[8,9216]{1,0:T(8,128)S(1)}, u32[]{:S(2)}, u32[]{:S(2)}) collective-permute-start(f32[8,9216]{1,0:T(8,128)S(1)} %copy-done.28), channel_id=1, source_target_pairs={{0,1},{1,0},{2,3},{3,2},{4,5},{5,4},{6,7},{7,6},{8,9},{9,8},{10,11... | collective-permute-start | bytes 884744 | tf_op jit(solution)/shard_map/ppermute | solution.py:327
  130.4 12.7 %collective-permute-start.29 = (f32[24,4608]{1,0:T(8,128)S(1)}, f32[24,4608]{1,0:T(8,128)S(1)}, u32[]{:S(2)}, u32[]{:S(2)}) collective-permute-start(f32[24,4608]{1,0:T(8,128)S(1)} %get-tuple-element.222), channel_id=1, source_target_pairs={{0,4},{1,5},{2,10},{3,11},{4,0},{5,1},{6,14},{7,15},{8,12},{9,13},... | collective-permute-start | bytes 1327112 | tf_op jit(solution)/shard_map/ppermute | solution.py:398
  132.1 11.3 %copy-start.24 = (f32[8,9216]{1,0:T(8,128)S(1)}, f32[8,9216]{1,0:T(8,128)}, u32[]{:S(2)}) copy-start(f32[8,9216]{1,0:T(8,128)} %get-tuple-element.233) | copy-start | bytes 884740
  132.2 13.9 %collective-permute-start.33 = (f32[8,9216]{1,0:T(8,128)S(1)}, f32[8,9216]{1,0:T(8,128)S(1)}, u32[]{:S(2)}, u32[]{:S(2)}) collective-permute-start(f32[8,9216]{1,0:T(8,128)S(1)} %copy-done.26), channel_id=1, source_target_pairs={{0,1},{1,0},{2,3},{3,2},{4,5},{5,4},{6,7},{7,6},{8,9},{9,8},{10,11... | collective-permute-start | bytes 884744 | tf_op jit(solution)/shard_map/ppermute | solution.py:327
  133.7 12.4 %collective-permute-start.32 = (f32[24,4608]{1,0:T(8,128)S(1)}, f32[24,4608]{1,0:T(8,128)S(1)}, u32[]{:S(2)}, u32[]{:S(2)}) collective-permute-start(f32[24,4608]{1,0:T(8,128)S(1)} %get-tuple-element.228), channel_id=1, source_target_pairs={{0,8},{1,9},{2,6},{3,7},{4,12},{5,13},{6,2},{7,3},{8,0},{9,1},{10,... | collective-permute-start | bytes 1327112 | tf_op jit(solution)/shard_map/ppermute | solution.py:398
  143.3 8.0 %collective-permute-start.34 = (f32[24,2304]{1,0:T(8,128)S(1)}, f32[24,2304]{1,0:T(8,128)S(1)}, u32[]{:S(2)}, u32[]{:S(2)}) collective-permute-start(f32[24,2304]{1,0:T(8,128)S(1)} %get-tuple-element.234), channel_id=1, source_target_pairs={{0,8},{1,9},{2,26},{3,27},{4,12},{5,13},{6,30},{7,31},{8,0},{9,1},... | collective-permute-start | bytes 663560 | tf_op jit(solution)/shard_map/ppermute | solution.py:398
  143.4 12.1 %copy-start.21 = (f32[8,9216]{1,0:T(8,128)S(1)}, f32[8,9216]{1,0:T(8,128)}, u32[]{:S(2)}) copy-start(f32[8,9216]{1,0:T(8,128)} %get-tuple-element.246) | copy-start | bytes 884740
  143.4 10.0 %collective-permute-start.35 = (f32[8,9216]{1,0:T(8,128)S(1)}, f32[8,9216]{1,0:T(8,128)S(1)}, u32[]{:S(2)}, u32[]{:S(2)}) collective-permute-start(f32[8,9216]{1,0:T(8,128)S(1)} %copy-done.24), channel_id=1, source_target_pairs={{0,1},{1,0},{2,3},{3,2},{4,5},{5,4},{6,7},{7,6},{8,9},{9,8},{10,11... | collective-permute-start | bytes 884744 | tf_op jit(solution)/shard_map/ppermute | solution.py:327
  146.2 15.1 %copy-start.19 = (f32[8,9216]{1,0:T(8,128)S(1)}, f32[8,9216]{1,0:T(8,128)}, u32[]{:S(2)}) copy-start(f32[8,9216]{1,0:T(8,128)} %get-tuple-element.252) | copy-start | bytes 884740
  146.2 9.4 %collective-permute-start.36 = (f32[24,2304]{1,0:T(8,128)S(1)}, f32[24,2304]{1,0:T(8,128)S(1)}, u32[]{:S(2)}, u32[]{:S(2)}) collective-permute-start(f32[24,2304]{1,0:T(8,128)S(1)} %get-tuple-element.240), channel_id=1, source_target_pairs={{0,24},{1,25},{2,10},{3,11},{4,28},{5,29},{6,14},{7,15},{8,16},{9,... | collective-permute-start | bytes 663560 | tf_op jit(solution)/shard_map/ppermute | solution.py:398
  146.3 16.7 %copy-start.3 = (f32[48,9216]{1,0:T(8,128)S(1)}, f32[48,9216]{1,0:T(8,128)}, u32[]{:S(2)}) copy-start(f32[48,9216]{1,0:T(8,128)} %get-tuple-element.203) | copy-start | bytes 5308420
  146.3 13.4 %collective-permute-start.37 = (f32[8,9216]{1,0:T(8,128)S(1)}, f32[8,9216]{1,0:T(8,128)S(1)}, u32[]{:S(2)}, u32[]{:S(2)}) collective-permute-start(f32[8,9216]{1,0:T(8,128)S(1)} %copy-done.22), channel_id=1, source_target_pairs={{0,1},{1,0},{2,3},{3,2},{4,5},{5,4},{6,7},{7,6},{8,9},{9,8},{10,11... | collective-permute-start | bytes 884744 | tf_op jit(solution)/shard_map/ppermute | solution.py:327
  153.4 9.9 %collective-permute-start.38 = (f32[24,2304]{1,0:T(8,128)S(1)}, f32[24,2304]{1,0:T(8,128)S(1)}, u32[]{:S(2)}, u32[]{:S(2)}) collective-permute-start(f32[24,2304]{1,0:T(8,128)S(1)} %add.189), channel_id=1, source_target_pairs={{0,24},{1,25},{2,6},{3,7},{4,28},{5,29},{6,2},{7,3},{8,16},{9,17},... | collective-permute-start | bytes 663560 | tf_op jit(solution)/shard_map/ppermute | solution.py:398
  155.4 10.6 %collective-permute-start.39 = (f32[8,9216]{1,0:T(8,128)S(1)}, f32[8,9216]{1,0:T(8,128)S(1)}, u32[]{:S(2)}, u32[]{:S(2)}) collective-permute-start(f32[8,9216]{1,0:T(8,128)S(1)} %copy-done.21), channel_id=1, source_target_pairs={{0,1},{1,0},{2,3},{3,2},{4,5},{5,4},{6,7},{7,6},{8,9},{9,8},{10,11... | collective-permute-start | bytes 884744 | tf_op jit(solution)/shard_map/ppermute | solution.py:327
  159.7 12.9 %collective-permute-start.40 = (f32[24,2304]{1,0:T(8,128)S(1)}, f32[24,2304]{1,0:T(8,128)S(1)}, u32[]{:S(2)}, u32[]{:S(2)}) collective-permute-start(f32[24,2304]{1,0:T(8,128)S(1)} %add.190), channel_id=1, source_target_pairs={{0,4},{1,5},{2,26},{3,27},{4,0},{5,1},{6,30},{7,31},{8,12},{9,13},... | collective-permute-start | bytes 663560 | tf_op jit(solution)/shard_map/ppermute | solution.py:398
  161.3 11.3 %collective-permute-start.41 = (f32[8,9216]{1,0:T(8,128)S(1)}, f32[8,9216]{1,0:T(8,128)S(1)}, u32[]{:S(2)}, u32[]{:S(2)}) collective-permute-start(f32[8,9216]{1,0:T(8,128)S(1)} %copy-done.19), channel_id=1, source_target_pairs={{0,1},{1,0},{2,3},{3,2},{4,5},{5,4},{6,7},{7,6},{8,9},{9,8},{10,11... | collective-permute-start | bytes 884744 | tf_op jit(solution)/shard_map/ppermute | solution.py:327
  163.3 18.9 %copy-start.15 = (f32[8,9216]{1,0:T(8,128)S(1)}, f32[8,9216]{1,0:T(8,128)}, u32[]{:S(2)}) copy-start(f32[8,9216]{1,0:T(8,128)} %get-tuple-element.264) | copy-start | bytes 884740
  166.1 17.4 %collective-permute-start.42 = (f32[24,2304]{1,0:T(8,128)S(1)}, f32[24,2304]{1,0:T(8,128)S(1)}, u32[]{:S(2)}, u32[]{:S(2)}) collective-permute-start(f32[24,2304]{1,0:T(8,128)S(1)} %add.191), channel_id=1, source_target_pairs={{0,8},{1,9},{2,26},{3,27},{4,12},{5,13},{6,30},{7,31},{8,0},{9,1},... | collective-permute-start | bytes 663560 | tf_op jit(solution)/shard_map/ppermute | solution.py:398
  170.6 13.0 %copy-start.13 = (f32[8,9216]{1,0:T(8,128)S(1)}, f32[8,9216]{1,0:T(8,128)}, u32[]{:S(2)}) copy-start(f32[8,9216]{1,0:T(8,128)} %get-tuple-element.270) | copy-start | bytes 884740
  170.6 12.9 %collective-permute-start.43 = (f32[8,9216]{1,0:T(8,128)S(1)}, f32[8,9216]{1,0:T(8,128)S(1)}, u32[]{:S(2)}, u32[]{:S(2)}) collective-permute-start(f32[8,9216]{1,0:T(8,128)S(1)} %copy-done.17), channel_id=1, source_target_pairs={{0,1},{1,0},{2,3},{3,2},{4,5},{5,4},{6,7},{7,6},{8,9},{9,8},{10,11... | collective-permute-start | bytes 884744 | tf_op jit(solution)/shard_map/ppermute | solution.py:327
  172.6 9.3 %collective-permute-start.44 = (f32[24,2304]{1,0:T(8,128)S(1)}, f32[24,2304]{1,0:T(8,128)S(1)}, u32[]{:S(2)}, u32[]{:S(2)}) collective-permute-start(f32[24,2304]{1,0:T(8,128)S(1)} %add.192), channel_id=1, source_target_pairs={{0,1},{1,0},{2,3},{3,2},{4,5},{5,4},{6,7},{7,6},{8,9},{9,8},{10,11... | collective-permute-start | bytes 663560 | tf_op jit(solution)/shard_map/ppermute | solution.py:327
  181.9 7.9 %collective-permute-start.45 = (f32[24,2304]{1,0:T(8,128)S(1)}, f32[24,2304]{1,0:T(8,128)S(1)}, u32[]{:S(2)}, u32[]{:S(2)}) collective-permute-start(f32[24,2304]{1,0:T(8,128)S(1)} %collective-permute-done.44), channel_id=1, source_target_pairs={{0,24},{1,25},{2,10},{3,11},{4,28},{5,29},{6,14},{7,15},{8,16},{9,... | collective-permute-start | bytes 663560 | tf_op jit(solution)/shard_map/ppermute | solution.py:398
  182.2 9.9 %collective-permute-start.46 = (f32[8,9216]{1,0:T(8,128)S(1)}, f32[8,9216]{1,0:T(8,128)S(1)}, u32[]{:S(2)}, u32[]{:S(2)}) collective-permute-start(f32[8,9216]{1,0:T(8,128)S(1)} %copy-done.15), channel_id=1, source_target_pairs={{0,1},{1,0},{2,3},{3,2},{4,5},{5,4},{6,7},{7,6},{8,9},{9,8},{10,11... | collective-permute-start | bytes 884744 | tf_op jit(solution)/shard_map/ppermute | solution.py:327
  183.5 8.8 %copy-start.12 = (f32[8,9216]{1,0:T(8,128)S(1)}, f32[8,9216]{1,0:T(8,128)}, u32[]{:S(2)}) copy-start(f32[8,9216]{1,0:T(8,128)} %get-tuple-element.276) | copy-start | bytes 884740
  183.5 13.9 %collective-permute-start.48 = (f32[8,9216]{1,0:T(8,128)S(1)}, f32[8,9216]{1,0:T(8,128)S(1)}, u32[]{:S(2)}, u32[]{:S(2)}) collective-permute-start(f32[8,9216]{1,0:T(8,128)S(1)} %copy-done.13), channel_id=1, source_target_pairs={{0,1},{1,0},{2,3},{3,2},{4,5},{5,4},{6,7},{7,6},{8,9},{9,8},{10,11... | collective-permute-start | bytes 884744 | tf_op jit(solution)/shard_map/ppermute | solution.py:327
  184.4 13.0 %collective-permute-start.47 = (f32[24,4608]{1,0:T(8,128)S(1)}, f32[24,4608]{1,0:T(8,128)S(1)}, u32[]{:S(2)}, u32[]{:S(2)}) collective-permute-start(f32[24,4608]{1,0:T(8,128)S(1)} %pad_maximum_fusion.10), channel_id=1, source_target_pairs={{0,4},{1,5},{2,10},{3,11},{4,0},{5,1},{6,14},{7,15},{8,12},{9,13},... | collective-permute-start | bytes 1327112 | tf_op jit(solution)/shard_map/ppermute | solution.py:398
  192.3 8.3 %collective-permute-start.50 = (f32[8,9216]{1,0:T(8,128)S(1)}, f32[8,9216]{1,0:T(8,128)S(1)}, u32[]{:S(2)}, u32[]{:S(2)}) collective-permute-start(f32[8,9216]{1,0:T(8,128)S(1)} %copy-done.12), channel_id=1, source_target_pairs={{0,1},{1,0},{2,3},{3,2},{4,5},{5,4},{6,7},{7,6},{8,9},{9,8},{10,11... | collective-permute-start | bytes 884744 | tf_op jit(solution)/shard_map/ppermute | solution.py:327
  193.5 8.3 %collective-permute-start.49 = (f32[24,4608]{1,0:T(8,128)S(1)}, f32[24,4608]{1,0:T(8,128)S(1)}, u32[]{:S(2)}, u32[]{:S(2)}) collective-permute-start(f32[24,4608]{1,0:T(8,128)S(1)} %pad_maximum_fusion.11), channel_id=1, source_target_pairs={{0,8},{1,9},{2,6},{3,7},{4,12},{5,13},{6,2},{7,3},{8,0},{9,1},{10,... | collective-permute-start | bytes 1327112 | tf_op jit(solution)/shard_map/ppermute | solution.py:398
  197.6 6.9 %collective-permute-start.52 = (f32[24,9216]{1,0:T(8,128)S(1)}, f32[24,9216]{1,0:T(8,128)S(1)}, u32[]{:S(2)}, u32[]{:S(2)}) collective-permute-start(f32[24,9216]{1,0:T(8,128)S(1)} %pad_maximum_fusion.7), channel_id=1, source_target_pairs={{0,2},{1,3},{2,0},{3,1},{4,6},{5,7},{6,4},{7,5},{8,10},{9,11},{10,... | collective-permute-start | bytes 2654216 | tf_op jit(solution)/shard_map/ppermute | solution.py:398
  202.0 2.6 %collective-permute-start.51 = (f32[24,9216]{1,0:T(8,128)S(1)}, f32[24,9216]{1,0:T(8,128)S(1)}, u32[]{:S(2)}, u32[]{:S(2)}) collective-permute-start(f32[24,9216]{1,0:T(8,128)S(1)} %pad_maximum_fusion.6), channel_id=1, source_target_pairs={{0,2},{1,3},{2,0},{3,1},{4,6},{5,7},{6,4},{7,5},{8,10},{9,11},{10,... | collective-permute-start | bytes 2654216 | tf_op jit(solution)/shard_map/ppermute | solution.py:398
  (19 other events, 68.7 us)

commit v4 on v3

--- a/solution.py
+++ b/solution.py
@@ -272,7 +272,7 @@
     count = 4 * quarter
     unit = math.lcm(count, LANES)
     batch = divisor(flat_cells // unit, 12)
-    planes = divisor(count, 16)
+    planes = divisor(count, 32)
     steps = flat_cells // (batch * unit)
     operands = [coulomb, *block, *arrays, *totals]
     vmem = pl.BlockSpec(memory_space=pltpu.VMEM)
@@ -302,7 +302,7 @@
             pltpu.SemaphoreType.DMA((6 + len(out_specs), steps)),
             pltpu.SemaphoreType.DMA,
         ],
-        compiler_params=pltpu.CompilerParams(vmem_limit_bytes=60 * 2**20),
+        compiler_params=pltpu.CompilerParams(vmem_limit_bytes=52 * 2**20),
         cost_estimate=pl.CostEstimate(
             flops=6 * flat_cells * count * 16 * LANES, bytes_accessed=moved, transcendentals=0
         ),

time: 208 us -> 211 us (1.014)
  starting transfers between devices: 62.2 us -> 65.3 us
    ppermute x25, starting transfers between devices: 30.8 us -> 33.3 us  [across(): return lax.ppermute(value, 'fft', [(0, 1), (1, 0)])]
  transfers between devices with their start and end apart: 53 -> 53, of which waited for: 27 -> 28; matrix products, arithmetic and copies ran while one was open for 7% -> 7% of each run, Pallas kernels for 15% -> 15%
where the time goes in v4:
time: 211 us; the launch traced here: 210 us
  waiting for transfers between devices  81.6 us (39%)
  starting transfers between devices  65.3 us (31%)
  Pallas kernels  32.2 us (15%)
  other arithmetic  19.9 us (9%)
  local copies, waits for them, and re-layouts  7.88 us (4%)
  between operations  3.4 us (2%)
    ppermute x25, waiting for transfers between devices, across(): return lax.ppermute(value, 'fft', [(0, 1), (1, 0)])  61.5 us
    ppermute x25, starting transfers between devices, across(): return lax.ppermute(value, 'fft', [(0, 1), (1, 0)])  33.3 us
    pallas_call x2, Pallas kernels, pair_terms(): pl.pallas_call(functools.partial(pair_kernel, count, unit, batch, planes,...  32.2 us
    ppermute x28, starting transfers between devices, swap(): arrived = lax.ppermute(value, ('band', 'fft'), pairs)  32 us
    ppermute x28, waiting for transfers between devices, swap(): arrived = lax.ppermute(value, ('band', 'fft'), pairs)  20.2 us
    div x1, other arithmetic, coulomb_table(): return factor * weights / jnp.maximum(squared, 1).astype(jnp.float32)  4.63 us
  transfers between devices with their start and end apart: 53, of which 28 were waited for; matrix products, arithmetic and copies ran while one was open for 7% of the time, Pallas kernels for 15%

profile of v4, /device:TPU:0, one launch (start us, length us, event | category | flops | bytes accessed | tf_op | source)
XLA Modules:
  0.0 210.3 jit_solution(2474266352632481171)
XLA Ops:
  1.3 3.5 %select_bitcast_fusion.5 = (f32[24,9216]{1,0:T(8,128)}, f32[24,9216]{1,0:T(8,128)}) fusion(f32[2,48,9216]{2,1,0:T(8,128)} %refs_7_.3, pred[]{:T(512)S(6)} %eq.88, pred[]{:T(512)S(6)} %eq.87), kind=kLoop, calls=%fused_computation.25 | loop fusion | flops 884736 | bytes 5308418 | tf_op jit(solution)/shard_map/jit(_where)/select_n | solution.py:493
  7.7 1.3 collective-permute-done.7
  8.9 1.7 bitcast_add_fusion.1
  10.6 1.3 slice_select_fusion.4
  12.7 2.9 %collective-permute-start.2 = (f32[8,9216]{1,0:T(8,128)}, f32[8,9216]{1,0:T(8,128)S(1)}, u32[]{:S(2)}, u32[]{:S(2)}) collective-permute-start(f32[8,9216]{1,0:T(8,128)} %slice_bitcast_fusion.10), channel_id=1, source_target_pairs={{0,1},{1,0},{2,3},{3,2},{4,5},{5,4},{6,7},{7,6},{8,9},{9,8},{10,11... | collective-permute-start | bytes 884744 | tf_op jit(solution)/shard_map/ppermute | solution.py:327
  15.5 1.6 collective-permute-start.1
  17.1 1.0 slice_bitcast_fusion.7
  18.1 1.3 select_reduce_fusion
  20.7 1.1 collective-permute-start.8
  21.9 1.7 collective-permute-done.2.refs_9_
  23.5 1.8 collective-permute-done.1
  25.4 3.9 %collective-permute-start.3 = (f32[24,2304]{1,0:T(8,128)S(1)}, f32[24,2304]{1,0:T(8,128)S(1)}, u32[]{:S(2)}, u32[]{:S(2)}) collective-permute-start(f32[24,2304]{1,0:T(8,128)S(1)} %get-tuple-element.148), channel_id=1, source_target_pairs={{0,24},{1,9},{2,10},{3,27},{4,28},{5,13},{6,14},{7,31},{8,16},{9,1... | collective-permute-start | bytes 663560 | tf_op jit(solution)/shard_map/ppermute | solution.py:398
  30.5 2.1 collective-permute-start.12
  32.6 1.0 collective-permute-start.10
  33.7 2.6 %collective-permute-start.11 = (f32[8,9216]{1,0:T(8,128)S(1)}, f32[8,9216]{1,0:T(8,128)S(1)}, u32[]{:S(2)}, u32[]{:S(2)}) collective-permute-start(f32[8,9216]{1,0:T(8,128)S(1)} %slice_bitcast_fusion.6), channel_id=1, source_target_pairs={{0,1},{1,0},{2,3},{3,2},{4,5},{5,4},{6,7},{7,6},{8,9},{9,8},{10,11... | collective-permute-start | bytes 884744 | tf_op jit(solution)/shard_map/ppermute | solution.py:327
  36.3 1.6 collective-permute-done.12
  37.9 3.4 %collective-permute-start.5 = (f32[24,2304]{1,0:T(8,128)S(1)}, f32[24,2304]{1,0:T(8,128)S(1)}, u32[]{:S(2)}, u32[]{:S(2)}) collective-permute-start(f32[24,2304]{1,0:T(8,128)S(1)} %add.167), channel_id=1, source_target_pairs={{0,4},{1,25},{2,26},{3,7},{4,0},{5,29},{6,30},{7,3},{8,12},{9,17},... | collective-permute-start | bytes 663560 | tf_op jit(solution)/shard_map/ppermute | solution.py:398
  42.1 2.1 collective-permute-done.11.refs_10_
  45.4 3.1 %collective-permute-start.13 = (f32[24,2304]{1,0:T(8,128)S(1)}, f32[24,2304]{1,0:T(8,128)S(1)}, u32[]{:S(2)}, u32[]{:S(2)}) collective-permute-start(f32[24,2304]{1,0:T(8,128)S(1)} %add.179), channel_id=1, source_target_pairs={{0,24},{1,5},{2,6},{3,27},{4,28},{5,1},{6,2},{7,31},{8,16},{9,13},... | collective-permute-start | bytes 663560 | tf_op jit(solution)/shard_map/ppermute | solution.py:398
  49.2 4.6 %convert_divide_fusion.refs_2_ = f32[96,96,128]{2,1,0:T(8,128)} fusion(s32[]{:T(128)} %bitcast.15, s32[128]{0:T(128)S(1)} %copy-done.15, s32[96]{0:T(128)S(1)} %iota_add_fusion.1, pred[96]{0:T(512)(128)(4,1)S(1)} %iota_compare_fusion.1, pred[128]{0:T(512)(128)(4,1)S(1)} %iota_compare_fusion), kind=kLoop, calls=%fused_computation | loop fusion | flops 17694720 | bytes 4719716 | tf_op jit(solution)/shard_map/div | solution.py:356
  53.8 2.3 %collective-permute-done.14.refs_12_ = f32[8,9216]{1,0:T(8,128)S(1)} collective-permute-done((f32[8,9216]{1,0:T(8,128)S(1)}, f32[8,9216]{1,0:T(8,128)S(1)}, u32[]{:S(2)}, u32[]{:S(2)}) %collective-permute-start.14) | collective-permute-done | bytes 294944 | tf_op jit(solution)/shard_map/ppermute | solution.py:327
  56.7 1.5 collective-permute-start.20
  58.8 6.1 %collective-permute-done.20 = f32[24,2304]{1,0:T(8,128)S(1)} collective-permute-done((f32[24,2304]{1,0:T(8,128)S(1)}, f32[24,2304]{1,0:T(8,128)S(1)}, u32[]{:S(2)}, u32[]{:S(2)}) %collective-permute-start.20) | collective-permute-done | bytes 221216 | tf_op jit(solution)/shard_map/ppermute | solution.py:327
  64.9 2.6 %collective-permute-start.21 = (f32[24,2304]{1,0:T(8,128)S(1)}, f32[24,2304]{1,0:T(8,128)S(1)}, u32[]{:S(2)}, u32[]{:S(2)}) collective-permute-start(f32[24,2304]{1,0:T(8,128)S(1)} %collective-permute-done.20), channel_id=1, source_target_pairs={{0,24},{1,25},{2,10},{3,11},{4,28},{5,29},{6,14},{7,15},{8,16},{9,... | collective-permute-start | bytes 663560 | tf_op jit(solution)/shard_map/ppermute | solution.py:398
  67.5 1.6 collective-permute-start.22
  69.1 2.1 %collective-permute-done.16.refs_8_ = f32[8,9216]{1,0:T(8,128)S(1)} collective-permute-done((f32[8,9216]{1,0:T(8,128)S(1)}, f32[8,9216]{1,0:T(8,128)S(1)}, u32[]{:S(2)}, u32[]{:S(2)}) %collective-permute-start.16) | collective-permute-done | bytes 294944 | tf_op jit(solution)/shard_map/ppermute | solution.py:327
  71.3 1.6 collective-permute-start.18
  73.0 1.5 collective-permute-start.17
  74.5 3.0 %collective-permute-done.22.refs_9_ = f32[8,9216]{1,0:T(8,128)S(1)} collective-permute-done((f32[8,9216]{1,0:T(8,128)S(1)}, f32[8,9216]{1,0:T(8,128)S(1)}, u32[]{:S(2)}, u32[]{:S(2)}) %collective-permute-start.22) | collective-permute-done | bytes 294944 | tf_op jit(solution)/shard_map/ppermute | solution.py:327
  77.7 1.6 collective-permute-start.24
  79.9 3.9 %collective-permute-done.18.refs_10_ = f32[8,9216]{1,0:T(8,128)S(1)} collective-permute-done((f32[8,9216]{1,0:T(8,128)S(1)}, f32[8,9216]{1,0:T(8,128)S(1)}, u32[]{:S(2)}, u32[]{:S(2)}) %collective-permute-start.18) | collective-permute-done | bytes 294944 | tf_op jit(solution)/shard_map/ppermute | solution.py:327
  84.6 5.3 %collective-permute-done.24.refs_11_ = f32[8,9216]{1,0:T(8,128)S(1)} collective-permute-done((f32[8,9216]{1,0:T(8,128)S(1)}, f32[8,9216]{1,0:T(8,128)S(1)}, u32[]{:S(2)}, u32[]{:S(2)}) %collective-permute-start.24) | collective-permute-done | bytes 294944 | tf_op jit(solution)/shard_map/ppermute | solution.py:327
  90.6 1.8 collective-permute-start.26
  93.4 1.0 copy-done.17
  94.4 15.6 %pair_terms.2 = (f32[24,9216]{1,0:T(8,128)}, f32[24,9216]{1,0:T(8,128)}, f32[24,9216]{1,0:T(8,128)}, f32[24,9216]{1,0:T(8,128)}, f32[48,9216]{1,0:T(8,128)}, /*i...) custom-call(s32[2]{0:T(128)S(1)} %pad_add_fusion.place_ref, ...), custom_call_target="tpu_custom_call" | custom-call | flops 10871635968 | bytes 20643840 | tf_op jit(solution)/shard_map/pair_terms/pallas_call | solution.py:286
  110.0 1.4 collective-permute-start.27
  112.3 16.6 %pair_terms.3 = (f32[24,9216]{1,0:T(8,128)}, f32[24,9216]{1,0:T(8,128)}, f32[24,9216]{1,0:T(8,128)}, f32[24,9216]{1,0:T(8,128)}, f32[48,9216]{1,0:T(8,128)}, /*i...) custom-call(s32[2]{0:T(128)S(1)} %pad_add_fusion.place_ref, ...), custom_call_target="tpu_custom_call" | custom-call | flops 10871635968 | bytes 24182784 | tf_op jit(solution)/shard_map/pair_terms/pallas_call | solution.py:286
  129.5 2.1 collective-permute-done.28
  132.5 1.4 collective-permute-start.29
  134.1 1.5 collective-permute-start.33
  135.6 6.1 %collective-permute-done.30 = f32[8,9216]{1,0:T(8,128)S(1)} collective-permute-done((f32[8,9216]{1,0:T(8,128)S(1)}, f32[8,9216]{1,0:T(8,128)S(1)}, u32[]{:S(2)}, u32[]{:S(2)}) %collective-permute-start.30) | collective-permute-done | bytes 294944 | tf_op jit(solution)/shard_map/ppermute | solution.py:327
  141.7 3.6 %collective-permute-done.29 = f32[24,4608]{1,0:T(8,128)S(1)} collective-permute-done((f32[24,4608]{1,0:T(8,128)S(1)}, f32[24,4608]{1,0:T(8,128)S(1)}, u32[]{:S(2)}, u32[]{:S(2)}) %collective-permute-start.29) | collective-permute-done | bytes 442400 | tf_op jit(solution)/shard_map/ppermute | solution.py:398
  145.5 1.5 collective-permute-start.35
  147.0 1.0 collective-permute-done.33
  149.0 4.5 %collective-permute-done.34 = f32[24,2304]{1,0:T(8,128)S(1)} collective-permute-done((f32[24,2304]{1,0:T(8,128)S(1)}, f32[24,2304]{1,0:T(8,128)S(1)}, u32[]{:S(2)}, u32[]{:S(2)}) %collective-permute-start.34) | collective-permute-done | bytes 221216 | tf_op jit(solution)/shard_map/ppermute | solution.py:398
  153.5 2.0 collective-permute-done.35
  156.0 1.4 collective-permute-start.39
  157.4 4.4 %collective-permute-done.37 = f32[8,9216]{1,0:T(8,128)S(1)} collective-permute-done((f32[8,9216]{1,0:T(8,128)S(1)}, f32[8,9216]{1,0:T(8,128)S(1)}, u32[]{:S(2)}, u32[]{:S(2)}) %collective-permute-start.37) | collective-permute-done | bytes 294944 | tf_op jit(solution)/shard_map/ppermute | solution.py:327
  161.8 1.5 collective-permute-start.40
  163.3 1.5 collective-permute-start.41
  165.1 3.0 %collective-permute-done.39 = f32[8,9216]{1,0:T(8,128)S(1)} collective-permute-done((f32[8,9216]{1,0:T(8,128)S(1)}, f32[8,9216]{1,0:T(8,128)S(1)}, u32[]{:S(2)}, u32[]{:S(2)}) %collective-permute-start.39) | collective-permute-done | bytes 294944 | tf_op jit(solution)/shard_map/ppermute | solution.py:327
  168.2 4.8 %collective-permute-start.42 = (f32[24,2304]{1,0:T(8,128)S(1)}, f32[24,2304]{1,0:T(8,128)S(1)}, u32[]{:S(2)}, u32[]{:S(2)}) collective-permute-start(f32[24,2304]{1,0:T(8,128)S(1)} %add.191), channel_id=1, source_target_pairs={{0,8},{1,9},{2,26},{3,27},{4,12},{5,13},{6,30},{7,31},{8,0},{9,1},... | collective-permute-start | bytes 663560 | tf_op jit(solution)/shard_map/ppermute | solution.py:398
  174.5 1.5 collective-permute-start.44
  176.0 7.9 %collective-permute-done.44 = f32[24,2304]{1,0:T(8,128)S(1)} collective-permute-done((f32[24,2304]{1,0:T(8,128)S(1)}, f32[24,2304]{1,0:T(8,128)S(1)}, u32[]{:S(2)}, u32[]{:S(2)}) %collective-permute-start.44) | collective-permute-done | bytes 221216 | tf_op jit(solution)/shard_map/ppermute | solution.py:327
  184.8 1.9 collective-permute-start.46
  187.0 2.1 collective-permute-start.47
  189.1 2.7 %collective-permute-done.45 = f32[24,2304]{1,0:T(8,128)S(1)} collective-permute-done((f32[24,2304]{1,0:T(8,128)S(1)}, f32[24,2304]{1,0:T(8,128)S(1)}, u32[]{:S(2)}, u32[]{:S(2)}) %collective-permute-start.45) | collective-permute-done | bytes 221216 | tf_op jit(solution)/shard_map/ppermute | solution.py:398
  191.8 2.9 %collective-permute-done.46 = f32[8,9216]{1,0:T(8,128)S(1)} collective-permute-done((f32[8,9216]{1,0:T(8,128)S(1)}, f32[8,9216]{1,0:T(8,128)S(1)}, u32[]{:S(2)}, u32[]{:S(2)}) %collective-permute-start.46) | collective-permute-done | bytes 294944 | tf_op jit(solution)/shard_map/ppermute | solution.py:327
  194.8 2.0 collective-permute-start.50
  196.9 2.5 %collective-permute-done.48 = f32[8,9216]{1,0:T(8,128)S(1)} collective-permute-done((f32[8,9216]{1,0:T(8,128)S(1)}, f32[8,9216]{1,0:T(8,128)S(1)}, u32[]{:S(2)}, u32[]{:S(2)}) %collective-permute-start.48) | collective-permute-done | bytes 294944 | tf_op jit(solution)/shard_map/ppermute | solution.py:327
  199.6 2.9 %collective-permute-done.50 = f32[8,9216]{1,0:T(8,128)S(1)} collective-permute-done((f32[8,9216]{1,0:T(8,128)S(1)}, f32[8,9216]{1,0:T(8,128)S(1)}, u32[]{:S(2)}, u32[]{:S(2)}) %collective-permute-start.50) | collective-permute-done | bytes 294944 | tf_op jit(solution)/shard_map/ppermute | solution.py:327
  202.5 2.6 %collective-permute-done.49 = f32[24,4608]{1,0:T(8,128)S(1)} collective-permute-done((f32[24,4608]{1,0:T(8,128)S(1)}, f32[24,4608]{1,0:T(8,128)S(1)}, u32[]{:S(2)}, u32[]{:S(2)}) %collective-permute-start.49) | collective-permute-done | bytes 442400 | tf_op jit(solution)/shard_map/ppermute | solution.py:398
  205.7 2.0 pad_maximum_fusion
  208.3 2.0 pad_maximum_fusion.1
  (176 shorter events, 20.3 us)
Async XLA Ops:
  1.3 7.6 %copy-start.2 = (f32[2,48,9216]{2,1,0:T(8,128)S(1)}, f32[2,48,9216]{2,1,0:T(8,128)}, u32[]{:S(2)}) copy-start(f32[2,48,9216]{2,1,0:T(8,128)} %refs_7_.3) | copy-start | bytes 10616836
  4.8 2.8 %collective-permute-start = (f32[24,9216]{1,0:T(8,128)}, f32[24,9216]{1,0:T(8,128)}, u32[]{:S(2)}, u32[]{:S(2)}) collective-permute-start(f32[24,9216]{1,0:T(8,128)} %get-tuple-element.288), channel_id=1, source_target_pairs={{0,2},{1,3},{2,0},{3,1},{4,6},{5,7},{6,4},{7,5},{8,10},{9,11},{10,... | collective-permute-start | bytes 2654216 | tf_op jit(solution)/shard_map/ppermute | solution.py:398
  5.3 3.7 %collective-permute-start.7 = (f32[24,9216]{1,0:T(8,128)}, f32[24,9216]{1,0:T(8,128)}, u32[]{:S(2)}, u32[]{:S(2)}) collective-permute-start(f32[24,9216]{1,0:T(8,128)} %get-tuple-element.289), channel_id=1, source_target_pairs={{0,2},{1,3},{2,0},{3,1},{4,6},{5,7},{6,4},{7,5},{8,10},{9,11},{10,... | collective-permute-start | bytes 2654216 | tf_op jit(solution)/shard_map/ppermute | solution.py:398
  12.7 8.1 %copy-start.13 = (f32[24,4608]{1,0:T(8,128)S(1)}, f32[24,4608]{1,0:T(8,128)}, u32[]{:S(2)}) copy-start(f32[24,4608]{1,0:T(8,128)} %get-tuple-element.158) | copy-start | bytes 1327108
  12.7 12.7 %copy-start.8 = (f32[24,4608]{1,0:T(8,128)S(1)}, f32[24,4608]{1,0:T(8,128)}, u32[]{:S(2)}) copy-start(f32[24,4608]{1,0:T(8,128)} %get-tuple-element.143) | copy-start | bytes 1327108
  12.7 10.9 %collective-permute-start.2 = (f32[8,9216]{1,0:T(8,128)}, f32[8,9216]{1,0:T(8,128)S(1)}, u32[]{:S(2)}, u32[]{:S(2)}) collective-permute-start(f32[8,9216]{1,0:T(8,128)} %slice_bitcast_fusion.10), channel_id=1, source_target_pairs={{0,1},{1,0},{2,3},{3,2},{4,5},{5,4},{6,7},{7,6},{8,9},{9,8},{10,11... | collective-permute-start | bytes 884744 | tf_op jit(solution)/shard_map/ppermute | solution.py:327
  15.5 9.8 %collective-permute-start.1 = (f32[24,4608]{1,0:T(8,128)}, f32[24,4608]{1,0:T(8,128)S(1)}, u32[]{:S(2)}, u32[]{:S(2)}) collective-permute-start(f32[24,4608]{1,0:T(8,128)} %get-tuple-element.144), channel_id=1, source_target_pairs={{0,8},{1,5},{2,6},{3,11},{4,12},{5,1},{6,2},{7,15},{8,0},{9,13},{1... | collective-permute-start | bytes 1327112 | tf_op jit(solution)/shard_map/ppermute | solution.py:398
  19.4 11.0 %copy-start.7 = (f32[24,4608]{1,0:T(8,128)S(1)}, f32[24,4608]{1,0:T(8,128)}, u32[]{:S(2)}) copy-start(f32[24,4608]{1,0:T(8,128)} %get-tuple-element.157) | copy-start | bytes 1327108
  20.2 10.2 %collective-permute-start.9 = (f32[8,9216]{1,0:T(8,128)S(1)}, f32[8,9216]{1,0:T(8,128)S(1)}, u32[]{:S(2)}, u32[]{:S(2)}) collective-permute-start(f32[8,9216]{1,0:T(8,128)S(1)} %slice_bitcast_fusion.7), channel_id=1, source_target_pairs={{0,1},{1,0},{2,3},{3,2},{4,5},{5,4},{6,7},{7,6},{8,9},{9,8},{10,11... | collective-permute-start | bytes 884744 | tf_op jit(solution)/shard_map/ppermute | solution.py:327
  20.7 9.7 %collective-permute-start.8 = (f32[24,4608]{1,0:T(8,128)S(1)}, f32[24,4608]{1,0:T(8,128)S(1)}, u32[]{:S(2)}, u32[]{:S(2)}) collective-permute-start(f32[24,4608]{1,0:T(8,128)S(1)} %copy-done.13), channel_id=1, source_target_pairs={{0,4},{1,9},{2,10},{3,7},{4,0},{5,13},{6,14},{7,3},{8,12},{9,1},{1... | collective-permute-start | bytes 1327112 | tf_op jit(solution)/shard_map/ppermute | solution.py:398
  25.4 8.3 %copy-start.3 = (f32[2,48,9216]{2,1,0:T(8,128)S(1)}, f32[2,48,9216]{2,1,0:T(8,128)}, u32[]{:S(2)}) copy-start(f32[2,48,9216]{2,1,0:T(8,128)} %refs_7_.3) | copy-start | bytes 10616836
  25.4 12.5 %collective-permute-start.3 = (f32[24,2304]{1,0:T(8,128)S(1)}, f32[24,2304]{1,0:T(8,128)S(1)}, u32[]{:S(2)}, u32[]{:S(2)}) collective-permute-start(f32[24,2304]{1,0:T(8,128)S(1)} %get-tuple-element.148), channel_id=1, source_target_pairs={{0,24},{1,9},{2,10},{3,27},{4,28},{5,13},{6,14},{7,31},{8,16},{9,1... | collective-permute-start | bytes 663560 | tf_op jit(solution)/shard_map/ppermute | solution.py:398
  30.3 7.6 %collective-permute-start.4 = (f32[8,9216]{1,0:T(8,128)S(1)}, f32[8,9216]{1,0:T(8,128)S(1)}, u32[]{:S(2)}, u32[]{:S(2)}) collective-permute-start(f32[8,9216]{1,0:T(8,128)S(1)} %slice_bitcast_fusion.9), channel_id=1, source_target_pairs={{0,1},{1,0},{2,3},{3,2},{4,5},{5,4},{6,7},{7,6},{8,9},{9,8},{10,11... | collective-permute-start | bytes 884744 | tf_op jit(solution)/shard_map/ppermute | solution.py:327
  30.5 18.6 %copy-start.15 = (s32[128]{0:T(128)S(1)}, s32[128]{0:T(128)}, u32[]{:S(2)}) copy-start(s32[128]{0:T(128)} %iota_add_fusion) | copy-start | bytes 1540
  30.5 7.4 %collective-permute-start.12 = (f32[8,128]{1,0:T(8,128)S(1)}, f32[8,128]{1,0:T(8,128)S(1)}, u32[]{:S(2)}, u32[]{:S(2)}) collective-permute-start(f32[8,128]{1,0:T(8,128)S(1)} %broadcast_in_dim.43), channel_id=1, source_target_pairs={{0,1},{1,0},{2,3},{3,2},{4,5},{5,4},{6,7},{7,6},{8,9},{9,8},{10,11... | collective-permute-start | bytes 12296 | tf_op jit(solution)/shard_map/ppermute | solution.py:327
  32.6 9.5 %collective-permute-start.10 = (f32[24,2304]{1,0:T(8,128)S(1)}, f32[24,2304]{1,0:T(8,128)S(1)}, u32[]{:S(2)}, u32[]{:S(2)}) collective-permute-start(f32[24,2304]{1,0:T(8,128)S(1)} %get-tuple-element.166), channel_id=1, source_target_pairs={{0,8},{1,25},{2,26},{3,11},{4,12},{5,29},{6,30},{7,15},{8,0},{9,17... | collective-permute-start | bytes 663560 | tf_op jit(solution)/shard_map/ppermute | solution.py:398
  33.7 10.5 %collective-permute-start.11 = (f32[8,9216]{1,0:T(8,128)S(1)}, f32[8,9216]{1,0:T(8,128)S(1)}, u32[]{:S(2)}, u32[]{:S(2)}) collective-permute-start(f32[8,9216]{1,0:T(8,128)S(1)} %slice_bitcast_fusion.6), channel_id=1, source_target_pairs={{0,1},{1,0},{2,3},{3,2},{4,5},{5,4},{6,7},{7,6},{8,9},{9,8},{10,11... | collective-permute-start | bytes 884744 | tf_op jit(solution)/shard_map/ppermute | solution.py:327
  37.9 15.9 %copy-start.19 = (f32[8,9216]{1,0:T(8,128)}, f32[8,9216]{1,0:T(8,128)S(1)}, u32[]{:S(2)}) copy-start(f32[8,9216]{1,0:T(8,128)S(1)} %collective-permute-done.4.refs_11_) | copy-start | bytes 884740
  37.9 15.9 %collective-permute-start.5 = (f32[24,2304]{1,0:T(8,128)S(1)}, f32[24,2304]{1,0:T(8,128)S(1)}, u32[]{:S(2)}, u32[]{:S(2)}) collective-permute-start(f32[24,2304]{1,0:T(8,128)S(1)} %add.167), channel_id=1, source_target_pairs={{0,4},{1,25},{2,26},{3,7},{4,0},{5,29},{6,30},{7,3},{8,12},{9,17},... | collective-permute-start | bytes 663560 | tf_op jit(solution)/shard_map/ppermute | solution.py:398
  41.4 12.5 %collective-permute-start.6 = (f32[8,9216]{1,0:T(8,128)S(1)}, f32[8,9216]{1,0:T(8,128)S(1)}, u32[]{:S(2)}, u32[]{:S(2)}) collective-permute-start(f32[8,9216]{1,0:T(8,128)S(1)} %slice_bitcast_fusion.8), channel_id=1, source_target_pairs={{0,1},{1,0},{2,3},{3,2},{4,5},{5,4},{6,7},{7,6},{8,9},{9,8},{10,11... | collective-permute-start | bytes 884744 | tf_op jit(solution)/shard_map/ppermute | solution.py:327
  44.2 9.6 %copy-start.20 = (f32[8,9216]{1,0:T(8,128)}, f32[8,9216]{1,0:T(8,128)S(1)}, u32[]{:S(2)}) copy-start(f32[8,9216]{1,0:T(8,128)S(1)} %collective-permute-done.11.refs_10_) | copy-start | bytes 884740
  45.4 8.4 %collective-permute-start.13 = (f32[24,2304]{1,0:T(8,128)S(1)}, f32[24,2304]{1,0:T(8,128)S(1)}, u32[]{:S(2)}, u32[]{:S(2)}) collective-permute-start(f32[24,2304]{1,0:T(8,128)S(1)} %add.179), channel_id=1, source_target_pairs={{0,24},{1,5},{2,6},{3,27},{4,28},{5,1},{6,2},{7,31},{8,16},{9,13},... | collective-permute-start | bytes 663560 | tf_op jit(solution)/shard_map/ppermute | solution.py:398
  48.5 7.6 %collective-permute-start.14 = (f32[8,9216]{1,0:T(8,128)S(1)}, f32[8,9216]{1,0:T(8,128)S(1)}, u32[]{:S(2)}, u32[]{:S(2)}) collective-permute-start(f32[8,9216]{1,0:T(8,128)S(1)} %slice_bitcast_fusion.5), channel_id=1, source_target_pairs={{0,1},{1,0},{2,3},{3,2},{4,5},{5,4},{6,7},{7,6},{8,9},{9,8},{10,11... | collective-permute-start | bytes 884744 | tf_op jit(solution)/shard_map/ppermute | solution.py:327
  53.8 17.5 %copy-start.21 = (f32[8,9216]{1,0:T(8,128)}, f32[8,9216]{1,0:T(8,128)S(1)}, u32[]{:S(2)}) copy-start(f32[8,9216]{1,0:T(8,128)S(1)} %collective-permute-done.6.refs_13_) | copy-start | bytes 884740
  56.1 15.2 %copy-start.22 = (f32[8,9216]{1,0:T(8,128)}, f32[8,9216]{1,0:T(8,128)S(1)}, u32[]{:S(2)}) copy-start(f32[8,9216]{1,0:T(8,128)S(1)} %collective-permute-done.14.refs_12_) | copy-start | bytes 884740
  56.2 12.9 %collective-permute-start.15 = (f32[24,2304]{1,0:T(8,128)S(1)}, f32[24,2304]{1,0:T(8,128)S(1)}, u32[]{:S(2)}, u32[]{:S(2)}) collective-permute-start(f32[24,2304]{1,0:T(8,128)S(1)} %get-tuple-element.178), channel_id=1, source_target_pairs={{0,8},{1,9},{2,26},{3,27},{4,12},{5,13},{6,30},{7,31},{8,0},{9,1},... | collective-permute-start | bytes 663560 | tf_op jit(solution)/shard_map/ppermute | solution.py:398
  56.7 8.2 %collective-permute-start.20 = (f32[24,2304]{1,0:T(8,128)S(1)}, f32[24,2304]{1,0:T(8,128)S(1)}, u32[]{:S(2)}, u32[]{:S(2)}) collective-permute-start(f32[24,2304]{1,0:T(8,128)S(1)} %get-tuple-element.304), channel_id=1, source_target_pairs={{0,1},{1,0},{2,3},{3,2},{4,5},{5,4},{6,7},{7,6},{8,9},{9,8},{10,11... | collective-permute-start | bytes 663560 | tf_op jit(solution)/shard_map/ppermute | solution.py:327
  58.2 13.0 %collective-permute-start.16 = (f32[8,9216]{1,0:T(8,128)S(1)}, f32[8,9216]{1,0:T(8,128)S(1)}, u32[]{:S(2)}, u32[]{:S(2)}) collective-permute-start(f32[8,9216]{1,0:T(8,128)S(1)} %slice_bitcast_fusion.4), channel_id=1, source_target_pairs={{0,1},{1,0},{2,3},{3,2},{4,5},{5,4},{6,7},{7,6},{8,9},{9,8},{10,11... | collective-permute-start | bytes 884744 | tf_op jit(solution)/shard_map/ppermute | solution.py:327
  64.9 9.6 %collective-permute-start.21 = (f32[24,2304]{1,0:T(8,128)S(1)}, f32[24,2304]{1,0:T(8,128)S(1)}, u32[]{:S(2)}, u32[]{:S(2)}) collective-permute-start(f32[24,2304]{1,0:T(8,128)S(1)} %collective-permute-done.20), channel_id=1, source_target_pairs={{0,24},{1,25},{2,10},{3,11},{4,28},{5,29},{6,14},{7,15},{8,16},{9,... | collective-permute-start | bytes 663560 | tf_op jit(solution)/shard_map/ppermute | solution.py:398
  67.5 10.0 %collective-permute-start.22 = (f32[8,9216]{1,0:T(8,128)S(1)}, f32[8,9216]{1,0:T(8,128)S(1)}, u32[]{:S(2)}, u32[]{:S(2)}) collective-permute-start(f32[8,9216]{1,0:T(8,128)S(1)} %slice_bitcast_fusion.2), channel_id=1, source_target_pairs={{0,1},{1,0},{2,3},{3,2},{4,5},{5,4},{6,7},{7,6},{8,9},{9,8},{10,11... | collective-permute-start | bytes 884744 | tf_op jit(solution)/shard_map/ppermute | solution.py:327
  71.3 12.5 %collective-permute-start.18 = (f32[8,9216]{1,0:T(8,128)S(1)}, f32[8,9216]{1,0:T(8,128)S(1)}, u32[]{:S(2)}, u32[]{:S(2)}) collective-permute-start(f32[8,9216]{1,0:T(8,128)S(1)} %slice_bitcast_fusion.3), channel_id=1, source_target_pairs={{0,1},{1,0},{2,3},{3,2},{4,5},{5,4},{6,7},{7,6},{8,9},{9,8},{10,11... | collective-permute-start | bytes 884744 | tf_op jit(solution)/shard_map/ppermute | solution.py:327
  73.0 10.9 %collective-permute-start.17 = (f32[24,4608]{1,0:T(8,128)S(1)}, f32[24,4608]{1,0:T(8,128)S(1)}, u32[]{:S(2)}, u32[]{:S(2)}) collective-permute-start(f32[24,4608]{1,0:T(8,128)S(1)} %pad_maximum_fusion.8), channel_id=1, source_target_pairs={{0,4},{1,5},{2,10},{3,11},{4,0},{5,1},{6,14},{7,15},{8,12},{9,13},... | collective-permute-start | bytes 1327112 | tf_op jit(solution)/shard_map/ppermute | solution.py:398
  77.7 12.2 %collective-permute-start.24 = (f32[8,9216]{1,0:T(8,128)S(1)}, f32[8,9216]{1,0:T(8,128)S(1)}, u32[]{:S(2)}, u32[]{:S(2)}) collective-permute-start(f32[8,9216]{1,0:T(8,128)S(1)} %slice_bitcast_fusion.1), channel_id=1, source_target_pairs={{0,1},{1,0},{2,3},{3,2},{4,5},{5,4},{6,7},{7,6},{8,9},{9,8},{10,11... | collective-permute-start | bytes 884744 | tf_op jit(solution)/shard_map/ppermute | solution.py:327
  79.3 10.6 %collective-permute-start.23 = (f32[24,4608]{1,0:T(8,128)S(1)}, f32[24,4608]{1,0:T(8,128)S(1)}, u32[]{:S(2)}, u32[]{:S(2)}) collective-permute-start(f32[24,4608]{1,0:T(8,128)S(1)} %pad_maximum_fusion.9), channel_id=1, source_target_pairs={{0,8},{1,9},{2,6},{3,7},{4,12},{5,13},{6,2},{7,3},{8,0},{9,1},{10,... | collective-permute-start | bytes 1327112 | tf_op jit(solution)/shard_map/ppermute | solution.py:398
  84.6 7.9 %collective-permute-start.19 = (f32[24,9216]{1,0:T(8,128)S(1)}, f32[24,9216]{1,0:T(8,128)S(1)}, u32[]{:S(2)}, u32[]{:S(2)}) collective-permute-start(f32[24,9216]{1,0:T(8,128)S(1)} %pad_maximum_fusion.4.refs_3_), channel_id=1, source_target_pairs={{0,2},{1,3},{2,0},{3,1},{4,6},{5,7},{6,4},{7,5},{8,10},{9,11},{10,... | collective-permute-start | bytes 2654216 | tf_op jit(solution)/shard_map/ppermute | solution.py:398
  90.6 2.4 %collective-permute-start.25 = (f32[24,9216]{1,0:T(8,128)S(1)}, f32[24,9216]{1,0:T(8,128)S(1)}, u32[]{:S(2)}, u32[]{:S(2)}) collective-permute-start(f32[24,9216]{1,0:T(8,128)S(1)} %pad_maximum_fusion.5.refs_5_), channel_id=1, source_target_pairs={{0,2},{1,3},{2,0},{3,1},{4,6},{5,7},{6,4},{7,5},{8,10},{9,11},{10,... | collective-permute-start | bytes 2654216 | tf_op jit(solution)/shard_map/ppermute | solution.py:398
  90.6 20.8 %collective-permute-start.26 = (f32[16,9216]{1,0:T(8,128)S(1)}, f32[16,9216]{1,0:T(8,128)S(1)}, u32[]{:S(2)}, u32[]{:S(2)}) collective-permute-start(f32[16,9216]{1,0:T(8,128)S(1)} %slice_bitcast_fusion), channel_id=1, source_target_pairs={{0,1},{1,0},{2,3},{3,2},{4,5},{5,4},{6,7},{7,6},{8,9},{9,8},{10,11... | collective-permute-start | bytes 1769480 | tf_op jit(solution)/shard_map/ppermute | solution.py:327
  110.0 18.9 %collective-permute-start.27 = (f32[16,9216]{1,0:T(8,128)}, f32[16,9216]{1,0:T(8,128)S(1)}, u32[]{:S(2)}, u32[]{:S(2)}) collective-permute-start(f32[16,9216]{1,0:T(8,128)} %get-tuple-element.217), channel_id=1, source_target_pairs={{0,1},{1,0},{2,3},{3,2},{4,5},{5,4},{6,7},{7,6},{8,9},{9,8},{10,11... | collective-permute-start | bytes 1769480 | tf_op jit(solution)/shard_map/ppermute | solution.py:327
  128.9 2.7 %collective-permute-start.28 = (f32[24,9216]{1,0:T(8,128)}, f32[24,9216]{1,0:T(8,128)S(1)}, u32[]{:S(2)}, u32[]{:S(2)}) collective-permute-start(f32[24,9216]{1,0:T(8,128)} %get-tuple-element.220), channel_id=1, source_target_pairs={{0,2},{1,3},{2,0},{3,1},{4,6},{5,7},{6,4},{7,5},{8,10},{9,11},{10,... | collective-permute-start | bytes 2654216 | tf_op jit(solution)/shard_map/ppermute | solution.py:398
  128.9 5.0 %collective-permute-start.31 = (f32[24,9216]{1,0:T(8,128)}, f32[24,9216]{1,0:T(8,128)S(1)}, u32[]{:S(2)}, u32[]{:S(2)}) collective-permute-start(f32[24,9216]{1,0:T(8,128)} %get-tuple-element.226), channel_id=1, source_target_pairs={{0,2},{1,3},{2,0},{3,1},{4,6},{5,7},{6,4},{7,5},{8,10},{9,11},{10,... | collective-permute-start | bytes 2654216 | tf_op jit(solution)/shard_map/ppermute | solution.py:398
  131.8 9.9 %collective-permute-start.30 = (f32[8,9216]{1,0:T(8,128)S(1)}, f32[8,9216]{1,0:T(8,128)S(1)}, u32[]{:S(2)}, u32[]{:S(2)}) collective-permute-start(f32[8,9216]{1,0:T(8,128)S(1)} %get-tuple-element.221), channel_id=1, source_target_pairs={{0,1},{1,0},{2,3},{3,2},{4,5},{5,4},{6,7},{7,6},{8,9},{9,8},{10,11... | collective-permute-start | bytes 884744 | tf_op jit(solution)/shard_map/ppermute | solution.py:327
  132.5 12.8 %collective-permute-start.29 = (f32[24,4608]{1,0:T(8,128)S(1)}, f32[24,4608]{1,0:T(8,128)S(1)}, u32[]{:S(2)}, u32[]{:S(2)}) collective-permute-start(f32[24,4608]{1,0:T(8,128)S(1)} %get-tuple-element.222), channel_id=1, source_target_pairs={{0,4},{1,5},{2,10},{3,11},{4,0},{5,1},{6,14},{7,15},{8,12},{9,13},... | collective-permute-start | bytes 1327112 | tf_op jit(solution)/shard_map/ppermute | solution.py:398
  134.1 13.9 %collective-permute-start.33 = (f32[8,9216]{1,0:T(8,128)S(1)}, f32[8,9216]{1,0:T(8,128)S(1)}, u32[]{:S(2)}, u32[]{:S(2)}) collective-permute-start(f32[8,9216]{1,0:T(8,128)S(1)} %get-tuple-element.227), channel_id=1, source_target_pairs={{0,1},{1,0},{2,3},{3,2},{4,5},{5,4},{6,7},{7,6},{8,9},{9,8},{10,11... | collective-permute-start | bytes 884744 | tf_op jit(solution)/shard_map/ppermute | solution.py:327
  135.6 12.4 %collective-permute-start.32 = (f32[24,4608]{1,0:T(8,128)S(1)}, f32[24,4608]{1,0:T(8,128)S(1)}, u32[]{:S(2)}, u32[]{:S(2)}) collective-permute-start(f32[24,4608]{1,0:T(8,128)S(1)} %get-tuple-element.228), channel_id=1, source_target_pairs={{0,8},{1,9},{2,6},{3,7},{4,12},{5,13},{6,2},{7,3},{8,0},{9,1},{10,... | collective-permute-start | bytes 1327112 | tf_op jit(solution)/shard_map/ppermute | solution.py:398
  145.4 8.1 %collective-permute-start.34 = (f32[24,2304]{1,0:T(8,128)S(1)}, f32[24,2304]{1,0:T(8,128)S(1)}, u32[]{:S(2)}, u32[]{:S(2)}) collective-permute-start(f32[24,2304]{1,0:T(8,128)S(1)} %get-tuple-element.234), channel_id=1, source_target_pairs={{0,8},{1,9},{2,26},{3,27},{4,12},{5,13},{6,30},{7,31},{8,0},{9,1},... | collective-permute-start | bytes 663560 | tf_op jit(solution)/shard_map/ppermute | solution.py:398
  145.5 10.0 %collective-permute-start.35 = (f32[8,9216]{1,0:T(8,128)S(1)}, f32[8,9216]{1,0:T(8,128)S(1)}, u32[]{:S(2)}, u32[]{:S(2)}) collective-permute-start(f32[8,9216]{1,0:T(8,128)S(1)} %get-tuple-element.233), channel_id=1, source_target_pairs={{0,1},{1,0},{2,3},{3,2},{4,5},{5,4},{6,7},{7,6},{8,9},{9,8},{10,11... | collective-permute-start | bytes 884744 | tf_op jit(solution)/shard_map/ppermute | solution.py:327
  148.1 9.3 %collective-permute-start.36 = (f32[24,2304]{1,0:T(8,128)S(1)}, f32[24,2304]{1,0:T(8,128)S(1)}, u32[]{:S(2)}, u32[]{:S(2)}) collective-permute-start(f32[24,2304]{1,0:T(8,128)S(1)} %get-tuple-element.240), channel_id=1, source_target_pairs={{0,24},{1,25},{2,10},{3,11},{4,28},{5,29},{6,14},{7,15},{8,16},{9,... | collective-permute-start | bytes 663560 | tf_op jit(solution)/shard_map/ppermute | solution.py:398
  148.3 16.5 %copy-start.6 = (f32[48,9216]{1,0:T(8,128)S(1)}, f32[48,9216]{1,0:T(8,128)}, u32[]{:S(2)}) copy-start(f32[48,9216]{1,0:T(8,128)} %get-tuple-element.203) | copy-start | bytes 5308420
  148.3 13.5 %collective-permute-start.37 = (f32[8,9216]{1,0:T(8,128)S(1)}, f32[8,9216]{1,0:T(8,128)S(1)}, u32[]{:S(2)}, u32[]{:S(2)}) collective-permute-start(f32[8,9216]{1,0:T(8,128)S(1)} %get-tuple-element.239), channel_id=1, source_target_pairs={{0,1},{1,0},{2,3},{3,2},{4,5},{5,4},{6,7},{7,6},{8,9},{9,8},{10,11... | collective-permute-start | bytes 884744 | tf_op jit(solution)/shard_map/ppermute | solution.py:327
  155.5 9.6 %collective-permute-start.38 = (f32[24,2304]{1,0:T(8,128)S(1)}, f32[24,2304]{1,0:T(8,128)S(1)}, u32[]{:S(2)}, u32[]{:S(2)}) collective-permute-start(f32[24,2304]{1,0:T(8,128)S(1)} %add.189), channel_id=1, source_target_pairs={{0,24},{1,25},{2,6},{3,7},{4,28},{5,29},{6,2},{7,3},{8,16},{9,17},... | collective-permute-start | bytes 663560 | tf_op jit(solution)/shard_map/ppermute | solution.py:398
  156.0 12.1 %collective-permute-start.39 = (f32[8,9216]{1,0:T(8,128)S(1)}, f32[8,9216]{1,0:T(8,128)S(1)}, u32[]{:S(2)}, u32[]{:S(2)}) collective-permute-start(f32[8,9216]{1,0:T(8,128)S(1)} %get-tuple-element.246), channel_id=1, source_target_pairs={{0,1},{1,0},{2,3},{3,2},{4,5},{5,4},{6,7},{7,6},{8,9},{9,8},{10,11... | collective-permute-start | bytes 884744 | tf_op jit(solution)/shard_map/ppermute | solution.py:327
  161.8 11.9 %collective-permute-start.40 = (f32[24,2304]{1,0:T(8,128)S(1)}, f32[24,2304]{1,0:T(8,128)S(1)}, u32[]{:S(2)}, u32[]{:S(2)}) collective-permute-start(f32[24,2304]{1,0:T(8,128)S(1)} %add.190), channel_id=1, source_target_pairs={{0,4},{1,5},{2,26},{3,27},{4,0},{5,1},{6,30},{7,31},{8,12},{9,13},... | collective-permute-start | bytes 663560 | tf_op jit(solution)/shard_map/ppermute | solution.py:398
  163.3 11.1 %collective-permute-start.41 = (f32[8,9216]{1,0:T(8,128)S(1)}, f32[8,9216]{1,0:T(8,128)S(1)}, u32[]{:S(2)}, u32[]{:S(2)}) collective-permute-start(f32[8,9216]{1,0:T(8,128)S(1)} %get-tuple-element.252), channel_id=1, source_target_pairs={{0,1},{1,0},{2,3},{3,2},{4,5},{5,4},{6,7},{7,6},{8,9},{9,8},{10,11... | collective-permute-start | bytes 884744 | tf_op jit(solution)/shard_map/ppermute | solution.py:327
  168.2 18.6 %collective-permute-start.42 = (f32[24,2304]{1,0:T(8,128)S(1)}, f32[24,2304]{1,0:T(8,128)S(1)}, u32[]{:S(2)}, u32[]{:S(2)}) collective-permute-start(f32[24,2304]{1,0:T(8,128)S(1)} %add.191), channel_id=1, source_target_pairs={{0,8},{1,9},{2,26},{3,27},{4,12},{5,13},{6,30},{7,31},{8,0},{9,1},... | collective-permute-start | bytes 663560 | tf_op jit(solution)/shard_map/ppermute | solution.py:398
  173.0 13.8 %collective-permute-start.43 = (f32[8,9216]{1,0:T(8,128)S(1)}, f32[8,9216]{1,0:T(8,128)S(1)}, u32[]{:S(2)}, u32[]{:S(2)}) collective-permute-start(f32[8,9216]{1,0:T(8,128)S(1)} %get-tuple-element.258), channel_id=1, source_target_pairs={{0,1},{1,0},{2,3},{3,2},{4,5},{5,4},{6,7},{7,6},{8,9},{9,8},{10,11... | collective-permute-start | bytes 884744 | tf_op jit(solution)/shard_map/ppermute | solution.py:327
  174.5 9.5 %collective-permute-start.44 = (f32[24,2304]{1,0:T(8,128)S(1)}, f32[24,2304]{1,0:T(8,128)S(1)}, u32[]{:S(2)}, u32[]{:S(2)}) collective-permute-start(f32[24,2304]{1,0:T(8,128)S(1)} %add.192), channel_id=1, source_target_pairs={{0,1},{1,0},{2,3},{3,2},{4,5},{5,4},{6,7},{7,6},{8,9},{9,8},{10,11... | collective-permute-start | bytes 663560 | tf_op jit(solution)/shard_map/ppermute | solution.py:327
  183.9 7.9 %collective-permute-start.45 = (f32[24,2304]{1,0:T(8,128)S(1)}, f32[24,2304]{1,0:T(8,128)S(1)}, u32[]{:S(2)}, u32[]{:S(2)}) collective-permute-start(f32[24,2304]{1,0:T(8,128)S(1)} %collective-permute-done.44), channel_id=1, source_target_pairs={{0,24},{1,25},{2,10},{3,11},{4,28},{5,29},{6,14},{7,15},{8,16},{9,... | collective-permute-start | bytes 663560 | tf_op jit(solution)/shard_map/ppermute | solution.py:398
  184.8 9.9 %collective-permute-start.46 = (f32[8,9216]{1,0:T(8,128)S(1)}, f32[8,9216]{1,0:T(8,128)S(1)}, u32[]{:S(2)}, u32[]{:S(2)}) collective-permute-start(f32[8,9216]{1,0:T(8,128)S(1)} %get-tuple-element.264), channel_id=1, source_target_pairs={{0,1},{1,0},{2,3},{3,2},{4,5},{5,4},{6,7},{7,6},{8,9},{9,8},{10,11... | collective-permute-start | bytes 884744 | tf_op jit(solution)/shard_map/ppermute | solution.py:327
  186.8 12.5 %collective-permute-start.48 = (f32[8,9216]{1,0:T(8,128)S(1)}, f32[8,9216]{1,0:T(8,128)S(1)}, u32[]{:S(2)}, u32[]{:S(2)}) collective-permute-start(f32[8,9216]{1,0:T(8,128)S(1)} %get-tuple-element.270), channel_id=1, source_target_pairs={{0,1},{1,0},{2,3},{3,2},{4,5},{5,4},{6,7},{7,6},{8,9},{9,8},{10,11... | collective-permute-start | bytes 884744 | tf_op jit(solution)/shard_map/ppermute | solution.py:327
  187.0 12.4 %collective-permute-start.47 = (f32[24,4608]{1,0:T(8,128)S(1)}, f32[24,4608]{1,0:T(8,128)S(1)}, u32[]{:S(2)}, u32[]{:S(2)}) collective-permute-start(f32[24,4608]{1,0:T(8,128)S(1)} %pad_maximum_fusion.10), channel_id=1, source_target_pairs={{0,4},{1,5},{2,10},{3,11},{4,0},{5,1},{6,14},{7,15},{8,12},{9,13},... | collective-permute-start | bytes 1327112 | tf_op jit(solution)/shard_map/ppermute | solution.py:398
  194.8 7.7 %collective-permute-start.50 = (f32[8,9216]{1,0:T(8,128)S(1)}, f32[8,9216]{1,0:T(8,128)S(1)}, u32[]{:S(2)}, u32[]{:S(2)}) collective-permute-start(f32[8,9216]{1,0:T(8,128)S(1)} %get-tuple-element.276), channel_id=1, source_target_pairs={{0,1},{1,0},{2,3},{3,2},{4,5},{5,4},{6,7},{7,6},{8,9},{9,8},{10,11... | collective-permute-start | bytes 884744 | tf_op jit(solution)/shard_map/ppermute | solution.py:327
  196.8 8.3 %collective-permute-start.49 = (f32[24,4608]{1,0:T(8,128)S(1)}, f32[24,4608]{1,0:T(8,128)S(1)}, u32[]{:S(2)}, u32[]{:S(2)}) collective-permute-start(f32[24,4608]{1,0:T(8,128)S(1)} %pad_maximum_fusion.11), channel_id=1, source_target_pairs={{0,8},{1,9},{2,6},{3,7},{4,12},{5,13},{6,2},{7,3},{8,0},{9,1},{10,... | collective-permute-start | bytes 1327112 | tf_op jit(solution)/shard_map/ppermute | solution.py:398
  199.5 8.2 %collective-permute-start.52 = (f32[24,9216]{1,0:T(8,128)S(1)}, f32[24,9216]{1,0:T(8,128)S(1)}, u32[]{:S(2)}, u32[]{:S(2)}) collective-permute-start(f32[24,9216]{1,0:T(8,128)S(1)} %pad_maximum_fusion.7), channel_id=1, source_target_pairs={{0,2},{1,3},{2,0},{3,1},{4,6},{5,7},{6,4},{7,5},{8,10},{9,11},{10,... | collective-permute-start | bytes 2654216 | tf_op jit(solution)/shard_map/ppermute | solution.py:398
  205.3 2.6 %collective-permute-start.51 = (f32[24,9216]{1,0:T(8,128)S(1)}, f32[24,9216]{1,0:T(8,128)S(1)}, u32[]{:S(2)}, u32[]{:S(2)}) collective-permute-start(f32[24,9216]{1,0:T(8,128)S(1)} %pad_maximum_fusion.6), channel_id=1, source_target_pairs={{0,2},{1,3},{2,0},{3,1},{4,6},{5,7},{6,4},{7,5},{8,10},{9,11},{10,... | collective-permute-start | bytes 2654216 | tf_op jit(solution)/shard_map/ppermute | solution.py:398
  (16 other events, 61.6 us)
